TPU v7x, 32 devices: a whole 2x2x4 slice. The times are simulated.
32 devices in a mesh: mocks: 2 (over x), blk: 8 (over z, y), offs: 2 (over core).
Axes of the slice: x: 2, y: 2, z: 4, core: 2. Of those that a mesh axis runs over, the one named last changes fastest.
Arguments:
- position: float32 [3, 16384], P(None, ('mocks', 'blk')), parts along dimension 1, may hold values from -200 to 200, as said below
- noise_var: float32 [16384], P(('mocks', 'blk')), parts along dimension 0, may hold values from 2 to 80
- rhs: float32 [8, 16384], P(None, ('mocks', 'blk')), parts along dimension 1, may hold values from -6 to 6
- block_count: int32 [16], P(('mocks', 'blk')), parts along dimension 0, may hold values from 1 to 1024, 5120 in all
Outputs:
- solution: float32 [8, 16384], P(None, ('mocks', 'blk')), parts along dimension 1
- residual: float32 [8, 16384], P(None, ('mocks', 'blk')), parts along dimension 1
There are 2 independent parts, one for each index of `mocks`. A program takes and returns all parts, laid end to end along the dimension named above; each array names one. Nothing has to cross between parts.
Inputs may be any that keep to these rules, and one draw needn't show every extreme that they name: `position`: every galaxy lies between 20 and 200 from the observer. Block b holds its galaxies in its first block_count[b] slots; the counts sum to 5120, and some block is full.
All inputs are finite; a program needn't handle non-finite values.
Results may differ from a plain program's by a relative error of at most 0.0001.
Values sent between devices are 32-bit elements; how exact they have to be, the bound alone decides.
No kernel may reach another device: no remote copies, remote signals or barrier semaphores. Data moves between devices by JAX's collectives and lax.ppermute only.
A program may use at most 64 MiB of HBM per device.

v0:
```python
import jax
import jax.numpy as jnp
from jax import lax
from jax.sharding import PartitionSpec as P

near_weight = 0.6
near_length = 40.0
far_weight = 0.4
far_length = 120.0


def shifted(block, axis, distance):
    devices = range(lax.axis_size(axis))
    route = [((i - distance) % len(devices), i) for i in devices]
    return lax.ppermute(block, axis, route)


def covariance(rows, cols):
    highest = lax.Precision.HIGHEST
    rows_pos = rows[0:3]
    cols_pos = cols[0:3]
    sq_rows = jnp.sum(rows_pos * rows_pos, axis=0)
    sq_cols = jnp.sum(cols_pos * cols_pos, axis=0)
    cross = jnp.einsum("ka,kb->ab", rows_pos, cols_pos, precision=highest)
    dist2 = jnp.maximum(sq_rows[:, None] + sq_cols[None, :] - 2.0 * cross, 0.0)
    cosine = cross / (jnp.sqrt(sq_rows)[:, None] * jnp.sqrt(sq_cols)[None, :])
    kernel = near_weight / (1.0 + dist2 / (near_length * near_length)) + far_weight / (
        1.0 + dist2 / (far_length * far_length)
    )
    return kernel * cosine * rows[3][:, None] * cols[3][None, :]


def squares(residual):
    local = jnp.dot(residual, residual.T, precision=lax.Precision.HIGHEST)
    return lax.psum(local, "blk")


def body(position, noise_var, rhs, block_count):
    highest = lax.Precision.HIGHEST
    slots = position.shape[1]
    half = slots // 2
    width = rhs.shape[0]
    blocks = lax.axis_size("blk")
    side = lax.axis_index("offs")
    start = side * half
    live = (jnp.arange(slots, dtype=jnp.int32) < block_count[0]).astype(jnp.float32)
    residual = rhs * live
    direction = residual
    solution = jnp.zeros_like(residual)
    norm_now = squares(residual)
    turn = 0
    own = jnp.concatenate([position, live[None, :], direction], axis=0)
    mine = lax.dynamic_slice_in_dim(own, start, half, 1)

    def pull(cols, cover):
        return lax.dot_general(
            cols[4 : 4 + width], cover, (((1,), (1,)), ((), ())), precision=highest
        )

    total = pull(mine, covariance(own, mine))
    packet = jnp.concatenate([mine, jnp.zeros((width, half), jnp.float32)], axis=0)

    def visit(turn, carry):
        packet, total = carry
        packet = shifted(packet, "blk", -1)
        cover = covariance(own, packet)
        total = total + pull(packet, cover)
        weight = (turn < blocks // 2).astype(jnp.float32)
        carried = jnp.dot(direction, cover, precision=highest) * weight
        packet = jnp.concatenate([packet[: 4 + width], packet[4 + width :] + carried], axis=0)
        return (packet, total)

    packet, total = lax.fori_loop(1, blocks // 2 + 1, visit, (packet, total))
    returned = shifted(packet[4 + width :], "blk", blocks // 2)
    total = total + lax.dynamic_update_slice_in_dim(jnp.zeros_like(direction), returned, start, 1)
    noise_term = noise_var * live * direction
    image = lax.psum(total, "offs") + noise_term
    curv = lax.psum(jnp.dot(direction, image.T, precision=highest), "blk")
    alpha = jax.scipy.linalg.cho_solve((jnp.linalg.cholesky(curv), True), norm_now)
    solution = solution + jnp.dot(alpha.T, direction, precision=highest)
    residual = residual - jnp.dot(alpha.T, image, precision=highest)
    return (solution, residual)


def solution(mesh):
    return jax.shard_map(
        body,
        mesh=mesh,
        in_specs=(
            P(None, ("mocks", "blk")),
            P(("mocks", "blk")),
            P(None, ("mocks", "blk")),
            P(("mocks", "blk")),
        ),
        out_specs=(P(None, ("mocks", "blk")), P(None, ("mocks", "blk"))),
        check_vma=False,
    )
```

profile of v0, /device:TPU:0, one launch (start us, length us, event | category | flops | bytes accessed | tf_op | source)
XLA Modules:
  0.0 97.9 jit_solution(194462380443469992)
XLA Ops:
  3.6 2.6 %fusion.36 = f32[512,1024]{1,0:T(8,128)S(1)} fusion(f32[3,1024]{1,0:T(4,128)} %param.6, f32[12,512]{1,0:T(8,128)S(1)} %fusion.31), kind=kOutput, calls=%fused_computation.51 | convolution fusion | flops 18874368 | bytes 2117632 | tf_op jit(solution)/shard_map/ka,kb->ab/dot_general | solution.py:24
  6.3 2.4 %fusion.15 = f32[8,1024]{1,0:T(8,128)S(1)} fusion(f32[512,1024]{1,0:T(8,128)S(1)} %fusion.36, f32[512]{0:T(512)S(1)} %bitcast.77, f32[1024]{0:T(1024)S(1)} %fusion.45, f32[512]{0:T(512)S(1)} %sqrt.43, f32[1024]{0:T(1024)S(1)} %sqrt.42, f32[512]{0:T(512)S(1)} %multiply_reduce_fusion.2, f32[1024]{0:T(1024)S(1)} %multiply_reduce_fusion.1, ...), kind=kOutput, calls=%fused_computation.21 | convolution fusion | flops 58720256 | bytes 2164736 | tf_op jit(solution)/shard_map/dot_general | solution.py:56
  8.7 53.7 %while.22 = (s32[]{:T(128)}, f32[20,512]{1,0:T(8,128)S(1)}, f32[8,1024]{1,0:T(8,128)S(1)}, f32[1024]{0:T(1024)S(1)}, f32[3,1024]{1,0:T(4,128)S(1)}, /*index=5*/f...) while((s32[]{:T(128)}, f32[20,512]{1,0:T(8,128)S(1)}, ...), condition=%wide.region_4.5_spmd.clone, body=%wide.region_2.4_spmd.clone.sunk | while | flops 127957504 | bytes 6797475 | solution.py:73
  8.7 6.0 %collective-permute-start = (f32[20,512]{1,0:T(8,128)S(1)}, f32[20,512]{1,0:T(8,128)S(1)}, u32[]{:S(2)}, u32[]{:S(2)}) collective-permute-start(f32[20,512]{1,0:T(8,128)S(1)} %get-tuple-element.261), channel_id=1, source_target_pairs={{2,0},{4,2},{6,4},{8,6},{10,8},{12,10},{14,12},{0,14},{3,1},{5,3},... | collective-permute-start | bytes 122888 | tf_op jit(solution)/shard_map/while/body/eval_jaxpr/ppermute | solution.py:15
  16.6 3.2 %multiply_multiply_fusion.2 = f32[1024,512]{1,0:T(8,128)S(1)} fusion(f32[512]{0:T(512)S(1)} %bitcast.74, f32[1024]{0:T(1024)S(1)} %fusion.82, f32[512]{0:T(512)S(1)} %sqrt.47, f32[1024]{0:T(1024)S(1)} %bitcast.76, f32[512]{0:T(512)S(1)} %multiply_reduce_fusion.4, f32[1024]{0:T(1024)S(1)} %get-tuple-element.273, ...), kind=kOutput, calls=%fused_computation.1.clone.1 | convolution fusion | flops 27262976 | bytes 2140160 | tf_op jit(solution)/shard_map/while/body/eval_jaxpr/ka,kb->ab/dot_general | solution.py:24
  19.8 1.2 %slice_add_fusion.2 = f32[8,512]{1,0:T(8,128)S(1)} fusion(f32[20,512]{1,0:T(8,128)S(1)} %collective-permute-done, f32[]{:T(128)S(6)} %convert_element_type.39, f32[1024,512]{1,0:T(8,128)S(1)} %multiply_multiply_fusion.2, f32[8,1024]{1,0:T(8,128)S(1)} %get-tuple-element.276), kind=kOutput, calls=%fused_computation.8.clone.1 | convolution fusion | flops 50339840 | bytes 2162692 | tf_op jit(solution)/shard_map/while/body/eval_jaxpr/dot_general | solution.py:69
  21.0 1.9 %fusion.83 = f32[8,1024]{1,0:T(8,128)S(1)} fusion(f32[8,1024]{1,0:T(8,128)S(1)} %get-tuple-element.262, f32[1024,512]{1,0:T(8,128)S(1)} %multiply_multiply_fusion.2, f32[20,512]{1,0:T(8,128)S(1)} %collective-permute-done), kind=kOutput, calls=%fused_computation.3.clone.1 | convolution fusion | flops 50339840 | bytes 2179072 | tf_op jit(solution)/shard_map/while/body/eval_jaxpr/dot_general | solution.py:56
  22.9 5.1 %collective-permute-start = (f32[20,512]{1,0:T(8,128)S(1)}, f32[20,512]{1,0:T(8,128)S(1)}, u32[]{:S(2)}, u32[]{:S(2)}) collective-permute-start(f32[20,512]{1,0:T(8,128)S(1)} %get-tuple-element.261), channel_id=1, source_target_pairs={{2,0},{4,2},{6,4},{8,6},{10,8},{12,10},{14,12},{0,14},{3,1},{5,3},... | collective-permute-start | bytes 122888 | tf_op jit(solution)/shard_map/while/body/eval_jaxpr/ppermute | solution.py:15
  28.6 1.1 %collective-permute-done = f32[20,512]{1,0:T(8,128)S(1)} collective-permute-done((f32[20,512]{1,0:T(8,128)S(1)}, f32[20,512]{1,0:T(8,128)S(1)}, u32[]{:S(2)}, u32[]{:S(2)}) %collective-permute-start) | collective-permute-done | bytes 40992 | tf_op jit(solution)/shard_map/while/body/eval_jaxpr/ppermute | solution.py:15
  29.7 3.2 %multiply_multiply_fusion.2 = f32[1024,512]{1,0:T(8,128)S(1)} fusion(f32[512]{0:T(512)S(1)} %bitcast.74, f32[1024]{0:T(1024)S(1)} %fusion.82, f32[512]{0:T(512)S(1)} %sqrt.47, f32[1024]{0:T(1024)S(1)} %bitcast.76, f32[512]{0:T(512)S(1)} %multiply_reduce_fusion.4, f32[1024]{0:T(1024)S(1)} %get-tuple-element.273, ...), kind=kOutput, calls=%fused_computation.1.clone.1 | convolution fusion | flops 27262976 | bytes 2140160 | tf_op jit(solution)/shard_map/while/body/eval_jaxpr/ka,kb->ab/dot_general | solution.py:24
  32.9 1.2 %slice_add_fusion.2 = f32[8,512]{1,0:T(8,128)S(1)} fusion(f32[20,512]{1,0:T(8,128)S(1)} %collective-permute-done, f32[]{:T(128)S(6)} %convert_element_type.39, f32[1024,512]{1,0:T(8,128)S(1)} %multiply_multiply_fusion.2, f32[8,1024]{1,0:T(8,128)S(1)} %get-tuple-element.276), kind=kOutput, calls=%fused_computation.8.clone.1 | convolution fusion | flops 50339840 | bytes 2162692 | tf_op jit(solution)/shard_map/while/body/eval_jaxpr/dot_general | solution.py:69
  34.2 1.9 %fusion.83 = f32[8,1024]{1,0:T(8,128)S(1)} fusion(f32[8,1024]{1,0:T(8,128)S(1)} %get-tuple-element.262, f32[1024,512]{1,0:T(8,128)S(1)} %multiply_multiply_fusion.2, f32[20,512]{1,0:T(8,128)S(1)} %collective-permute-done), kind=kOutput, calls=%fused_computation.3.clone.1 | convolution fusion | flops 50339840 | bytes 2179072 | tf_op jit(solution)/shard_map/while/body/eval_jaxpr/dot_general | solution.py:56
  36.0 5.1 %collective-permute-start = (f32[20,512]{1,0:T(8,128)S(1)}, f32[20,512]{1,0:T(8,128)S(1)}, u32[]{:S(2)}, u32[]{:S(2)}) collective-permute-start(f32[20,512]{1,0:T(8,128)S(1)} %get-tuple-element.261), channel_id=1, source_target_pairs={{2,0},{4,2},{6,4},{8,6},{10,8},{12,10},{14,12},{0,14},{3,1},{5,3},... | collective-permute-start | bytes 122888 | tf_op jit(solution)/shard_map/while/body/eval_jaxpr/ppermute | solution.py:15
  42.9 3.2 %multiply_multiply_fusion.2 = f32[1024,512]{1,0:T(8,128)S(1)} fusion(f32[512]{0:T(512)S(1)} %bitcast.74, f32[1024]{0:T(1024)S(1)} %fusion.82, f32[512]{0:T(512)S(1)} %sqrt.47, f32[1024]{0:T(1024)S(1)} %bitcast.76, f32[512]{0:T(512)S(1)} %multiply_reduce_fusion.4, f32[1024]{0:T(1024)S(1)} %get-tuple-element.273, ...), kind=kOutput, calls=%fused_computation.1.clone.1 | convolution fusion | flops 27262976 | bytes 2140160 | tf_op jit(solution)/shard_map/while/body/eval_jaxpr/ka,kb->ab/dot_general | solution.py:24
  46.1 1.2 %slice_add_fusion.2 = f32[8,512]{1,0:T(8,128)S(1)} fusion(f32[20,512]{1,0:T(8,128)S(1)} %collective-permute-done, f32[]{:T(128)S(6)} %convert_element_type.39, f32[1024,512]{1,0:T(8,128)S(1)} %multiply_multiply_fusion.2, f32[8,1024]{1,0:T(8,128)S(1)} %get-tuple-element.276), kind=kOutput, calls=%fused_computation.8.clone.1 | convolution fusion | flops 50339840 | bytes 2162692 | tf_op jit(solution)/shard_map/while/body/eval_jaxpr/dot_general | solution.py:69
  47.3 1.9 %fusion.83 = f32[8,1024]{1,0:T(8,128)S(1)} fusion(f32[8,1024]{1,0:T(8,128)S(1)} %get-tuple-element.262, f32[1024,512]{1,0:T(8,128)S(1)} %multiply_multiply_fusion.2, f32[20,512]{1,0:T(8,128)S(1)} %collective-permute-done), kind=kOutput, calls=%fused_computation.3.clone.1 | convolution fusion | flops 50339840 | bytes 2179072 | tf_op jit(solution)/shard_map/while/body/eval_jaxpr/dot_general | solution.py:56
  49.2 5.1 %collective-permute-start = (f32[20,512]{1,0:T(8,128)S(1)}, f32[20,512]{1,0:T(8,128)S(1)}, u32[]{:S(2)}, u32[]{:S(2)}) collective-permute-start(f32[20,512]{1,0:T(8,128)S(1)} %get-tuple-element.261), channel_id=1, source_target_pairs={{2,0},{4,2},{6,4},{8,6},{10,8},{12,10},{14,12},{0,14},{3,1},{5,3},... | collective-permute-start | bytes 122888 | tf_op jit(solution)/shard_map/while/body/eval_jaxpr/ppermute | solution.py:15
  54.9 1.1 %collective-permute-done = f32[20,512]{1,0:T(8,128)S(1)} collective-permute-done((f32[20,512]{1,0:T(8,128)S(1)}, f32[20,512]{1,0:T(8,128)S(1)}, u32[]{:S(2)}, u32[]{:S(2)}) %collective-permute-start) | collective-permute-done | bytes 40992 | tf_op jit(solution)/shard_map/while/body/eval_jaxpr/ppermute | solution.py:15
  56.1 3.2 %multiply_multiply_fusion.2 = f32[1024,512]{1,0:T(8,128)S(1)} fusion(f32[512]{0:T(512)S(1)} %bitcast.74, f32[1024]{0:T(1024)S(1)} %fusion.82, f32[512]{0:T(512)S(1)} %sqrt.47, f32[1024]{0:T(1024)S(1)} %bitcast.76, f32[512]{0:T(512)S(1)} %multiply_reduce_fusion.4, f32[1024]{0:T(1024)S(1)} %get-tuple-element.273, ...), kind=kOutput, calls=%fused_computation.1.clone.1 | convolution fusion | flops 27262976 | bytes 2140160 | tf_op jit(solution)/shard_map/while/body/eval_jaxpr/ka,kb->ab/dot_general | solution.py:24
  59.3 1.2 %slice_add_fusion.2 = f32[8,512]{1,0:T(8,128)S(1)} fusion(f32[20,512]{1,0:T(8,128)S(1)} %collective-permute-done, f32[]{:T(128)S(6)} %convert_element_type.39, f32[1024,512]{1,0:T(8,128)S(1)} %multiply_multiply_fusion.2, f32[8,1024]{1,0:T(8,128)S(1)} %get-tuple-element.276), kind=kOutput, calls=%fused_computation.8.clone.1 | convolution fusion | flops 50339840 | bytes 2162692 | tf_op jit(solution)/shard_map/while/body/eval_jaxpr/dot_general | solution.py:69
  60.5 1.9 %fusion.83 = f32[8,1024]{1,0:T(8,128)S(1)} fusion(f32[8,1024]{1,0:T(8,128)S(1)} %get-tuple-element.262, f32[1024,512]{1,0:T(8,128)S(1)} %multiply_multiply_fusion.2, f32[20,512]{1,0:T(8,128)S(1)} %collective-permute-done), kind=kOutput, calls=%fused_computation.3.clone.1 | convolution fusion | flops 50339840 | bytes 2179072 | tf_op jit(solution)/shard_map/while/body/eval_jaxpr/dot_general | solution.py:56
  62.7 4.4 %collective-permute-done.1 = f32[8,512]{1,0:T(8,128)S(1)} collective-permute-done((f32[8,512]{1,0:T(8,128)S(1)}, f32[8,512]{1,0:T(8,128)S(1)}, u32[]{:S(2)}, u32[]{:S(2)}) %collective-permute-start.1) | collective-permute-done | bytes 16416 | tf_op jit(solution)/shard_map/ppermute | solution.py:15
  67.1 3.4 %psum.21 = f32[8,1024]{1,0:T(8,128)S(1)} all-reduce(f32[8,1024]{1,0:T(8,128)S(1)} %add_dynamic-update-slice_fusion), channel_id=1, replica_groups=mesh['mocks'=2,'blk'=8,'offs'=2] {'offs'}, use_global_device_ids=true, to_apply=%region_5.6 | all-reduce | flops 8192 | bytes 65536 | tf_op jit(solution)/shard_map/psum | solution.py:77
  70.7 22.4 %all-reduce.1 = (f32[8,8]{1,0:T(8,128)S(1)}, f32[8,8]{0,1:T(8,128)S(1)}) all-reduce(f32[8,8]{1,0:T(8,128)S(1)} %fusion.53, f32[8,8]{0,1:T(8,128)S(1)} %fusion.32), channel_id=1, replica_groups=mesh['mocks'=2,'blk'=8,'offs'=2] {'blk'}, use_global_device_ids=true, to_apply=%region_9.10 | all-reduce | flops 128 | bytes 1024 | tf_op jit(solution)/shard_map/psum | solution.py:35
  (57 shorter events, 12.5 us)
Async XLA Ops:
  6.2 2.5 %copy-start = (f32[3,1024]{1,0:T(4,128)S(1)}, f32[3,1024]{1,0:T(4,128)}, u32[]{:S(2)}) copy-start(f32[3,1024]{1,0:T(4,128)} %param.6) | copy-start | bytes 36868
  8.7 53.9 %copy-start.1 = (f32[1024]{0:T(1024)S(1)}, f32[1024]{0:T(1024)}, u32[]{:S(2)}) copy-start(f32[1024]{0:T(1024)} %param.7) | copy-start | bytes 12292
  8.7 7.8 %collective-permute-start = (f32[20,512]{1,0:T(8,128)S(1)}, f32[20,512]{1,0:T(8,128)S(1)}, u32[]{:S(2)}, u32[]{:S(2)}) collective-permute-start(f32[20,512]{1,0:T(8,128)S(1)} %get-tuple-element.261), channel_id=1, source_target_pairs={{2,0},{4,2},{6,4},{8,6},{10,8},{12,10},{14,12},{0,14},{3,1},{5,3},... | collective-permute-start | bytes 122888 | tf_op jit(solution)/shard_map/while/body/eval_jaxpr/ppermute | solution.py:15
  22.9 6.8 %collective-permute-start = (f32[20,512]{1,0:T(8,128)S(1)}, f32[20,512]{1,0:T(8,128)S(1)}, u32[]{:S(2)}, u32[]{:S(2)}) collective-permute-start(f32[20,512]{1,0:T(8,128)S(1)} %get-tuple-element.261), channel_id=1, source_target_pairs={{2,0},{4,2},{6,4},{8,6},{10,8},{12,10},{14,12},{0,14},{3,1},{5,3},... | collective-permute-start | bytes 122888 | tf_op jit(solution)/shard_map/while/body/eval_jaxpr/ppermute | solution.py:15
  36.0 6.8 %collective-permute-start = (f32[20,512]{1,0:T(8,128)S(1)}, f32[20,512]{1,0:T(8,128)S(1)}, u32[]{:S(2)}, u32[]{:S(2)}) collective-permute-start(f32[20,512]{1,0:T(8,128)S(1)} %get-tuple-element.261), channel_id=1, source_target_pairs={{2,0},{4,2},{6,4},{8,6},{10,8},{12,10},{14,12},{0,14},{3,1},{5,3},... | collective-permute-start | bytes 122888 | tf_op jit(solution)/shard_map/while/body/eval_jaxpr/ppermute | solution.py:15
  49.2 6.8 %collective-permute-start = (f32[20,512]{1,0:T(8,128)S(1)}, f32[20,512]{1,0:T(8,128)S(1)}, u32[]{:S(2)}, u32[]{:S(2)}) collective-permute-start(f32[20,512]{1,0:T(8,128)S(1)} %get-tuple-element.261), channel_id=1, source_target_pairs={{2,0},{4,2},{6,4},{8,6},{10,8},{12,10},{14,12},{0,14},{3,1},{5,3},... | collective-permute-start | bytes 122888 | tf_op jit(solution)/shard_map/while/body/eval_jaxpr/ppermute | solution.py:15
  62.4 4.7 %collective-permute-start.1 = (f32[8,512]{1,0:T(8,128)S(1)}, f32[8,512]{1,0:T(8,128)S(1)}, u32[]{:S(2)}, u32[]{:S(2)}) collective-permute-start(f32[8,512]{1,0:T(8,128)S(1)} %slice.78), channel_id=1, source_target_pairs={{8,0},{10,2},{12,4},{14,6},{0,8},{2,10},{4,12},{6,14},{9,1},{11,3}... | collective-permute-start | bytes 49160 | tf_op jit(solution)/shard_map/ppermute | solution.py:15
where the time goes:
time: 98.4 us; the launch traced here: 97.9 us
  matrix products  32.5 us (33%)
  blocking collectives  25.8 us (26%)
  starting transfers between devices  21.3 us (22%)
  waiting for transfers between devices  8.79 us (9%)
  other arithmetic  7.73 us (8%)
  between operations  1.41 us (1%)
    psum x1, blocking collectives, squares(): return lax.psum(local, 'blk')  22.4 us
    ppermute x5, starting transfers between devices, shifted(): return lax.ppermute(block, axis, route)  21.3 us
    dot_general x5, matrix products, covariance(): cross = jnp.einsum('ka,kb->ab', rows_pos, cols_pos, precision=highest)  15.4 us
    dot_general x5, matrix products, pull(): lax.dot_general(cols[4:4 + width], cover, (((1,), (1,)), ((), ())), preci...  9.95 us
    ppermute x5, waiting for transfers between devices, shifted(): return lax.ppermute(block, axis, route)  8.79 us
    dot_general x4, matrix products, visit(): carried = jnp.dot(direction, cover, precision=highest) * weight  4.8 us
    psum x1, blocking collectives, body(): image = lax.psum(total, 'offs') + noise_term  3.39 us
    convert_element_type x6, other arithmetic, body(): (jnp.arange(slots, dtype=jnp.int32) < block_count[0]).astype(jnp.float32)  2.6 us
  transfers between devices with their start and end apart: 5, of which 5 were waited for; matrix products, arithmetic and copies ran while one was open for 3% of the time, Pallas kernels for 0%

commit v1 on v0

v1 whole, which is shorter than its diff:
```python
import functools

import jax
import jax.numpy as jnp
from jax import lax
from jax.experimental import pallas as pl
from jax.experimental.pallas import tpu as pltpu
from jax.sharding import PartitionSpec as P

near_weight = 0.6
near_length = 40.0
far_weight = 0.4
far_length = 120.0
near_sq = near_length * near_length
far_sq = far_length * far_length
gap = far_sq - near_sq
scale = near_weight * near_sq + far_weight * far_sq
lift = near_weight * near_sq * gap / scale

LANES = 128
STEP = 512
f32 = jnp.float32
bf16 = jnp.bfloat16
VMEM = pl.BlockSpec(memory_space=pltpu.VMEM)
HBM = pl.BlockSpec(memory_space=pl.ANY)
LIMIT = 24 * 2**20
highest = lax.Precision.HIGHEST


def split3(x):
    top = x.astype(bf16).astype(f32)
    rest = x - top
    mid = rest.astype(bf16).astype(f32)
    return top, mid, rest - mid


def stack(rows, width):
    rows = rows + [jnp.zeros((32 - len(rows), width), f32)]
    return jnp.concatenate(rows, axis=0).astype(bf16)


def row_side(pos):
    width = pos.shape[1]
    rows = []
    for k in range(3):
        top, mid, low = split3(pos[k : k + 1])
        rows += [top, mid, top, low, top, mid]
    one = jnp.ones((1, width), f32)
    square = jnp.sum(pos * pos, axis=0, keepdims=True) + near_sq
    return stack(rows + [one] * 3 + list(split3(square)), width)


def column_side(pos):
    width = pos.shape[1]
    rows = []
    for k in range(3):
        top, mid, low = split3(-2.0 * pos[k : k + 1])
        rows += [top, top, mid, top, low, mid]
    one = jnp.ones((1, width), f32)
    square = jnp.sum(pos * pos, axis=0, keepdims=True)
    return stack(rows + list(split3(square)) + [one] * 3, width)


def unit_of(pos):
    square = jnp.sum(pos * pos, axis=0, keepdims=True)
    return pos * jnp.where(square > 0.0, lax.rsqrt(square), 0.0)


def pack_kernel(pos_hbm, rhs_hbm, count_hbm, out, pos, rhs, count, sems):
    copies = [
        pltpu.make_async_copy(pos_hbm, pos, sems.at[0]),
        pltpu.make_async_copy(rhs_hbm, rhs, sems.at[1]),
        pltpu.make_async_copy(count_hbm, count, sems.at[2]),
    ]
    for copy in copies:
        copy.start()
    for copy in copies:
        copy.wait()
    width, slots = rhs.shape
    tiles = slots // LANES // 2
    side = (lax.axis_index("offs") + lax.axis_index("blk")) % 2
    odd = side == 1
    n = count[0]
    lane = lax.broadcasted_iota(jnp.int32, (1, LANES), 1)
    held = jnp.clip((n + LANES - 1 - side * LANES + LANES) // (2 * LANES), 0, tiles)
    held = jnp.full((1, LANES), held.astype(f32))
    for t in range(tiles):
        even_at = slice(2 * t * LANES, (2 * t + 1) * LANES)
        odd_at = slice((2 * t + 1) * LANES, (2 * t + 2) * LANES)
        first = (2 * t + side) * LANES
        value = jnp.where(odd, rhs[:, odd_at], rhs[:, even_at])
        out[:, t * LANES : (t + 1) * LANES] = jnp.where(first + lane < n, value, 0.0)
        place = jnp.where(odd, pos[:, odd_at], pos[:, even_at])
        at = (tiles + t // 2) * LANES
        row = (t % 2) * 4
        out[row : row + 4, at : at + LANES] = jnp.concatenate([place, held], axis=0)


def pair_kernel(first, last, blocks, tiles, *refs):
    refs = list(refs)
    packet = refs.pop(0)
    if first:
        pos_hbm = refs.pop(0)
    else:
        rows_in, acc_in = refs.pop(0), refs.pop(0)
    if last:
        pos_hbm, noise_hbm, rhs_hbm, count_hbm = (refs.pop(0) for _ in range(4))
        out = refs.pop(0)
    else:
        if first:
            rows_out = refs.pop(0)
        acc_out = refs.pop(0)
    cols, weights = refs.pop(0), refs.pop(0)
    if first or last:
        sems = refs.pop(0)
        pos = refs.pop(0)
        copies = [pltpu.make_async_copy(pos_hbm, pos, sems.at[0])]
    if last:
        noise, rhs, count = (refs.pop(0) for _ in range(3))
        copies += [
            pltpu.make_async_copy(noise_hbm, noise, sems.at[1]),
            pltpu.make_async_copy(rhs_hbm, rhs, sems.at[2]),
            pltpu.make_async_copy(count_hbm, count, sems.at[3]),
        ]
    if first or last:
        for copy in copies:
            copy.start()

    width = packet.shape[0]
    half = tiles * LANES
    stride = half + half // 2
    filled = jnp.int32(0)
    for b in range(blocks):
        base = b * stride
        v = packet[:, base : base + half]
        parts = []
        for t in range(tiles):
            at = base + half + (t // 2) * LANES
            row = (t % 2) * 4
            parts.append(packet[row : row + 3, at : at + LANES])
        place = jnp.concatenate(parts, axis=1)
        unit = unit_of(place)
        product = jnp.concatenate([unit[k : k + 1] * v for k in range(3)], axis=0)
        top = product.astype(bf16)
        low = (product - top.astype(f32)).astype(bf16)
        at = pl.ds(pl.multiple_of(filled, LANES), half)
        cols[:, at] = column_side(place)
        weights[:, at] = jnp.concatenate([top, low], axis=0)
        held = jnp.max(packet[3:4, base + half : base + half + LANES])
        filled = filled + held.astype(jnp.int32) * LANES
    at = pl.ds(pl.multiple_of(filled, LANES), STEP)
    cols[:, at] = jnp.zeros((cols.shape[0], STEP), bf16)
    weights[:, at] = jnp.zeros((weights.shape[0], STEP), bf16)

    if first:
        for copy in copies:
            copy.wait()
        rows = row_side(pos[...])
        rows_out[...] = rows
        slots = rows.shape[1]
        total = jnp.zeros((6 * width, slots), f32)
    else:
        rows = rows_in[...]
        slots = rows.shape[1]
        total = acc_in[...]

    def step(i, total):
        at = pl.ds(pl.multiple_of(i * STEP, STEP), STEP)
        u = lax.dot_general(
            cols[:, at], rows, (((0,), (0,)), ((), ())), preferred_element_type=f32
        )
        u = jnp.maximum(u, near_sq)
        value = (u + lift) * pl.reciprocal(u * (u + gap), approx=True)
        top = value.astype(bf16)
        low = (value - top.astype(f32)).astype(bf16)
        w = weights[:, at]
        total = total + jnp.dot(w, top, preferred_element_type=f32)
        return total + jnp.dot(w, low, preferred_element_type=f32)

    total = lax.fori_loop(0, (filled + STEP - 1) // STEP, step, total)
    if not last:
        acc_out[...] = total
        return
    for copy in copies:
        copy.wait()
    total = total[: 3 * width] + total[3 * width :]
    lane = lax.broadcasted_iota(jnp.int32, (1, slots), 1)
    live = (lane < count[0]).astype(f32)
    unit = unit_of(pos[...]) * (live * scale)
    image = sum(unit[k : k + 1] * total[k * width : (k + 1) * width] for k in range(3))
    direction = rhs[...] * live
    mine = (lax.axis_index("offs") == 0).astype(f32)
    noise_row = noise[...].reshape(1, slots)
    image = image + (mine * noise_row * live) * direction
    out[:, :slots] = image
    dims = (((1,), (1,)), ((), ()))
    both = jnp.concatenate([image, direction * mine], axis=0)
    small = lax.dot_general(
        direction, both, dims, precision=highest, preferred_element_type=f32
    )
    pad = jnp.zeros((width, LANES - 2 * width), f32)
    out[:, slots:] = jnp.concatenate([small, pad], axis=1)


def tail_kernel(small, mine, other, rhs_hbm, count_hbm, sol, res, rhs, count, sems):
    copies = [
        pltpu.make_async_copy(rhs_hbm, rhs, sems.at[0]),
        pltpu.make_async_copy(count_hbm, count, sems.at[1]),
    ]
    for copy in copies:
        copy.start()
    a = small[...]
    width = a.shape[0]
    row = lax.broadcasted_iota(jnp.int32, a.shape, 0)
    for k in range(width):
        pivot = a[k : k + 1] / a[k : k + 1, k : k + 1]
        a = jnp.where(row == k, pivot, a - a[:, k : k + 1] * pivot)
    alpha = a[:, width : 2 * width]
    for copy in copies:
        copy.wait()
    slots = rhs.shape[1]
    lane = lax.broadcasted_iota(jnp.int32, (1, slots), 1)
    direction = rhs[...] * (lane < count[0]).astype(f32)
    image = mine[:, :slots] + other[:, :slots]
    dims = (((0,), (0,)), ((), ()))
    sol[...] = lax.dot_general(
        alpha, direction, dims, precision=highest, preferred_element_type=f32
    )
    res[...] = direction - lax.dot_general(
        alpha, image, dims, precision=highest, preferred_element_type=f32
    )


def call(kernel, out_shape, in_specs, out_specs, scratch, name, flops=0):
    return pl.pallas_call(
        kernel,
        out_shape=out_shape,
        in_specs=in_specs,
        out_specs=out_specs,
        scratch_shapes=scratch,
        compiler_params=pltpu.CompilerParams(vmem_limit_bytes=LIMIT),
        cost_estimate=pl.CostEstimate(
            flops=flops, bytes_accessed=1 << 17, transcendentals=0
        ),
        name=name,
    )


def exchanged(block, axis, distance):
    n = lax.axis_size(axis)
    return lax.ppermute(block, axis, [(i ^ distance, i) for i in range(n)])


def body(position, noise_var, rhs, block_count):
    width, slots = rhs.shape
    blocks = lax.axis_size("blk")
    tiles = slots // LANES // 2
    half = tiles * LANES
    shape = jax.ShapeDtypeStruct
    pos_buf = pltpu.VMEM(position.shape, f32)
    rhs_buf = pltpu.VMEM(rhs.shape, f32)
    noise_buf = pltpu.VMEM(noise_var.shape, f32)
    count_buf = pltpu.SMEM((1,), jnp.int32)

    packet = call(
        pack_kernel,
        shape((width, half + half // 2), f32),
        [HBM, HBM, HBM],
        VMEM,
        [pos_buf, rhs_buf, count_buf, pltpu.SemaphoreType.DMA((3,))],
        "pack",
    )(position, rhs, block_count)

    acc_shape = shape((6 * width, slots), f32)
    rows_shape = shape((32, slots), bf16)

    def pairs(fresh, count, first=False, last=False, rows=None, acc=None):
        scratch = [
            pltpu.VMEM((32, count * half + STEP), bf16),
            pltpu.VMEM((6 * width, count * half + STEP), bf16),
        ]
        if first:
            args, specs = [fresh, position], [VMEM, HBM]
            outs, out_specs = (rows_shape, acc_shape), (VMEM, VMEM)
        else:
            args, specs = [fresh, rows, acc], [VMEM] * 3
            outs, out_specs = acc_shape, VMEM
        if first or last:
            scratch += [pltpu.SemaphoreType.DMA((4,)), pos_buf]
        if last:
            args += [position, noise_var, rhs, block_count]
            specs += [HBM] * 4
            outs = shape((width, slots + LANES), f32)
            scratch += [noise_buf, rhs_buf, count_buf]
        kernel = functools.partial(pair_kernel, first, last, count, tiles)
        flops = 2 * slots * count * half * 64
        name = f"pairs_{count}"
        return call(kernel, outs, specs, out_specs, scratch, name, flops)(*args)

    known, fresh, count = packet, packet, 1
    rows = acc = None
    distance = blocks // 2
    while distance:
        arrived = exchanged(known, "blk", distance)
        if rows is None:
            rows, acc = pairs(fresh, count, first=True)
        else:
            acc = pairs(fresh, count, rows=rows, acc=acc)
            count *= 2
        if distance > 1:
            known = jnp.concatenate([known, arrived], axis=1)
        fresh = arrived
        distance //= 2
    mine = pairs(fresh, count, last=True, rows=rows, acc=acc)
    other = exchanged(mine, "offs", 1)
    small = mine[:, slots:] + other[:, slots:]
    distance = blocks // 2
    while distance:
        small = small + exchanged(small, "blk", distance)
        distance //= 2

    return tuple(
        call(
            tail_kernel,
            (shape(rhs.shape, f32),) * 2,
            [VMEM, VMEM, VMEM, HBM, HBM],
            (VMEM, VMEM),
            [rhs_buf, count_buf, pltpu.SemaphoreType.DMA((2,))],
            "tail",
        )(small, mine, other, rhs, block_count)
    )


def solution(mesh):
    return jax.shard_map(
        body,
        mesh=mesh,
        in_specs=(
            P(None, ("mocks", "blk")),
            P(("mocks", "blk")),
            P(None, ("mocks", "blk")),
            P(("mocks", "blk")),
        ),
        out_specs=(P(None, ("mocks", "blk")), P(None, ("mocks", "blk"))),
        check_vma=False,
    )
```

time: 98.4 us -> 39 us (0.40)
  matrix products: 32.5 us -> 0 us
  blocking collectives: 25.8 us -> 0 us
  Pallas kernels: 0 us -> 10.8 us
  starting transfers between devices: 21.3 us -> 12 us
  other arithmetic: 7.73 us -> 0.02 us
  waiting for transfers between devices: 8.79 us -> 13 us
  local copies, waits for them, and re-layouts: 0.19 us -> 1.48 us
    dot_general x18 -> x0, matrix products: 32.2 us -> none  [the longest x5 15.4 us: covariance(): cross = jnp.einsum('ka,kb->ab', rows_pos, cols_pos, precision=highest)]
    psum x2 -> x0, blocking collectives: 25.8 us -> none  [the longest x1 22.4 us: squares(): return lax.psum(local, 'blk')]
    pallas_call x0 -> x6, Pallas kernels: none -> 10.8 us  [the longest x4 8.48 us: pairs(): return call(kernel, outs, specs, out_specs, scratch, name, flops)(*args)]
    ppermute x5 -> x7, starting transfers between devices: 21.3 us -> 12 us  [exchanged(): return lax.ppermute(block, axis, [(i ^ distance, i) for i in range(n)])]
    ppermute x5 -> x7, waiting for transfers between devices: 8.79 us -> 13 us  [exchanged(): return lax.ppermute(block, axis, [(i ^ distance, i) for i in range(n)])]
    another operation x5 -> x0, other arithmetic: 2.67 us -> none  [the longest x3 1.39 us: body(): jnp.linalg.cholesky(curv)]
    convert_element_type x6 -> x0, other arithmetic: 2.6 us -> none  [body(): (jnp.arange(slots, dtype=jnp.int32) < block_count[0]).astype(jnp.float32)]
    unnamed x4 -> x8, local copies, waits for them, and re-layouts: 0.01 us -> 1.48 us
  transfers between devices with their start and end apart: 5 -> 7, of which waited for: 5 -> 6; matrix products, arithmetic and copies ran while one was open for 3% -> 0% of each run, Pallas kernels for 0% -> 12%
where the time goes in v1:
time: 39 us; the launch traced here: 38.7 us
  waiting for transfers between devices  13 us (33%)
  starting transfers between devices  12 us (31%)
  Pallas kernels  10.8 us (28%)
  local copies, waits for them, and re-layouts  1.48 us (4%)
  between operations  1.38 us (4%)
    ppermute x7, waiting for transfers between devices, exchanged(): return lax.ppermute(block, axis, [(i ^ distance, i) for i in range(n)])  13 us
    ppermute x7, starting transfers between devices, exchanged(): return lax.ppermute(block, axis, [(i ^ distance, i) for i in range(n)])  12 us
    pallas_call x4, Pallas kernels, pairs(): return call(kernel, outs, specs, out_specs, scratch, name, flops)(*args)  8.48 us
    pallas_call x1, Pallas kernels, body(): call(tail_kernel, (shape(rhs.shape, f32),) * 2, [VMEM, VMEM, VMEM, HBM, H...  1.66 us
    unnamed x8, local copies, waits for them, and re-layouts  1.48 us
  transfers between devices with their start and end apart: 7, of which 6 were waited for; matrix products, arithmetic and copies ran while one was open for 0% of the time, Pallas kernels for 12%

profile of v1, /device:TPU:0, one launch (start us, length us, event | category | flops | bytes accessed | tf_op | source)
XLA Modules:
  0.0 38.7 jit_solution(17069902999951407911)
XLA Ops:
  1.3 0.0 copy-start
  1.3 0.7 %copy-done = f32[8,1024]{1,0:T(8,128)S(1)} copy-done((f32[8,1024]{1,0:T(8,128)S(1)}, f32[8,1024]{1,0:T(8,128)}, u32[]{:S(2)}) %copy-start) | copy-done | bytes 32792
  2.0 0.7 %copy-done.2 = f32[3,1024]{1,0:T(4,128)S(1)} copy-done((f32[3,1024]{1,0:T(4,128)S(1)}, f32[3,1024]{1,0:T(4,128)}, u32[]{:S(2)}) %copy-start.2) | copy-done | bytes 12312
  2.8 0.6 %pack.1.refs_0_ = f32[8,768]{1,0:T(8,128)S(1)} custom-call(f32[3,1024]{1,0:T(4,128)S(1)} %copy-done.2, f32[8,1024]{1,0:T(8,128)S(1)} %copy-done, s32[1]{0:T(128)S(6)} %copy.6.count_hbm.refs_6_), custom_call_target="tpu_custom_call" | custom-call | bytes 131072 | tf_op jit(solution)/shard_map/pack/pallas_call | solution.py:265
  3.4 4.1 %collective-permute-start = (f32[8,768]{1,0:T(8,128)S(1)}, f32[8,768]{1,0:T(8,128)S(1)}, u32[]{:S(2)}, u32[]{:S(2)}) collective-permute-start(f32[8,768]{1,0:T(8,128)S(1)} %pack.1.refs_0_), channel_id=1, source_target_pairs={{8,0},{10,2},{12,4},{14,6},{0,8},{2,10},{4,12},{6,14},{9,1},{11,3}... | collective-permute-start | bytes 73736 | tf_op jit(solution)/shard_map/ppermute | solution.py:251
  7.5 1.8 %collective-permute-done.refs_0_ = f32[8,768]{1,0:T(8,128)S(1)} collective-permute-done((f32[8,768]{1,0:T(8,128)S(1)}, f32[8,768]{1,0:T(8,128)S(1)}, u32[]{:S(2)}, u32[]{:S(2)}) %collective-permute-start) | collective-permute-done | bytes 24608 | tf_op jit(solution)/shard_map/ppermute | solution.py:251
  9.3 1.9 %collective-permute-start.1 = (f32[8,1536]{1,0:T(8,128)S(1)}, f32[8,1536]{1,0:T(8,128)S(1)}, u32[]{:S(2)}, u32[]{:S(2)}) collective-permute-start(f32[8,1536]{1,0:T(8,128)S(1)} %pad_maximum_fusion.1), channel_id=1, source_target_pairs={{4,0},{6,2},{0,4},{2,6},{12,8},{14,10},{8,12},{10,14},{5,1},{7,3},... | collective-permute-start | bytes 147464 | tf_op jit(solution)/shard_map/ppermute | solution.py:251
  11.2 2.2 %collective-permute-done.1.refs_0_ = f32[8,1536]{1,0:T(8,128)S(1)} collective-permute-done((f32[8,1536]{1,0:T(8,128)S(1)}, f32[8,1536]{1,0:T(8,128)S(1)}, u32[]{:S(2)}, u32[]{:S(2)}) %collective-permute-start.1) | collective-permute-done | bytes 49184 | tf_op jit(solution)/shard_map/ppermute | solution.py:251
  13.4 2.0 %collective-permute-start.2 = (f32[8,3072]{1,0:T(8,128)S(1)}, f32[8,3072]{1,0:T(8,128)S(1)}, u32[]{:S(2)}, u32[]{:S(2)}) collective-permute-start(f32[8,3072]{1,0:T(8,128)S(1)} %pad_maximum_fusion), channel_id=1, source_target_pairs={{2,0},{0,2},{6,4},{4,6},{10,8},{8,10},{14,12},{12,14},{3,1},{1,3},... | collective-permute-start | bytes 294920 | tf_op jit(solution)/shard_map/ppermute | solution.py:251
  15.5 1.3 %pairs_1.2 = (bf16[32,1024]{1,0:T(8,128)(2,1)S(1)}, f32[48,1024]{1,0:T(8,128)S(1)}) custom-call(f32[8,768]{1,0:T(8,128)S(1)} %pack.1.refs_0_, f32[3,1024]{1,0:T(4,128)S(1)} %copy-done.2), custom_call_target="tpu_custom_call" | custom-call | flops 67108864 | bytes 131072 | tf_op jit(solution)/shard_map/pairs_1/pallas_call | solution.py:298
  16.8 1.2 %pairs_1.3.refs_2_ = f32[48,1024]{1,0:T(8,128)S(1)} custom-call(f32[8,768]{1,0:T(8,128)S(1)} %collective-permute-done.refs_0_, bf16[32,1024]{1,0:T(8,128)(2,1)S(1)} %get-tuple-element.4.refs_1_, f32[48,1024]{1,0:T(8,128)S(1)} %get-tuple-element.5.refs_2_), custom_call_target="tpu_custom_call" | custom-call | flops 67108864 | bytes 131072 | tf_op jit(solution)/shard_map/pairs_1/pallas_call | solution.py:298
  18.0 0.0 copy-start.1
  18.0 0.0 copy-start.3
  18.0 2.3 %pairs_2.1.refs_2_ = f32[48,1024]{1,0:T(8,128)S(1)} custom-call(f32[8,1536]{1,0:T(8,128)S(1)} %collective-permute-done.1.refs_0_, bf16[32,1024]{1,0:T(8,128)(2,1)S(1)} %get-tuple-element.4.refs_1_, f32[48,1024]{1,0:T(8,128)S(1)} %pairs_1.3.refs_2_), custom_call_target="tpu_custom_call" | custom-call | flops 134217728 | bytes 131072 | tf_op jit(solution)/shard_map/pairs_2/pallas_call | solution.py:298
  20.3 3.7 %pairs_4.1.mine = f32[8,1152]{1,0:T(8,128)S(1)} custom-call(f32[8,3072]{1,0:T(8,128)S(1)} %collective-permute-done.2.refs_0_, bf16[32,1024]{1,0:T(8,128)(2,1)S(1)} %get-tuple-element.4.refs_1_, f32[48,1024]{1,0:T(8,128)S(1)} %pairs_2.1.refs_2_, f32[3,1024]{1,0:T(4,128)S(1)} %copy-done.2, f32[1024]{0:T(1024)S(1)} %copy-done.3, f32[8,1024]{1,0:T(8,128)S(1)} %copy-done.1, ...), custom_call_target="tpu_custom_call" | custom-call | flops 268435456 | bytes 131072 | tf_op jit(solution)/shard_map/pairs_4/pallas_call | solution.py:298
  24.0 0.1 collective-permute-start.3
  24.1 1.2 %collective-permute-done.3.other = f32[8,1152]{1,0:T(8,128)S(1)} collective-permute-done((f32[8,1152]{1,0:T(8,128)S(1)}, f32[8,1152]{1,0:T(8,128)S(1)}, u32[]{:S(2)}, u32[]{:S(2)}) %collective-permute-start.3) | collective-permute-done | bytes 36896 | tf_op jit(solution)/shard_map/ppermute | solution.py:251
  25.3 2.5 %collective-permute-start.4 = (f32[8,128]{1,0:T(8,128)S(1)}, f32[8,128]{1,0:T(8,128)S(1)}, u32[]{:S(2)}, u32[]{:S(2)}) collective-permute-start(f32[8,128]{1,0:T(8,128)S(1)} %slice_add_fusion), channel_id=1, source_target_pairs={{8,0},{10,2},{12,4},{14,6},{0,8},{2,10},{4,12},{6,14},{9,1},{11,3}... | collective-permute-start | bytes 12296 | tf_op jit(solution)/shard_map/ppermute | solution.py:251
  27.8 2.0 %collective-permute-done.4 = f32[8,128]{1,0:T(8,128)S(1)} collective-permute-done((f32[8,128]{1,0:T(8,128)S(1)}, f32[8,128]{1,0:T(8,128)S(1)}, u32[]{:S(2)}, u32[]{:S(2)}) %collective-permute-start.4) | collective-permute-done | bytes 4128 | tf_op jit(solution)/shard_map/ppermute | solution.py:251
  29.8 1.4 %collective-permute-start.5 = (f32[8,128]{1,0:T(8,128)S(1)}, f32[8,128]{1,0:T(8,128)S(1)}, u32[]{:S(2)}, u32[]{:S(2)}) collective-permute-start(f32[8,128]{1,0:T(8,128)S(1)} %add.13), channel_id=1, source_target_pairs={{4,0},{6,2},{0,4},{2,6},{12,8},{14,10},{8,12},{10,14},{5,1},{7,3},... | collective-permute-start | bytes 12296 | tf_op jit(solution)/shard_map/ppermute | solution.py:251
  31.3 2.2 %collective-permute-done.5 = f32[8,128]{1,0:T(8,128)S(1)} collective-permute-done((f32[8,128]{1,0:T(8,128)S(1)}, f32[8,128]{1,0:T(8,128)S(1)}, u32[]{:S(2)}, u32[]{:S(2)}) %collective-permute-start.5) | collective-permute-done | bytes 4128 | tf_op jit(solution)/shard_map/ppermute | solution.py:251
  33.4 0.0 collective-permute-start.6
  33.4 3.6 %collective-permute-done.6 = f32[8,128]{1,0:T(8,128)S(1)} collective-permute-done((f32[8,128]{1,0:T(8,128)S(1)}, f32[8,128]{1,0:T(8,128)S(1)}, u32[]{:S(2)}, u32[]{:S(2)}) %collective-permute-start.6) | collective-permute-done | bytes 4128 | tf_op jit(solution)/shard_map/ppermute | solution.py:251
  37.1 1.7 %tail.1 = (f32[8,1024]{1,0:T(8,128)}, f32[8,1024]{1,0:T(8,128)}) custom-call(f32[8,128]{1,0:T(8,128)S(1)} %add.15.small, f32[8,1152]{1,0:T(8,128)S(1)} %pairs_4.1.mine, f32[8,1152]{1,0:T(8,128)S(1)} %collective-permute-done.3.other, f32[8,1024]{1,0:T(8,128)S(1)} %copy-done.1, s32[1]{0:T(128)S(6)} %copy.6.count_hbm.refs_6_), custom_call_target="tpu_custom_call" | custom-call | bytes 131072 | tf_op jit(solution)/shard_map/tail/pallas_call | solution.py:323
  (10 shorter events, 0.0 us)
Async XLA Ops:
  1.3 0.8 %copy-start = (f32[8,1024]{1,0:T(8,128)S(1)}, f32[8,1024]{1,0:T(8,128)}, u32[]{:S(2)}) copy-start(f32[8,1024]{1,0:T(8,128)} %rhs_hbm.3) | copy-start | bytes 98308
  2.0 0.7 %copy-start.2 = (f32[3,1024]{1,0:T(4,128)S(1)}, f32[3,1024]{1,0:T(4,128)}, u32[]{:S(2)}) copy-start(f32[3,1024]{1,0:T(4,128)} %refs_3_.1) | copy-start | bytes 36868
  3.4 5.9 %collective-permute-start = (f32[8,768]{1,0:T(8,128)S(1)}, f32[8,768]{1,0:T(8,128)S(1)}, u32[]{:S(2)}, u32[]{:S(2)}) collective-permute-start(f32[8,768]{1,0:T(8,128)S(1)} %pack.1.refs_0_), channel_id=1, source_target_pairs={{8,0},{10,2},{12,4},{14,6},{0,8},{2,10},{4,12},{6,14},{9,1},{11,3}... | collective-permute-start | bytes 73736 | tf_op jit(solution)/shard_map/ppermute | solution.py:251
  9.3 4.1 %collective-permute-start.1 = (f32[8,1536]{1,0:T(8,128)S(1)}, f32[8,1536]{1,0:T(8,128)S(1)}, u32[]{:S(2)}, u32[]{:S(2)}) collective-permute-start(f32[8,1536]{1,0:T(8,128)S(1)} %pad_maximum_fusion.1), channel_id=1, source_target_pairs={{4,0},{6,2},{0,4},{2,6},{12,8},{14,10},{8,12},{10,14},{5,1},{7,3},... | collective-permute-start | bytes 147464 | tf_op jit(solution)/shard_map/ppermute | solution.py:251
  13.4 6.8 %collective-permute-start.2 = (f32[8,3072]{1,0:T(8,128)S(1)}, f32[8,3072]{1,0:T(8,128)S(1)}, u32[]{:S(2)}, u32[]{:S(2)}) collective-permute-start(f32[8,3072]{1,0:T(8,128)S(1)} %pad_maximum_fusion), channel_id=1, source_target_pairs={{2,0},{0,2},{6,4},{4,6},{10,8},{8,10},{14,12},{12,14},{3,1},{1,3},... | collective-permute-start | bytes 294920 | tf_op jit(solution)/shard_map/ppermute | solution.py:251
  18.0 2.3 %copy-start.1 = (f32[8,1024]{1,0:T(8,128)S(1)}, f32[8,1024]{1,0:T(8,128)}, u32[]{:S(2)}) copy-start(f32[8,1024]{1,0:T(8,128)} %rhs_hbm.3) | copy-start | bytes 98308
  18.0 2.3 %copy-start.3 = (f32[1024]{0:T(1024)S(1)}, f32[1024]{0:T(1024)}, u32[]{:S(2)}) copy-start(f32[1024]{0:T(1024)} %refs_4_.1) | copy-start | bytes 12292
  24.0 1.3 %collective-permute-start.3 = (f32[8,1152]{1,0:T(8,128)S(1)}, f32[8,1152]{1,0:T(8,128)S(1)}, u32[]{:S(2)}, u32[]{:S(2)}) collective-permute-start(f32[8,1152]{1,0:T(8,128)S(1)} %pairs_4.1.mine), channel_id=1, source_target_pairs={{1,0},{0,1},{3,2},{2,3},{5,4},{4,5},{7,6},{6,7},{9,8},{8,9},{11,10... | collective-permute-start | bytes 110600 | tf_op jit(solution)/shard_map/ppermute | solution.py:251
  25.3 4.5 %collective-permute-start.4 = (f32[8,128]{1,0:T(8,128)S(1)}, f32[8,128]{1,0:T(8,128)S(1)}, u32[]{:S(2)}, u32[]{:S(2)}) collective-permute-start(f32[8,128]{1,0:T(8,128)S(1)} %slice_add_fusion), channel_id=1, source_target_pairs={{8,0},{10,2},{12,4},{14,6},{0,8},{2,10},{4,12},{6,14},{9,1},{11,3}... | collective-permute-start | bytes 12296 | tf_op jit(solution)/shard_map/ppermute | solution.py:251
  29.8 3.6 %collective-permute-start.5 = (f32[8,128]{1,0:T(8,128)S(1)}, f32[8,128]{1,0:T(8,128)S(1)}, u32[]{:S(2)}, u32[]{:S(2)}) collective-permute-start(f32[8,128]{1,0:T(8,128)S(1)} %add.13), channel_id=1, source_target_pairs={{4,0},{6,2},{0,4},{2,6},{12,8},{14,10},{8,12},{10,14},{5,1},{7,3},... | collective-permute-start | bytes 12296 | tf_op jit(solution)/shard_map/ppermute | solution.py:251
  33.4 3.6 %collective-permute-start.6 = (f32[8,128]{1,0:T(8,128)S(1)}, f32[8,128]{1,0:T(8,128)S(1)}, u32[]{:S(2)}, u32[]{:S(2)}) collective-permute-start(f32[8,128]{1,0:T(8,128)S(1)} %add.14), channel_id=1, source_target_pairs={{2,0},{0,2},{6,4},{4,6},{10,8},{8,10},{14,12},{12,14},{3,1},{1,3},... | collective-permute-start | bytes 12296 | tf_op jit(solution)/shard_map/ppermute | solution.py:251

commit v2 on v1

--- a/solution.py
+++ b/solution.py
@@ -22,7 +22,7 @@
 f32 = jnp.float32
 bf16 = jnp.bfloat16
 VMEM = pl.BlockSpec(memory_space=pltpu.VMEM)
-HBM = pl.BlockSpec(memory_space=pl.ANY)
+HBM = pl.BlockSpec(memory_space=pltpu.HBM)
 LIMIT = 24 * 2**20
 highest = lax.Precision.HIGHEST
 
@@ -96,25 +96,26 @@
         out[row : row + 4, at : at + LANES] = jnp.concatenate([place, held], axis=0)
 
 
-def pair_kernel(first, last, blocks, tiles, *refs):
+def pair_kernel(first, last, start, blocks, tiles, *refs):
     refs = list(refs)
     packet = refs.pop(0)
-    if first:
+    if first or last:
         pos_hbm = refs.pop(0)
-    else:
+    if not first:
         rows_in, acc_in = refs.pop(0), refs.pop(0)
     if last:
-        pos_hbm, noise_hbm, rhs_hbm, count_hbm = (refs.pop(0) for _ in range(4))
-        out = refs.pop(0)
+        noise_hbm, rhs_hbm, count_hbm, out = (refs.pop(0) for _ in range(4))
+        acc = refs.pop(0)
     else:
-        if first:
-            rows_out = refs.pop(0)
-        acc_out = refs.pop(0)
+        known_out, acc = refs.pop(0), refs.pop(0)
+        rows_ref = refs.pop(0) if first else rows_in
+    if last:
+        rows_ref = rows_in
     cols, weights = refs.pop(0), refs.pop(0)
+    copies = []
     if first or last:
-        sems = refs.pop(0)
-        pos = refs.pop(0)
-        copies = [pltpu.make_async_copy(pos_hbm, pos, sems.at[0])]
+        sems, pos = refs.pop(0), refs.pop(0)
+        copies.append(pltpu.make_async_copy(pos_hbm, pos, sems.at[0]))
     if last:
         noise, rhs, count = (refs.pop(0) for _ in range(3))
         copies += [
@@ -122,15 +123,16 @@
             pltpu.make_async_copy(rhs_hbm, rhs, sems.at[2]),
             pltpu.make_async_copy(count_hbm, count, sems.at[3]),
         ]
-    if first or last:
-        for copy in copies:
-            copy.start()
+    for copy in copies:
+        copy.start()
+    if not last:
+        known_out[...] = packet[...]
 
     width = packet.shape[0]
     half = tiles * LANES
     stride = half + half // 2
     filled = jnp.int32(0)
-    for b in range(blocks):
+    for b in range(start, start + blocks):
         base = b * stride
         v = packet[:, base : base + half]
         parts = []
@@ -152,38 +154,46 @@
     cols[:, at] = jnp.zeros((cols.shape[0], STEP), bf16)
     weights[:, at] = jnp.zeros((weights.shape[0], STEP), bf16)
 
+    slots = acc.shape[1]
     if first:
-        for copy in copies:
-            copy.wait()
-        rows = row_side(pos[...])
-        rows_out[...] = rows
-        slots = rows.shape[1]
-        total = jnp.zeros((6 * width, slots), f32)
+        copies[0].wait()
+        rows_ref[...] = row_side(pos[...])
+        acc[...] = jnp.zeros(acc.shape, f32)
     else:
-        rows = rows_in[...]
-        slots = rows.shape[1]
-        total = acc_in[...]
-
-    def step(i, total):
-        at = pl.ds(pl.multiple_of(i * STEP, STEP), STEP)
+        acc[...] = acc_in[...]
+
+    def step(begin, size):
+        at = pl.ds(pl.multiple_of(begin, LANES), size)
         u = lax.dot_general(
-            cols[:, at], rows, (((0,), (0,)), ((), ())), preferred_element_type=f32
+            cols[:, at],
+            rows_ref[...],
+            (((0,), (0,)), ((), ())),
+            preferred_element_type=f32,
         )
         u = jnp.maximum(u, near_sq)
         value = (u + lift) * pl.reciprocal(u * (u + gap), approx=True)
         top = value.astype(bf16)
         low = (value - top.astype(f32)).astype(bf16)
         w = weights[:, at]
-        total = total + jnp.dot(w, top, preferred_element_type=f32)
-        return total + jnp.dot(w, low, preferred_element_type=f32)
-
-    total = lax.fori_loop(0, (filled + STEP - 1) // STEP, step, total)
+        acc[...] += jnp.dot(w, top, preferred_element_type=f32) + jnp.dot(
+            w, low, preferred_element_type=f32
+        )
+
+    steps = (filled + STEP // 2 - 1) // STEP
+
+    @pl.loop(0, steps)
+    def _(i):
+        step(i * STEP, STEP)
+
+    @pl.when(filled > steps * STEP)
+    def _():
+        step(steps * STEP, STEP // 2)
+
     if not last:
-        acc_out[...] = total
         return
     for copy in copies:
         copy.wait()
-    total = total[: 3 * width] + total[3 * width :]
+    total = acc[: 3 * width] + acc[3 * width :]
     lane = lax.broadcasted_iota(jnp.int32, (1, slots), 1)
     live = (lane < count[0]).astype(f32)
     unit = unit_of(pos[...]) * (live * scale)
@@ -246,9 +256,14 @@
     )
 
 
-def exchanged(block, axis, distance):
-    n = lax.axis_size(axis)
-    return lax.ppermute(block, axis, [(i ^ distance, i) for i in range(n)])
+def exchanged(block, distance):
+    blocks, sides = lax.axis_size("blk"), lax.axis_size("offs")
+    route = [
+        ((b ^ distance) * sides + sides - 1 - c, b * sides + c)
+        for b in range(blocks)
+        for c in range(sides)
+    ]
+    return lax.ppermute(block, ("blk", "offs"), route)
 
 
 def body(position, noise_var, rhs, block_count):
@@ -274,49 +289,55 @@
     acc_shape = shape((6 * width, slots), f32)
     rows_shape = shape((32, slots), bf16)
 
-    def pairs(fresh, count, first=False, last=False, rows=None, acc=None):
+    def pairs(known, start, count, last, rows=None, acc=None):
+        first = rows is None
+        args, specs = [known], [VMEM]
+        if first or last:
+            args.append(position)
+            specs.append(HBM)
+        if not first:
+            args += [rows, acc]
+            specs += [VMEM] * 2
         scratch = [
             pltpu.VMEM((32, count * half + STEP), bf16),
             pltpu.VMEM((6 * width, count * half + STEP), bf16),
         ]
-        if first:
-            args, specs = [fresh, position], [VMEM, HBM]
-            outs, out_specs = (rows_shape, acc_shape), (VMEM, VMEM)
-        else:
-            args, specs = [fresh, rows, acc], [VMEM] * 3
-            outs, out_specs = acc_shape, VMEM
         if first or last:
             scratch += [pltpu.SemaphoreType.DMA((4,)), pos_buf]
         if last:
-            args += [position, noise_var, rhs, block_count]
-            specs += [HBM] * 4
-            outs = shape((width, slots + LANES), f32)
+            args += [noise_var, rhs, block_count]
+            specs += [HBM] * 3
+            outs = (shape((width, slots + LANES), f32),)
+            scratch = [pltpu.VMEM(acc_shape.shape, f32)] + scratch
             scratch += [noise_buf, rhs_buf, count_buf]
-        kernel = functools.partial(pair_kernel, first, last, count, tiles)
+        else:
+            outs = (shape(known.shape, f32), acc_shape)
+            if first:
+                outs += (rows_shape,)
+        kernel = functools.partial(pair_kernel, first, last, start, count, tiles)
         flops = 2 * slots * count * half * 64
-        name = f"pairs_{count}"
-        return call(kernel, outs, specs, out_specs, scratch, name, flops)(*args)
-
-    known, fresh, count = packet, packet, 1
+        specs_out = (VMEM,) * len(outs)
+        return call(kernel, outs, specs, specs_out, scratch, f"pairs_{start}", flops)(*args)
+
+    known, start, count = packet, 0, 1
     rows = acc = None
     distance = blocks // 2
     while distance:
-        arrived = exchanged(known, "blk", distance)
+        arrived = exchanged(known, distance)
         if rows is None:
-            rows, acc = pairs(fresh, count, first=True)
+            known, acc, rows = pairs(known, start, count, False)
         else:
-            acc = pairs(fresh, count, rows=rows, acc=acc)
-            count *= 2
-        if distance > 1:
-            known = jnp.concatenate([known, arrived], axis=1)
-        fresh = arrived
+            known, acc = pairs(known, start, count, False, rows, acc)
+        start += count
+        count = start
+        known = jnp.concatenate([known, arrived], axis=1)
         distance //= 2
-    mine = pairs(fresh, count, last=True, rows=rows, acc=acc)
-    other = exchanged(mine, "offs", 1)
+    (mine,) = pairs(arrived, 0, count, True, rows, acc)
+    other = exchanged(mine, 0)
     small = mine[:, slots:] + other[:, slots:]
     distance = blocks // 2
     while distance:
-        small = small + exchanged(small, "blk", distance)
+        small = small + exchanged(small, distance)
         distance //= 2
 
     return tuple(

time: 39 us -> 35 us (0.90)
  waiting for transfers between devices: 13 us -> 6.92 us
  starting transfers between devices: 12 us -> 13.9 us
    ppermute x7, waiting for transfers between devices: 13 us -> 6.92 us  [exchanged(): return lax.ppermute(block, ('blk', 'offs'), route)]
    ppermute x7, starting transfers between devices: 12 us -> 13.9 us  [exchanged(): return lax.ppermute(block, ('blk', 'offs'), route)]
    unnamed x8 -> x12, local copies, waits for them, and re-layouts: 1.48 us -> 1.49 us
  transfers between devices with their start and end apart: 7 -> 7, of which waited for: 6 -> 7; matrix products, arithmetic and copies ran while one was open for 0% -> 0% of each run, Pallas kernels for 12% -> 14%
where the time goes in v2:
time: 35 us; the launch traced here: 34.8 us
  starting transfers between devices  13.9 us (40%)
  Pallas kernels  11.1 us (32%)
  waiting for transfers between devices  6.92 us (20%)
  local copies, waits for them, and re-layouts  1.5 us (4%)
  between operations  1.35 us (4%)
    ppermute x7, starting transfers between devices, exchanged(): return lax.ppermute(block, ('blk', 'offs'), route)  13.9 us
    pallas_call x4, Pallas kernels, pairs(): call(kernel, outs, specs, specs_out, scratch, f'pairs_{start}', flops)  8.78 us
    ppermute x7, waiting for transfers between devices, exchanged(): return lax.ppermute(block, ('blk', 'offs'), route)  6.92 us
    pallas_call x1, Pallas kernels, body(): call(tail_kernel, (shape(rhs.shape, f32),) * 2, [VMEM, VMEM, VMEM, HBM, H...  1.66 us
    unnamed x12, local copies, waits for them, and re-layouts  1.49 us
  transfers between devices with their start and end apart: 7, of which 7 were waited for; matrix products, arithmetic and copies ran while one was open for 0% of the time, Pallas kernels for 14%

profile of v2, /device:TPU:0, one launch (start us, length us, event | category | flops | bytes accessed | tf_op | source)
XLA Modules:
  0.0 34.8 jit_solution(4484526145082705837)
XLA Ops:
  1.3 0.0 copy-start
  1.3 0.7 %copy-done = f32[8,1024]{1,0:T(8,128)S(1)} copy-done((f32[8,1024]{1,0:T(8,128)S(1)}, f32[8,1024]{1,0:T(8,128)}, u32[]{:S(2)}) %copy-start) | copy-done | bytes 32792
  2.0 0.7 %copy-done.2 = f32[3,1024]{1,0:T(4,128)S(1)} copy-done((f32[3,1024]{1,0:T(4,128)S(1)}, f32[3,1024]{1,0:T(4,128)}, u32[]{:S(2)}) %copy-start.2) | copy-done | bytes 12312
  2.8 0.6 %pack.1.refs_0_ = f32[8,768]{1,0:T(8,128)S(1)} custom-call(f32[3,1024]{1,0:T(4,128)S(1)} %copy-done.2, f32[8,1024]{1,0:T(8,128)S(1)} %copy-done, s32[1]{0:T(128)S(6)} %copy.8.count_hbm.refs_6_), custom_call_target="tpu_custom_call" | custom-call | bytes 131072 | tf_op jit(solution)/shard_map/pack/pallas_call | solution.py:280
  3.4 3.5 %collective-permute-start = (f32[8,768]{1,0:T(8,128)S(1)}, f32[8,768]{1,0:T(8,128)S(1)}, u32[]{:S(2)}, u32[]{:S(2)}) collective-permute-start(f32[8,768]{1,0:T(8,128)S(1)} %pack.1.refs_0_), channel_id=1, source_target_pairs={{9,0},{8,1},{11,2},{10,3},{13,4},{12,5},{15,6},{14,7},{1,8},{0,9},... | collective-permute-start | bytes 73736 | tf_op jit(solution)/shard_map/ppermute | solution.py:266
  6.9 1.0 %pairs_0.2 = (f32[8,768]{1,0:T(8,128)S(1)}, f32[48,1024]{1,0:T(8,128)S(1)}, bf16[32,1024]{1,0:T(8,128)(2,1)S(1)}) custom-call(f32[8,768]{1,0:T(8,128)S(1)} %pack.1.refs_0_, f32[3,1024]{1,0:T(4,128)S(1)} %copy-done.2), custom_call_target="tpu_custom_call" | custom-call | flops 67108864 | bytes 131072 | tf_op jit(solution)/shard_map/pairs_0/pallas_call | solution.py:320
  7.9 0.6 %collective-permute-done = f32[8,768]{1,0:T(8,128)S(1)} collective-permute-done((f32[8,768]{1,0:T(8,128)S(1)}, f32[8,768]{1,0:T(8,128)S(1)}, u32[]{:S(2)}, u32[]{:S(2)}) %collective-permute-start) | collective-permute-done | bytes 24608 | tf_op jit(solution)/shard_map/ppermute | solution.py:266
  8.5 1.8 %collective-permute-start.1 = (f32[8,1536]{1,0:T(8,128)S(1)}, f32[8,1536]{1,0:T(8,128)S(1)}, u32[]{:S(2)}, u32[]{:S(2)}) collective-permute-start(f32[8,1536]{1,0:T(8,128)S(1)} %constant_dynamic-update-slice_fusion.refs_0_), channel_id=1, source_target_pairs={{5,0},{4,1},{7,2},{6,3},{1,4},{0,5},{3,6},{2,7},{13,8},{12,9},{15,... | collective-permute-start | bytes 147464 | tf_op jit(solution)/shard_map/ppermute | solution.py:266
  10.4 1.3 %pairs_1.1 = (f32[8,1536]{1,0:T(8,128)S(1)}, f32[48,1024]{1,0:T(8,128)S(1)}) custom-call(f32[8,1536]{1,0:T(8,128)S(1)} %constant_dynamic-update-slice_fusion.refs_0_, bf16[32,1024]{1,0:T(8,128)(2,1)S(1)} %get-tuple-element.9.refs_1_.refs_2_, f32[48,1024]{1,0:T(8,128)S(1)} %get-tuple-element.10.refs_2_), custom_call_target="tpu_custom_call" | custom-call | flops 67108864 | bytes 131072 | tf_op jit(solution)/shard_map/pairs_1/pallas_call | solution.py:320
  11.7 0.6 %collective-permute-done.1 = f32[8,1536]{1,0:T(8,128)S(1)} collective-permute-done((f32[8,1536]{1,0:T(8,128)S(1)}, f32[8,1536]{1,0:T(8,128)S(1)}, u32[]{:S(2)}, u32[]{:S(2)}) %collective-permute-start.1) | collective-permute-done | bytes 49184 | tf_op jit(solution)/shard_map/ppermute | solution.py:266
  12.2 1.8 %collective-permute-start.2 = (f32[8,3072]{1,0:T(8,128)S(1)}, f32[8,3072]{1,0:T(8,128)S(1)}, u32[]{:S(2)}, u32[]{:S(2)}) collective-permute-start(f32[8,3072]{1,0:T(8,128)S(1)} %constant_dynamic-update-slice_fusion.2.refs_0_), channel_id=1, source_target_pairs={{3,0},{2,1},{1,2},{0,3},{7,4},{6,5},{5,6},{4,7},{11,8},{10,9},{9,1... | collective-permute-start | bytes 294920 | tf_op jit(solution)/shard_map/ppermute | solution.py:266
  14.1 2.6 %pairs_2.1 = (f32[8,3072]{1,0:T(8,128)}, f32[48,1024]{1,0:T(8,128)S(1)}) custom-call(f32[8,3072]{1,0:T(8,128)S(1)} %constant_dynamic-update-slice_fusion.2.refs_0_, bf16[32,1024]{1,0:T(8,128)(2,1)S(1)} %get-tuple-element.9.refs_1_.refs_2_, f32[48,1024]{1,0:T(8,128)S(1)} %get-tuple-element.12.refs_2_), custom_call_target="tpu_custom_call" | custom-call | flops 134217728 | bytes 131072 | tf_op jit(solution)/shard_map/pairs_2/pallas_call | solution.py:320
  16.7 0.3 collective-permute-done.2.refs_0_
  17.0 0.0 copy-done.3
  17.0 3.9 %pairs_0.3.mine = f32[8,1152]{1,0:T(8,128)S(1)} custom-call(f32[8,3072]{1,0:T(8,128)S(1)} %collective-permute-done.2.refs_0_, f32[3,1024]{1,0:T(4,128)S(1)} %copy-done.3, bf16[32,1024]{1,0:T(8,128)(2,1)S(1)} %get-tuple-element.9.refs_1_.refs_2_, f32[48,1024]{1,0:T(8,128)S(1)} %get-tuple-element.13.refs_3_, f32[1024]{0:T(1024)S(1)} %copy-done.4, ...), custom_call_target="tpu_custom_call" | custom-call | flops 268435456 | bytes 131072 | tf_op jit(solution)/shard_map/pairs_0/pallas_call | solution.py:320
  20.9 0.2 collective-permute-start.3
  21.1 1.1 %collective-permute-done.3.other = f32[8,1152]{1,0:T(8,128)S(1)} collective-permute-done((f32[8,1152]{1,0:T(8,128)S(1)}, f32[8,1152]{1,0:T(8,128)S(1)}, u32[]{:S(2)}, u32[]{:S(2)}) %collective-permute-start.3) | collective-permute-done | bytes 36896 | tf_op jit(solution)/shard_map/ppermute | solution.py:266
  22.2 3.1 %collective-permute-start.4 = (f32[8,128]{1,0:T(8,128)S(1)}, f32[8,128]{1,0:T(8,128)S(1)}, u32[]{:S(2)}, u32[]{:S(2)}) collective-permute-start(f32[8,128]{1,0:T(8,128)S(1)} %slice_add_fusion), channel_id=1, source_target_pairs={{9,0},{8,1},{11,2},{10,3},{13,4},{12,5},{15,6},{14,7},{1,8},{0,9},... | collective-permute-start | bytes 12296 | tf_op jit(solution)/shard_map/ppermute | solution.py:266
  25.3 1.3 %collective-permute-done.4 = f32[8,128]{1,0:T(8,128)S(1)} collective-permute-done((f32[8,128]{1,0:T(8,128)S(1)}, f32[8,128]{1,0:T(8,128)S(1)}, u32[]{:S(2)}, u32[]{:S(2)}) %collective-permute-start.4) | collective-permute-done | bytes 4128 | tf_op jit(solution)/shard_map/ppermute | solution.py:266
  26.6 2.1 %collective-permute-start.5 = (f32[8,128]{1,0:T(8,128)S(1)}, f32[8,128]{1,0:T(8,128)S(1)}, u32[]{:S(2)}, u32[]{:S(2)}) collective-permute-start(f32[8,128]{1,0:T(8,128)S(1)} %add.13), channel_id=1, source_target_pairs={{5,0},{4,1},{7,2},{6,3},{1,4},{0,5},{3,6},{2,7},{13,8},{12,9},{15,... | collective-permute-start | bytes 12296 | tf_op jit(solution)/shard_map/ppermute | solution.py:266
  28.7 1.3 %collective-permute-done.5 = f32[8,128]{1,0:T(8,128)S(1)} collective-permute-done((f32[8,128]{1,0:T(8,128)S(1)}, f32[8,128]{1,0:T(8,128)S(1)}, u32[]{:S(2)}, u32[]{:S(2)}) %collective-permute-start.5) | collective-permute-done | bytes 4128 | tf_op jit(solution)/shard_map/ppermute | solution.py:266
  30.1 1.3 %collective-permute-start.6 = (f32[8,128]{1,0:T(8,128)S(1)}, f32[8,128]{1,0:T(8,128)S(1)}, u32[]{:S(2)}, u32[]{:S(2)}) collective-permute-start(f32[8,128]{1,0:T(8,128)S(1)} %add.14), channel_id=1, source_target_pairs={{3,0},{2,1},{1,2},{0,3},{7,4},{6,5},{5,6},{4,7},{11,8},{10,9},{9,1... | collective-permute-start | bytes 12296 | tf_op jit(solution)/shard_map/ppermute | solution.py:266
  31.3 1.7 %collective-permute-done.6 = f32[8,128]{1,0:T(8,128)S(1)} collective-permute-done((f32[8,128]{1,0:T(8,128)S(1)}, f32[8,128]{1,0:T(8,128)S(1)}, u32[]{:S(2)}, u32[]{:S(2)}) %collective-permute-start.6) | collective-permute-done | bytes 4128 | tf_op jit(solution)/shard_map/ppermute | solution.py:266
  33.1 1.7 %tail.1 = (f32[8,1024]{1,0:T(8,128)}, f32[8,1024]{1,0:T(8,128)}) custom-call(f32[8,128]{1,0:T(8,128)S(1)} %add.15.small, f32[8,1152]{1,0:T(8,128)S(1)} %pairs_0.3.mine, f32[8,1152]{1,0:T(8,128)S(1)} %collective-permute-done.3.other, f32[8,1024]{1,0:T(8,128)S(1)} %copy-done.1, s32[1]{0:T(128)S(6)} %copy.8.count_hbm.refs_6_), custom_call_target="tpu_custom_call" | custom-call | bytes 131072 | tf_op jit(solution)/shard_map/tail/pallas_call | solution.py:344
  (14 shorter events, 0.0 us)
Async XLA Ops:
  1.3 0.8 %copy-start = (f32[8,1024]{1,0:T(8,128)S(1)}, f32[8,1024]{1,0:T(8,128)}, u32[]{:S(2)}) copy-start(f32[8,1024]{1,0:T(8,128)} %rhs_hbm.3) | copy-start | bytes 98308
  2.0 0.7 %copy-start.2 = (f32[3,1024]{1,0:T(4,128)S(1)}, f32[3,1024]{1,0:T(4,128)}, u32[]{:S(2)}) copy-start(f32[3,1024]{1,0:T(4,128)} %refs_1_.3) | copy-start | bytes 36868
  3.4 5.1 %collective-permute-start = (f32[8,768]{1,0:T(8,128)S(1)}, f32[8,768]{1,0:T(8,128)S(1)}, u32[]{:S(2)}, u32[]{:S(2)}) collective-permute-start(f32[8,768]{1,0:T(8,128)S(1)} %pack.1.refs_0_), channel_id=1, source_target_pairs={{9,0},{8,1},{11,2},{10,3},{13,4},{12,5},{15,6},{14,7},{1,8},{0,9},... | collective-permute-start | bytes 73736 | tf_op jit(solution)/shard_map/ppermute | solution.py:266
  8.5 3.7 %collective-permute-start.1 = (f32[8,1536]{1,0:T(8,128)S(1)}, f32[8,1536]{1,0:T(8,128)S(1)}, u32[]{:S(2)}, u32[]{:S(2)}) collective-permute-start(f32[8,1536]{1,0:T(8,128)S(1)} %constant_dynamic-update-slice_fusion.refs_0_), channel_id=1, source_target_pairs={{5,0},{4,1},{7,2},{6,3},{1,4},{0,5},{3,6},{2,7},{13,8},{12,9},{15,... | collective-permute-start | bytes 147464 | tf_op jit(solution)/shard_map/ppermute | solution.py:266
  12.2 4.7 %collective-permute-start.2 = (f32[8,3072]{1,0:T(8,128)S(1)}, f32[8,3072]{1,0:T(8,128)S(1)}, u32[]{:S(2)}, u32[]{:S(2)}) collective-permute-start(f32[8,3072]{1,0:T(8,128)S(1)} %constant_dynamic-update-slice_fusion.2.refs_0_), channel_id=1, source_target_pairs={{3,0},{2,1},{1,2},{0,3},{7,4},{6,5},{5,6},{4,7},{11,8},{10,9},{9,1... | collective-permute-start | bytes 294920 | tf_op jit(solution)/shard_map/ppermute | solution.py:266
  14.1 2.9 %copy-start.1 = (f32[8,1024]{1,0:T(8,128)S(1)}, f32[8,1024]{1,0:T(8,128)}, u32[]{:S(2)}) copy-start(f32[8,1024]{1,0:T(8,128)} %rhs_hbm.3) | copy-start | bytes 98308
  14.1 2.9 %copy-start.3 = (f32[3,1024]{1,0:T(4,128)S(1)}, f32[3,1024]{1,0:T(4,128)}, u32[]{:S(2)}) copy-start(f32[3,1024]{1,0:T(4,128)} %refs_1_.3) | copy-start | bytes 36868
  14.1 2.9 %copy-start.4 = (f32[1024]{0:T(1024)S(1)}, f32[1024]{0:T(1024)}, u32[]{:S(2)}) copy-start(f32[1024]{0:T(1024)} %refs_4_.1) | copy-start | bytes 12292
  20.9 1.3 %collective-permute-start.3 = (f32[8,1152]{1,0:T(8,128)S(1)}, f32[8,1152]{1,0:T(8,128)S(1)}, u32[]{:S(2)}, u32[]{:S(2)}) collective-permute-start(f32[8,1152]{1,0:T(8,128)S(1)} %pairs_0.3.mine), channel_id=1, source_target_pairs={{1,0},{0,1},{3,2},{2,3},{5,4},{4,5},{7,6},{6,7},{9,8},{8,9},{11,10... | collective-permute-start | bytes 110600 | tf_op jit(solution)/shard_map/ppermute | solution.py:266
  22.2 4.4 %collective-permute-start.4 = (f32[8,128]{1,0:T(8,128)S(1)}, f32[8,128]{1,0:T(8,128)S(1)}, u32[]{:S(2)}, u32[]{:S(2)}) collective-permute-start(f32[8,128]{1,0:T(8,128)S(1)} %slice_add_fusion), channel_id=1, source_target_pairs={{9,0},{8,1},{11,2},{10,3},{13,4},{12,5},{15,6},{14,7},{1,8},{0,9},... | collective-permute-start | bytes 12296 | tf_op jit(solution)/shard_map/ppermute | solution.py:266
  26.6 3.4 %collective-permute-start.5 = (f32[8,128]{1,0:T(8,128)S(1)}, f32[8,128]{1,0:T(8,128)S(1)}, u32[]{:S(2)}, u32[]{:S(2)}) collective-permute-start(f32[8,128]{1,0:T(8,128)S(1)} %add.13), channel_id=1, source_target_pairs={{5,0},{4,1},{7,2},{6,3},{1,4},{0,5},{3,6},{2,7},{13,8},{12,9},{15,... | collective-permute-start | bytes 12296 | tf_op jit(solution)/shard_map/ppermute | solution.py:266
  30.1 3.0 %collective-permute-start.6 = (f32[8,128]{1,0:T(8,128)S(1)}, f32[8,128]{1,0:T(8,128)S(1)}, u32[]{:S(2)}, u32[]{:S(2)}) collective-permute-start(f32[8,128]{1,0:T(8,128)S(1)} %add.14), channel_id=1, source_target_pairs={{3,0},{2,1},{1,2},{0,3},{7,4},{6,5},{5,6},{4,7},{11,8},{10,9},{9,1... | collective-permute-start | bytes 12296 | tf_op jit(solution)/shard_map/ppermute | solution.py:266

commit v3 on v2

--- a/solution.py
+++ b/solution.py
@@ -34,31 +34,34 @@
     return top, mid, rest - mid
 
 
-def stack(rows, width):
-    rows = rows + [jnp.zeros((32 - len(rows), width), f32)]
-    return jnp.concatenate(rows, axis=0).astype(bf16)
-
-
 def row_side(pos):
     width = pos.shape[1]
-    rows = []
-    for k in range(3):
-        top, mid, low = split3(pos[k : k + 1])
-        rows += [top, mid, top, low, top, mid]
-    one = jnp.ones((1, width), f32)
-    square = jnp.sum(pos * pos, axis=0, keepdims=True) + near_sq
-    return stack(rows + [one] * 3 + list(split3(square)), width)
-
-
-def column_side(pos):
-    width = pos.shape[1]
-    rows = []
-    for k in range(3):
-        top, mid, low = split3(-2.0 * pos[k : k + 1])
-        rows += [top, top, mid, top, low, mid]
-    one = jnp.ones((1, width), f32)
-    square = jnp.sum(pos * pos, axis=0, keepdims=True)
-    return stack(rows + list(split3(square)) + [one] * 3, width)
+    one, none = jnp.ones((1, width), f32), jnp.zeros((1, width), f32)
+    top, mid, low = split3(pos)
+    square = split3(jnp.sum(pos * pos, axis=0, keepdims=True) + near_sq)
+    a = jnp.concatenate([top, one, mid, none], axis=0)
+    b = jnp.concatenate([top, one, low, none], axis=0)
+    c = jnp.concatenate([*square, *[none] * 5], axis=0)
+    return jnp.concatenate([a, b, a, c], axis=0).astype(bf16)
+
+
+def column_sides(group):
+    row = lax.broadcasted_iota(jnp.int32, group.shape, 0)
+    fourth = row % 4 == 3
+    upper = row < 4
+    square = group * group
+    square = sum(pltpu.roll(square, k, 0) for k in (1, 2, 3))
+    scaled = jnp.where(fourth, square, -2.0 * group)
+    ahead = split3(scaled)
+    swapped = [pltpu.roll(x, 4, 0) for x in ahead]
+    tail = jnp.where(upper, 1.0, 0.0)
+    sides = []
+    for (t, m, w), (tt, mm, _) in ((ahead, swapped), (swapped, ahead)):
+        pairs = [(t, tt), (m, tt), (w, mm)]
+        rows = [jnp.where(upper, x, y) for x, y in pairs] + [tail]
+        sides.append(jnp.concatenate(rows, axis=0).astype(bf16))
+    inverse = jnp.where(square > 0.0, lax.rsqrt(square), 0.0)
+    return sides, inverse
 
 
 def unit_of(pos):
@@ -134,20 +137,22 @@
     filled = jnp.int32(0)
     for b in range(start, start + blocks):
         base = b * stride
-        v = packet[:, base : base + half]
-        parts = []
         for t in range(tiles):
-            at = base + half + (t // 2) * LANES
+            if t % 2 == 0:
+                at = base + half + (t // 2) * LANES
+                group = packet[:, at : at + LANES]
+                sides, inverse = column_sides(group)
+            v = packet[:, base + t * LANES : base + (t + 1) * LANES]
             row = (t % 2) * 4
-            parts.append(packet[row : row + 3, at : at + LANES])
-        place = jnp.concatenate(parts, axis=1)
-        unit = unit_of(place)
-        product = jnp.concatenate([unit[k : k + 1] * v for k in range(3)], axis=0)
-        top = product.astype(bf16)
-        low = (product - top.astype(f32)).astype(bf16)
-        at = pl.ds(pl.multiple_of(filled, LANES), half)
-        cols[:, at] = column_side(place)
-        weights[:, at] = jnp.concatenate([top, low], axis=0)
+            v = v * inverse[row + 3 : row + 4]
+            rows = []
+            for k in range(3):
+                product = group[row + k : row + k + 1] * v
+                top = product.astype(bf16).astype(f32)
+                rows += [top, product - top]
+            at = pl.ds(pl.multiple_of(filled + t * LANES, LANES), LANES)
+            cols[:, at] = sides[t % 2]
+            weights[:, at] = jnp.concatenate(rows, axis=0).astype(bf16)
         held = jnp.max(packet[3:4, base + half : base + half + LANES])
         filled = filled + held.astype(jnp.int32) * LANES
     at = pl.ds(pl.multiple_of(filled, LANES), STEP)
@@ -193,11 +198,14 @@
         return
     for copy in copies:
         copy.wait()
-    total = acc[: 3 * width] + acc[3 * width :]
     lane = lax.broadcasted_iota(jnp.int32, (1, slots), 1)
     live = (lane < count[0]).astype(f32)
     unit = unit_of(pos[...]) * (live * scale)
-    image = sum(unit[k : k + 1] * total[k * width : (k + 1) * width] for k in range(3))
+    image = jnp.zeros((width, slots), f32)
+    for k in range(3):
+        at = 2 * k * width
+        pulled = acc[at : at + width] + acc[at + width : at + 2 * width]
+        image += unit[k : k + 1] * pulled
     direction = rhs[...] * live
     mine = (lax.axis_index("offs") == 0).astype(f32)
     noise_row = noise[...].reshape(1, slots)
@@ -284,7 +292,7 @@
         VMEM,
         [pos_buf, rhs_buf, count_buf, pltpu.SemaphoreType.DMA((3,))],
         "pack",
-    )(position, rhs, block_count)
+    )(*(pltpu.with_memory_space_constraint(x, pltpu.HBM) for x in (position, rhs)), block_count)
 
     acc_shape = shape((6 * width, slots), f32)
     rows_shape = shape((32, slots), bf16)

time: 35 us -> 34 us (0.971)
  local copies, waits for them, and re-layouts: 1.5 us -> 0.03 us
  Pallas kernels: 11.1 us -> 11.6 us
    unnamed x12 -> x8, local copies, waits for them, and re-layouts: 1.49 us -> 0.02 us
  transfers between devices with their start and end apart: 7 -> 7, of which waited for: 7 -> 6; matrix products, arithmetic and copies ran while one was open for 0% -> 0% of each run, Pallas kernels for 14% -> 16%
where the time goes in v3:
time: 34 us; the launch traced here: 33.4 us
  starting transfers between devices  13.7 us (40%)
  Pallas kernels  11.6 us (34%)
  waiting for transfers between devices  6.73 us (20%)
  between operations  1.35 us (4%)
    ppermute x7, starting transfers between devices, exchanged(): return lax.ppermute(block, ('blk', 'offs'), route)  13.7 us
    pallas_call x4, Pallas kernels, pairs(): call(kernel, outs, specs, specs_out, scratch, f'pairs_{start}', flops)  9.09 us
    ppermute x7, waiting for transfers between devices, exchanged(): return lax.ppermute(block, ('blk', 'offs'), route)  6.73 us
    pallas_call x1, Pallas kernels, body(): call(tail_kernel, (shape(rhs.shape, f32),) * 2, [VMEM, VMEM, VMEM, HBM, H...  1.66 us
    pallas_call x1, Pallas kernels, body(): call(pack_kernel, shape((width, half + half // 2), f32), [HBM, HBM, HBM],...  0.85 us
  transfers between devices with their start and end apart: 7, of which 6 were waited for; matrix products, arithmetic and copies ran while one was open for 0% of the time, Pallas kernels for 16%

profile of v3, /device:TPU:0, one launch (start us, length us, event | category | flops | bytes accessed | tf_op | source)
XLA Modules:
  0.0 33.4 jit_solution(5397591200768975405)
XLA Ops:
  1.3 0.0 copy-start.1
  1.3 0.8 %pack.1.refs_0_ = f32[8,768]{1,0:T(8,128)S(1)} custom-call(f32[3,1024]{1,0:T(4,128)} %refs_1_.3, f32[8,1024]{1,0:T(8,128)} %rhs_hbm.3, s32[1]{0:T(128)S(6)} %copy.8.count_hbm.refs_6_), custom_call_target="tpu_custom_call" | custom-call | bytes 131072 | tf_op jit(solution)/shard_map/pack/pallas_call | solution.py:288
  2.1 3.5 %collective-permute-start = (f32[8,768]{1,0:T(8,128)S(1)}, f32[8,768]{1,0:T(8,128)S(1)}, u32[]{:S(2)}, u32[]{:S(2)}) collective-permute-start(f32[8,768]{1,0:T(8,128)S(1)} %pack.1.refs_0_), channel_id=1, source_target_pairs={{9,0},{8,1},{11,2},{10,3},{13,4},{12,5},{15,6},{14,7},{1,8},{0,9},... | collective-permute-start | bytes 73736 | tf_op jit(solution)/shard_map/ppermute | solution.py:274
  5.7 0.0 copy-done.1
  5.7 1.3 %pairs_0.2 = (f32[8,768]{1,0:T(8,128)S(1)}, f32[48,1024]{1,0:T(8,128)S(1)}, bf16[32,1024]{1,0:T(8,128)(2,1)S(1)}) custom-call(f32[8,768]{1,0:T(8,128)S(1)} %pack.1.refs_0_, f32[3,1024]{1,0:T(4,128)S(1)} %copy-done.1), custom_call_target="tpu_custom_call" | custom-call | flops 67108864 | bytes 131072 | tf_op jit(solution)/shard_map/pairs_0/pallas_call | solution.py:328
  7.1 0.2 collective-permute-done
  7.3 1.8 %collective-permute-start.1 = (f32[8,1536]{1,0:T(8,128)S(1)}, f32[8,1536]{1,0:T(8,128)S(1)}, u32[]{:S(2)}, u32[]{:S(2)}) collective-permute-start(f32[8,1536]{1,0:T(8,128)S(1)} %constant_dynamic-update-slice_fusion.refs_0_), channel_id=1, source_target_pairs={{5,0},{4,1},{7,2},{6,3},{1,4},{0,5},{3,6},{2,7},{13,8},{12,9},{15,... | collective-permute-start | bytes 147464 | tf_op jit(solution)/shard_map/ppermute | solution.py:274
  9.1 0.9 %pairs_1.1 = (f32[8,1536]{1,0:T(8,128)S(1)}, f32[48,1024]{1,0:T(8,128)S(1)}) custom-call(f32[8,1536]{1,0:T(8,128)S(1)} %constant_dynamic-update-slice_fusion.refs_0_, bf16[32,1024]{1,0:T(8,128)(2,1)S(1)} %get-tuple-element.9.refs_1_.refs_2_, f32[48,1024]{1,0:T(8,128)S(1)} %get-tuple-element.10.refs_2_), custom_call_target="tpu_custom_call" | custom-call | flops 67108864 | bytes 131072 | tf_op jit(solution)/shard_map/pairs_1/pallas_call | solution.py:328
  10.0 1.0 %collective-permute-done.1 = f32[8,1536]{1,0:T(8,128)S(1)} collective-permute-done((f32[8,1536]{1,0:T(8,128)S(1)}, f32[8,1536]{1,0:T(8,128)S(1)}, u32[]{:S(2)}, u32[]{:S(2)}) %collective-permute-start.1) | collective-permute-done | bytes 49184 | tf_op jit(solution)/shard_map/ppermute | solution.py:274
  11.0 1.8 %collective-permute-start.2 = (f32[8,3072]{1,0:T(8,128)S(1)}, f32[8,3072]{1,0:T(8,128)S(1)}, u32[]{:S(2)}, u32[]{:S(2)}) collective-permute-start(f32[8,3072]{1,0:T(8,128)S(1)} %constant_dynamic-update-slice_fusion.2.refs_0_), channel_id=1, source_target_pairs={{3,0},{2,1},{1,2},{0,3},{7,4},{6,5},{5,6},{4,7},{11,8},{10,9},{9,1... | collective-permute-start | bytes 294920 | tf_op jit(solution)/shard_map/ppermute | solution.py:274
  12.8 3.0 %pairs_2.1 = (f32[8,3072]{1,0:T(8,128)}, f32[48,1024]{1,0:T(8,128)S(1)}) custom-call(f32[8,3072]{1,0:T(8,128)S(1)} %constant_dynamic-update-slice_fusion.2.refs_0_, bf16[32,1024]{1,0:T(8,128)(2,1)S(1)} %get-tuple-element.9.refs_1_.refs_2_, f32[48,1024]{1,0:T(8,128)S(1)} %get-tuple-element.12.refs_2_), custom_call_target="tpu_custom_call" | custom-call | flops 134217728 | bytes 131072 | tf_op jit(solution)/shard_map/pairs_2/pallas_call | solution.py:328
  15.8 0.0 collective-permute-done.2.refs_0_
  15.8 0.0 copy-done
  15.8 0.0 copy-done.2
  15.8 3.9 %pairs_0.3.mine = f32[8,1152]{1,0:T(8,128)S(1)} custom-call(f32[8,3072]{1,0:T(8,128)S(1)} %collective-permute-done.2.refs_0_, f32[3,1024]{1,0:T(4,128)S(1)} %copy-done.1, bf16[32,1024]{1,0:T(8,128)(2,1)S(1)} %get-tuple-element.9.refs_1_.refs_2_, f32[48,1024]{1,0:T(8,128)S(1)} %get-tuple-element.13.refs_3_, f32[1024]{0:T(1024)S(1)} %copy-done.2, ...), custom_call_target="tpu_custom_call" | custom-call | flops 268435456 | bytes 131072 | tf_op jit(solution)/shard_map/pairs_0/pallas_call | solution.py:328
  19.7 0.2 collective-permute-start.3
  19.9 1.1 %collective-permute-done.3.other = f32[8,1152]{1,0:T(8,128)S(1)} collective-permute-done((f32[8,1152]{1,0:T(8,128)S(1)}, f32[8,1152]{1,0:T(8,128)S(1)}, u32[]{:S(2)}, u32[]{:S(2)}) %collective-permute-start.3) | collective-permute-done | bytes 36896 | tf_op jit(solution)/shard_map/ppermute | solution.py:274
  21.0 3.0 %collective-permute-start.4 = (f32[8,128]{1,0:T(8,128)S(1)}, f32[8,128]{1,0:T(8,128)S(1)}, u32[]{:S(2)}, u32[]{:S(2)}) collective-permute-start(f32[8,128]{1,0:T(8,128)S(1)} %slice_add_fusion), channel_id=1, source_target_pairs={{9,0},{8,1},{11,2},{10,3},{13,4},{12,5},{15,6},{14,7},{1,8},{0,9},... | collective-permute-start | bytes 12296 | tf_op jit(solution)/shard_map/ppermute | solution.py:274
  24.0 1.3 %collective-permute-done.4 = f32[8,128]{1,0:T(8,128)S(1)} collective-permute-done((f32[8,128]{1,0:T(8,128)S(1)}, f32[8,128]{1,0:T(8,128)S(1)}, u32[]{:S(2)}, u32[]{:S(2)}) %collective-permute-start.4) | collective-permute-done | bytes 4128 | tf_op jit(solution)/shard_map/ppermute | solution.py:274
  25.3 2.1 %collective-permute-start.5 = (f32[8,128]{1,0:T(8,128)S(1)}, f32[8,128]{1,0:T(8,128)S(1)}, u32[]{:S(2)}, u32[]{:S(2)}) collective-permute-start(f32[8,128]{1,0:T(8,128)S(1)} %add.13), channel_id=1, source_target_pairs={{5,0},{4,1},{7,2},{6,3},{1,4},{0,5},{3,6},{2,7},{13,8},{12,9},{15,... | collective-permute-start | bytes 12296 | tf_op jit(solution)/shard_map/ppermute | solution.py:274
  27.4 1.3 %collective-permute-done.5 = f32[8,128]{1,0:T(8,128)S(1)} collective-permute-done((f32[8,128]{1,0:T(8,128)S(1)}, f32[8,128]{1,0:T(8,128)S(1)}, u32[]{:S(2)}, u32[]{:S(2)}) %collective-permute-start.5) | collective-permute-done | bytes 4128 | tf_op jit(solution)/shard_map/ppermute | solution.py:274
  28.7 1.2 %collective-permute-start.6 = (f32[8,128]{1,0:T(8,128)S(1)}, f32[8,128]{1,0:T(8,128)S(1)}, u32[]{:S(2)}, u32[]{:S(2)}) collective-permute-start(f32[8,128]{1,0:T(8,128)S(1)} %add.14), channel_id=1, source_target_pairs={{3,0},{2,1},{1,2},{0,3},{7,4},{6,5},{5,6},{4,7},{11,8},{10,9},{9,1... | collective-permute-start | bytes 12296 | tf_op jit(solution)/shard_map/ppermute | solution.py:274
  30.0 1.8 %collective-permute-done.6 = f32[8,128]{1,0:T(8,128)S(1)} collective-permute-done((f32[8,128]{1,0:T(8,128)S(1)}, f32[8,128]{1,0:T(8,128)S(1)}, u32[]{:S(2)}, u32[]{:S(2)}) %collective-permute-start.6) | collective-permute-done | bytes 4128 | tf_op jit(solution)/shard_map/ppermute | solution.py:274
  31.8 1.7 %tail.1 = (f32[8,1024]{1,0:T(8,128)}, f32[8,1024]{1,0:T(8,128)}) custom-call(f32[8,128]{1,0:T(8,128)S(1)} %add.15.small, f32[8,1152]{1,0:T(8,128)S(1)} %pairs_0.3.mine, f32[8,1152]{1,0:T(8,128)S(1)} %collective-permute-done.3.other, f32[8,1024]{1,0:T(8,128)S(1)} %copy-done, s32[1]{0:T(128)S(6)} %copy.8.count_hbm.refs_6_), custom_call_target="tpu_custom_call" | custom-call | bytes 131072 | tf_op jit(solution)/shard_map/tail/pallas_call | solution.py:352
  (10 shorter events, 0.0 us)
Async XLA Ops:
  1.3 4.4 %copy-start.1 = (f32[3,1024]{1,0:T(4,128)S(1)}, f32[3,1024]{1,0:T(4,128)}, u32[]{:S(2)}) copy-start(f32[3,1024]{1,0:T(4,128)} %refs_1_.3) | copy-start | bytes 36868
  2.1 5.1 %collective-permute-start = (f32[8,768]{1,0:T(8,128)S(1)}, f32[8,768]{1,0:T(8,128)S(1)}, u32[]{:S(2)}, u32[]{:S(2)}) collective-permute-start(f32[8,768]{1,0:T(8,128)S(1)} %pack.1.refs_0_), channel_id=1, source_target_pairs={{9,0},{8,1},{11,2},{10,3},{13,4},{12,5},{15,6},{14,7},{1,8},{0,9},... | collective-permute-start | bytes 73736 | tf_op jit(solution)/shard_map/ppermute | solution.py:274
  7.3 3.7 %collective-permute-start.1 = (f32[8,1536]{1,0:T(8,128)S(1)}, f32[8,1536]{1,0:T(8,128)S(1)}, u32[]{:S(2)}, u32[]{:S(2)}) collective-permute-start(f32[8,1536]{1,0:T(8,128)S(1)} %constant_dynamic-update-slice_fusion.refs_0_), channel_id=1, source_target_pairs={{5,0},{4,1},{7,2},{6,3},{1,4},{0,5},{3,6},{2,7},{13,8},{12,9},{15,... | collective-permute-start | bytes 147464 | tf_op jit(solution)/shard_map/ppermute | solution.py:274
  11.0 4.9 %collective-permute-start.2 = (f32[8,3072]{1,0:T(8,128)S(1)}, f32[8,3072]{1,0:T(8,128)S(1)}, u32[]{:S(2)}, u32[]{:S(2)}) collective-permute-start(f32[8,3072]{1,0:T(8,128)S(1)} %constant_dynamic-update-slice_fusion.2.refs_0_), channel_id=1, source_target_pairs={{3,0},{2,1},{1,2},{0,3},{7,4},{6,5},{5,6},{4,7},{11,8},{10,9},{9,1... | collective-permute-start | bytes 294920 | tf_op jit(solution)/shard_map/ppermute | solution.py:274
  12.8 3.0 %copy-start = (f32[8,1024]{1,0:T(8,128)S(1)}, f32[8,1024]{1,0:T(8,128)}, u32[]{:S(2)}) copy-start(f32[8,1024]{1,0:T(8,128)} %rhs_hbm.3) | copy-start | bytes 98308
  12.8 3.0 %copy-start.2 = (f32[1024]{0:T(1024)S(1)}, f32[1024]{0:T(1024)}, u32[]{:S(2)}) copy-start(f32[1024]{0:T(1024)} %refs_4_.1) | copy-start | bytes 12292
  19.7 1.3 %collective-permute-start.3 = (f32[8,1152]{1,0:T(8,128)S(1)}, f32[8,1152]{1,0:T(8,128)S(1)}, u32[]{:S(2)}, u32[]{:S(2)}) collective-permute-start(f32[8,1152]{1,0:T(8,128)S(1)} %pairs_0.3.mine), channel_id=1, source_target_pairs={{1,0},{0,1},{3,2},{2,3},{5,4},{4,5},{7,6},{6,7},{9,8},{8,9},{11,10... | collective-permute-start | bytes 110600 | tf_op jit(solution)/shard_map/ppermute | solution.py:274
  21.0 4.3 %collective-permute-start.4 = (f32[8,128]{1,0:T(8,128)S(1)}, f32[8,128]{1,0:T(8,128)S(1)}, u32[]{:S(2)}, u32[]{:S(2)}) collective-permute-start(f32[8,128]{1,0:T(8,128)S(1)} %slice_add_fusion), channel_id=1, source_target_pairs={{9,0},{8,1},{11,2},{10,3},{13,4},{12,5},{15,6},{14,7},{1,8},{0,9},... | collective-permute-start | bytes 12296 | tf_op jit(solution)/shard_map/ppermute | solution.py:274
  25.3 3.4 %collective-permute-start.5 = (f32[8,128]{1,0:T(8,128)S(1)}, f32[8,128]{1,0:T(8,128)S(1)}, u32[]{:S(2)}, u32[]{:S(2)}) collective-permute-start(f32[8,128]{1,0:T(8,128)S(1)} %add.13), channel_id=1, source_target_pairs={{5,0},{4,1},{7,2},{6,3},{1,4},{0,5},{3,6},{2,7},{13,8},{12,9},{15,... | collective-permute-start | bytes 12296 | tf_op jit(solution)/shard_map/ppermute | solution.py:274
  28.7 3.0 %collective-permute-start.6 = (f32[8,128]{1,0:T(8,128)S(1)}, f32[8,128]{1,0:T(8,128)S(1)}, u32[]{:S(2)}, u32[]{:S(2)}) collective-permute-start(f32[8,128]{1,0:T(8,128)S(1)} %add.14), channel_id=1, source_target_pairs={{3,0},{2,1},{1,2},{0,3},{7,4},{6,5},{5,6},{4,7},{11,8},{10,9},{9,1... | collective-permute-start | bytes 12296 | tf_op jit(solution)/shard_map/ppermute | solution.py:274

commit v4 on v3

--- a/solution.py
+++ b/solution.py
@@ -18,7 +18,8 @@
 lift = near_weight * near_sq * gap / scale
 
 LANES = 128
-STEP = 512
+UNIT = 256
+STEP = 1024
 f32 = jnp.float32
 bf16 = jnp.bfloat16
 VMEM = pl.BlockSpec(memory_space=pltpu.VMEM)
@@ -67,6 +68,17 @@
 def unit_of(pos):
     square = jnp.sum(pos * pos, axis=0, keepdims=True)
     return pos * jnp.where(square > 0.0, lax.rsqrt(square), 0.0)
+
+
+def gram(left, right, first):
+    width, slots = left.shape
+    lane = lax.broadcasted_iota(jnp.int32, (width, LANES), 1)
+    out = jnp.zeros((width, LANES), f32)
+    for s in range(width):
+        product = left * right[s : s + 1]
+        folded = sum(product[:, t : t + LANES] for t in range(0, slots, LANES))
+        out = jnp.where(lane == first + s, jnp.sum(folded, axis=1, keepdims=True), out)
+    return out
 
 
 def pack_kernel(pos_hbm, rhs_hbm, count_hbm, out, pos, rhs, count, sems):
@@ -107,11 +119,14 @@
     if not first:
         rows_in, acc_in = refs.pop(0), refs.pop(0)
     if last:
+        norm = refs.pop(0)
         noise_hbm, rhs_hbm, count_hbm, out = (refs.pop(0) for _ in range(4))
         acc = refs.pop(0)
     else:
         known_out, acc = refs.pop(0), refs.pop(0)
         rows_ref = refs.pop(0) if first else rows_in
+        if first:
+            norm = refs.pop(0)
     if last:
         rows_ref = rows_in
     cols, weights = refs.pop(0), refs.pop(0)
@@ -155,44 +170,50 @@
             weights[:, at] = jnp.concatenate(rows, axis=0).astype(bf16)
         held = jnp.max(packet[3:4, base + half : base + half + LANES])
         filled = filled + held.astype(jnp.int32) * LANES
-    at = pl.ds(pl.multiple_of(filled, LANES), STEP)
-    cols[:, at] = jnp.zeros((cols.shape[0], STEP), bf16)
-    weights[:, at] = jnp.zeros((weights.shape[0], STEP), bf16)
+    at = pl.ds(pl.multiple_of(filled, LANES), UNIT)
+    cols[:, at] = jnp.zeros((cols.shape[0], UNIT), bf16)
+    weights[:, at] = jnp.zeros((weights.shape[0], UNIT), bf16)
 
     slots = acc.shape[1]
     if first:
         copies[0].wait()
         rows_ref[...] = row_side(pos[...])
+        norm[...] = gram(packet[:, :half], packet[:, :half], width)
         acc[...] = jnp.zeros(acc.shape, f32)
     else:
         acc[...] = acc_in[...]
 
     def step(begin, size):
         at = pl.ds(pl.multiple_of(begin, LANES), size)
-        u = lax.dot_general(
-            cols[:, at],
-            rows_ref[...],
-            (((0,), (0,)), ((), ())),
-            preferred_element_type=f32,
-        )
-        u = jnp.maximum(u, near_sq)
-        value = (u + lift) * pl.reciprocal(u * (u + gap), approx=True)
-        top = value.astype(bf16)
-        low = (value - top.astype(f32)).astype(bf16)
-        w = weights[:, at]
-        acc[...] += jnp.dot(w, top, preferred_element_type=f32) + jnp.dot(
-            w, low, preferred_element_type=f32
-        )
-
-    steps = (filled + STEP // 2 - 1) // STEP
+        side, w = cols[:, at], weights[:, at]
+        for r in range(0, slots, UNIT):
+            near = slice(r, r + UNIT)
+            u = lax.dot_general(
+                side,
+                rows_ref[:, near],
+                (((0,), (0,)), ((), ())),
+                preferred_element_type=f32,
+            )
+            u = jnp.maximum(u, near_sq)
+            value = (u + lift) * pl.reciprocal(u * (u + gap), approx=True)
+            top = value.astype(bf16)
+            low = (value - top.astype(f32)).astype(bf16)
+            part = acc[:, near] + jnp.dot(w, top, preferred_element_type=f32)
+            acc[:, near] = part + jnp.dot(w, low, preferred_element_type=f32)
+
+    full = min(STEP, blocks * half)
+    steps = (filled + UNIT - LANES) // full
+    rest = filled - steps * full
 
     @pl.loop(0, steps)
     def _(i):
-        step(i * STEP, STEP)
-
-    @pl.when(filled > steps * STEP)
-    def _():
-        step(steps * STEP, STEP // 2)
+        step(i * full, full)
+
+    for size in range(UNIT, full, UNIT):
+
+        @pl.when((rest > size - UNIT) & (rest <= size))
+        def _(size=size):
+            step(steps * full, size)
 
     if not last:
         return
@@ -211,13 +232,7 @@
     noise_row = noise[...].reshape(1, slots)
     image = image + (mine * noise_row * live) * direction
     out[:, :slots] = image
-    dims = (((1,), (1,)), ((), ()))
-    both = jnp.concatenate([image, direction * mine], axis=0)
-    small = lax.dot_general(
-        direction, both, dims, precision=highest, preferred_element_type=f32
-    )
-    pad = jnp.zeros((width, LANES - 2 * width), f32)
-    out[:, slots:] = jnp.concatenate([small, pad], axis=1)
+    out[:, slots:] = norm[...] + gram(direction, image, 0)
 
 
 def tail_kernel(small, mine, other, rhs_hbm, count_hbm, sol, res, rhs, count, sems):
@@ -297,7 +312,7 @@
     acc_shape = shape((6 * width, slots), f32)
     rows_shape = shape((32, slots), bf16)
 
-    def pairs(known, start, count, last, rows=None, acc=None):
+    def pairs(known, start, count, last, rows=None, acc=None, norm=None):
         first = rows is None
         args, specs = [known], [VMEM]
         if first or last:
@@ -307,21 +322,21 @@
             args += [rows, acc]
             specs += [VMEM] * 2
         scratch = [
-            pltpu.VMEM((32, count * half + STEP), bf16),
-            pltpu.VMEM((6 * width, count * half + STEP), bf16),
+            pltpu.VMEM((32, count * half + UNIT), bf16),
+            pltpu.VMEM((6 * width, count * half + UNIT), bf16),
         ]
         if first or last:
             scratch += [pltpu.SemaphoreType.DMA((4,)), pos_buf]
         if last:
-            args += [noise_var, rhs, block_count]
-            specs += [HBM] * 3
+            args += [norm, noise_var, rhs, block_count]
+            specs += [VMEM] + [HBM] * 3
             outs = (shape((width, slots + LANES), f32),)
             scratch = [pltpu.VMEM(acc_shape.shape, f32)] + scratch
             scratch += [noise_buf, rhs_buf, count_buf]
         else:
             outs = (shape(known.shape, f32), acc_shape)
             if first:
-                outs += (rows_shape,)
+                outs += (rows_shape, shape((width, LANES), f32))
         kernel = functools.partial(pair_kernel, first, last, start, count, tiles)
         flops = 2 * slots * count * half * 64
         specs_out = (VMEM,) * len(outs)
@@ -333,14 +348,14 @@
     while distance:
         arrived = exchanged(known, distance)
         if rows is None:
-            known, acc, rows = pairs(known, start, count, False)
+            known, acc, rows, norm = pairs(known, start, count, False)
         else:
             known, acc = pairs(known, start, count, False, rows, acc)
         start += count
         count = start
         known = jnp.concatenate([known, arrived], axis=1)
         distance //= 2
-    (mine,) = pairs(arrived, 0, count, True, rows, acc)
+    (mine,) = pairs(arrived, 0, count, True, rows, acc, norm)
     other = exchanged(mine, 0)
     small = mine[:, slots:] + other[:, slots:]
     distance = blocks // 2

time: 34 us -> 32.9 us (0.968); the launches traced: 33.4 us -> 32.7 us
  Pallas kernels: 11.6 us -> 9.22 us
  starting transfers between devices: 13.7 us -> 15.5 us
    pallas_call x4, Pallas kernels: 9.09 us -> 6.73 us  [pairs(): call(kernel, outs, specs, specs_out, scratch, f'pairs_{start}', flops)]
    ppermute x7, starting transfers between devices: 13.7 us -> 15.5 us  [exchanged(): return lax.ppermute(block, ('blk', 'offs'), route)]
  transfers between devices with their start and end apart: 7 -> 7, of which waited for: 6 -> 7; matrix products, arithmetic and copies ran while one was open for 0% -> 0% of each run, Pallas kernels for 16% -> 14%
where the time goes in v4:
time: 32.9 us; the launch traced here: 32.7 us
  starting transfers between devices  15.5 us (47%)
  Pallas kernels  9.22 us (28%)
  waiting for transfers between devices  6.56 us (20%)
  between operations  1.35 us (4%)
    ppermute x7, starting transfers between devices, exchanged(): return lax.ppermute(block, ('blk', 'offs'), route)  15.5 us
    pallas_call x4, Pallas kernels, pairs(): call(kernel, outs, specs, specs_out, scratch, f'pairs_{start}', flops)  6.73 us
    ppermute x7, waiting for transfers between devices, exchanged(): return lax.ppermute(block, ('blk', 'offs'), route)  6.56 us
    pallas_call x1, Pallas kernels, body(): call(tail_kernel, (shape(rhs.shape, f32),) * 2, [VMEM, VMEM, VMEM, HBM, H...  1.65 us
    pallas_call x1, Pallas kernels, body(): call(pack_kernel, shape((width, half + half // 2), f32), [HBM, HBM, HBM],...  0.85 us
  transfers between devices with their start and end apart: 7, of which 7 were waited for; matrix products, arithmetic and copies ran while one was open for 0% of the time, Pallas kernels for 14%

profile of v4, /device:TPU:0, one launch (start us, length us, event | category | flops | bytes accessed | tf_op | source)
XLA Modules:
  0.0 32.7 jit_solution(16419328766114530935)
XLA Ops:
  1.3 0.0 copy-start.1
  1.3 0.8 %pack.1.refs_0_ = f32[8,768]{1,0:T(8,128)S(1)} custom-call(f32[3,1024]{1,0:T(4,128)} %refs_1_.3, f32[8,1024]{1,0:T(8,128)} %rhs_hbm.3, s32[1]{0:T(128)S(6)} %copy.8.count_hbm.refs_7_), custom_call_target="tpu_custom_call" | custom-call | bytes 131072 | tf_op jit(solution)/shard_map/pack/pallas_call | solution.py:303
  2.1 3.5 %collective-permute-start = (f32[8,768]{1,0:T(8,128)S(1)}, f32[8,768]{1,0:T(8,128)S(1)}, u32[]{:S(2)}, u32[]{:S(2)}) collective-permute-start(f32[8,768]{1,0:T(8,128)S(1)} %pack.1.refs_0_), channel_id=1, source_target_pairs={{9,0},{8,1},{11,2},{10,3},{13,4},{12,5},{15,6},{14,7},{1,8},{0,9},... | collective-permute-start | bytes 73736 | tf_op jit(solution)/shard_map/ppermute | solution.py:289
  5.7 0.0 copy-done.1
  5.7 0.9 %pairs_0.2 = (f32[8,768]{1,0:T(8,128)S(1)}, f32[48,1024]{1,0:T(8,128)S(1)}, bf16[32,1024]{1,0:T(8,128)(2,1)S(1)}, f32[8,128]{1,0:T(8,128)S(1)}) custom-call(f32[8,768]{1,0:T(8,128)S(1)} %pack.1.refs_0_, f32[3,1024]{1,0:T(4,128)S(1)} %copy-done.1), custom_call_target="tpu_custom_call" | custom-call | flops 67108864 | bytes 131072 | tf_op jit(solution)/shard_map/pairs_0/pallas_call | solution.py:343
  6.7 0.6 %collective-permute-done = f32[8,768]{1,0:T(8,128)S(1)} collective-permute-done((f32[8,768]{1,0:T(8,128)S(1)}, f32[8,768]{1,0:T(8,128)S(1)}, u32[]{:S(2)}, u32[]{:S(2)}) %collective-permute-start) | collective-permute-done | bytes 24608 | tf_op jit(solution)/shard_map/ppermute | solution.py:289
  7.3 1.8 %collective-permute-start.1 = (f32[8,1536]{1,0:T(8,128)S(1)}, f32[8,1536]{1,0:T(8,128)S(1)}, u32[]{:S(2)}, u32[]{:S(2)}) collective-permute-start(f32[8,1536]{1,0:T(8,128)S(1)} %constant_dynamic-update-slice_fusion.refs_0_), channel_id=1, source_target_pairs={{5,0},{4,1},{7,2},{6,3},{1,4},{0,5},{3,6},{2,7},{13,8},{12,9},{15,... | collective-permute-start | bytes 147464 | tf_op jit(solution)/shard_map/ppermute | solution.py:289
  9.1 1.1 %pairs_1.1 = (f32[8,1536]{1,0:T(8,128)S(1)}, f32[48,1024]{1,0:T(8,128)S(1)}) custom-call(f32[8,1536]{1,0:T(8,128)S(1)} %constant_dynamic-update-slice_fusion.refs_0_, bf16[32,1024]{1,0:T(8,128)(2,1)S(1)} %get-tuple-element.10.refs_1_.refs_2_, f32[48,1024]{1,0:T(8,128)S(1)} %get-tuple-element.11.refs_2_), custom_call_target="tpu_custom_call" | custom-call | flops 67108864 | bytes 131072 | tf_op jit(solution)/shard_map/pairs_1/pallas_call | solution.py:343
  10.3 0.7 %collective-permute-done.1 = f32[8,1536]{1,0:T(8,128)S(1)} collective-permute-done((f32[8,1536]{1,0:T(8,128)S(1)}, f32[8,1536]{1,0:T(8,128)S(1)}, u32[]{:S(2)}, u32[]{:S(2)}) %collective-permute-start.1) | collective-permute-done | bytes 49184 | tf_op jit(solution)/shard_map/ppermute | solution.py:289
  11.0 1.8 %collective-permute-start.2 = (f32[8,3072]{1,0:T(8,128)S(1)}, f32[8,3072]{1,0:T(8,128)S(1)}, u32[]{:S(2)}, u32[]{:S(2)}) collective-permute-start(f32[8,3072]{1,0:T(8,128)S(1)} %constant_dynamic-update-slice_fusion.2.refs_0_), channel_id=1, source_target_pairs={{3,0},{2,1},{1,2},{0,3},{7,4},{6,5},{5,6},{4,7},{11,8},{10,9},{9,1... | collective-permute-start | bytes 294920 | tf_op jit(solution)/shard_map/ppermute | solution.py:289
  12.8 2.5 %pairs_2.1 = (f32[8,3072]{1,0:T(8,128)}, f32[48,1024]{1,0:T(8,128)S(1)}) custom-call(f32[8,3072]{1,0:T(8,128)S(1)} %constant_dynamic-update-slice_fusion.2.refs_0_, bf16[32,1024]{1,0:T(8,128)(2,1)S(1)} %get-tuple-element.10.refs_1_.refs_2_, f32[48,1024]{1,0:T(8,128)S(1)} %get-tuple-element.13.refs_2_), custom_call_target="tpu_custom_call" | custom-call | flops 134217728 | bytes 131072 | tf_op jit(solution)/shard_map/pairs_2/pallas_call | solution.py:343
  15.3 0.4 %collective-permute-done.2.refs_0_ = f32[8,3072]{1,0:T(8,128)S(1)} collective-permute-done((f32[8,3072]{1,0:T(8,128)S(1)}, f32[8,3072]{1,0:T(8,128)S(1)}, u32[]{:S(2)}, u32[]{:S(2)}) %collective-permute-start.2) | collective-permute-done | bytes 98336 | tf_op jit(solution)/shard_map/ppermute | solution.py:289
  15.7 0.0 copy-done
  15.7 0.0 copy-done.2
  15.7 2.2 %pairs_0.3.mine = f32[8,1152]{1,0:T(8,128)S(1)} custom-call(f32[8,3072]{1,0:T(8,128)S(1)} %collective-permute-done.2.refs_0_, f32[3,1024]{1,0:T(4,128)S(1)} %copy-done.1, bf16[32,1024]{1,0:T(8,128)(2,1)S(1)} %get-tuple-element.10.refs_1_.refs_2_, f32[48,1024]{1,0:T(8,128)S(1)} %get-tuple-element.14.refs_3_, f32[8,128]{1,0:T(8,128)S(1)} %get-tuple-element.15.refs_4_, ...), custom_call_target="tpu_custom_call" | custom-call | flops 268435456 | bytes 131072 | tf_op jit(solution)/shard_map/pairs_0/pallas_call | solution.py:343
  17.9 1.0 %collective-permute-start.3 = (f32[8,1152]{1,0:T(8,128)S(1)}, f32[8,1152]{1,0:T(8,128)S(1)}, u32[]{:S(2)}, u32[]{:S(2)}) collective-permute-start(f32[8,1152]{1,0:T(8,128)S(1)} %pairs_0.3.mine), channel_id=1, source_target_pairs={{1,0},{0,1},{3,2},{2,3},{5,4},{4,5},{7,6},{6,7},{9,8},{8,9},{11,10... | collective-permute-start | bytes 110600 | tf_op jit(solution)/shard_map/ppermute | solution.py:289
  18.9 0.9 %collective-permute-done.3.other = f32[8,1152]{1,0:T(8,128)S(1)} collective-permute-done((f32[8,1152]{1,0:T(8,128)S(1)}, f32[8,1152]{1,0:T(8,128)S(1)}, u32[]{:S(2)}, u32[]{:S(2)}) %collective-permute-start.3) | collective-permute-done | bytes 36896 | tf_op jit(solution)/shard_map/ppermute | solution.py:289
  19.8 3.1 %collective-permute-start.4 = (f32[8,128]{1,0:T(8,128)S(1)}, f32[8,128]{1,0:T(8,128)S(1)}, u32[]{:S(2)}, u32[]{:S(2)}) collective-permute-start(f32[8,128]{1,0:T(8,128)S(1)} %slice_add_fusion), channel_id=1, source_target_pairs={{9,0},{8,1},{11,2},{10,3},{13,4},{12,5},{15,6},{14,7},{1,8},{0,9},... | collective-permute-start | bytes 12296 | tf_op jit(solution)/shard_map/ppermute | solution.py:289
  22.9 1.3 %collective-permute-done.4 = f32[8,128]{1,0:T(8,128)S(1)} collective-permute-done((f32[8,128]{1,0:T(8,128)S(1)}, f32[8,128]{1,0:T(8,128)S(1)}, u32[]{:S(2)}, u32[]{:S(2)}) %collective-permute-start.4) | collective-permute-done | bytes 4128 | tf_op jit(solution)/shard_map/ppermute | solution.py:289
  24.2 1.9 %collective-permute-start.5 = (f32[8,128]{1,0:T(8,128)S(1)}, f32[8,128]{1,0:T(8,128)S(1)}, u32[]{:S(2)}, u32[]{:S(2)}) collective-permute-start(f32[8,128]{1,0:T(8,128)S(1)} %add.13), channel_id=1, source_target_pairs={{5,0},{4,1},{7,2},{6,3},{1,4},{0,5},{3,6},{2,7},{13,8},{12,9},{15,... | collective-permute-start | bytes 12296 | tf_op jit(solution)/shard_map/ppermute | solution.py:289
  26.1 1.3 %collective-permute-done.5 = f32[8,128]{1,0:T(8,128)S(1)} collective-permute-done((f32[8,128]{1,0:T(8,128)S(1)}, f32[8,128]{1,0:T(8,128)S(1)}, u32[]{:S(2)}, u32[]{:S(2)}) %collective-permute-start.5) | collective-permute-done | bytes 4128 | tf_op jit(solution)/shard_map/ppermute | solution.py:289
  27.4 2.2 %collective-permute-start.6 = (f32[8,128]{1,0:T(8,128)S(1)}, f32[8,128]{1,0:T(8,128)S(1)}, u32[]{:S(2)}, u32[]{:S(2)}) collective-permute-start(f32[8,128]{1,0:T(8,128)S(1)} %add.14), channel_id=1, source_target_pairs={{3,0},{2,1},{1,2},{0,3},{7,4},{6,5},{5,6},{4,7},{11,8},{10,9},{9,1... | collective-permute-start | bytes 12296 | tf_op jit(solution)/shard_map/ppermute | solution.py:289
  29.7 1.3 %collective-permute-done.6 = f32[8,128]{1,0:T(8,128)S(1)} collective-permute-done((f32[8,128]{1,0:T(8,128)S(1)}, f32[8,128]{1,0:T(8,128)S(1)}, u32[]{:S(2)}, u32[]{:S(2)}) %collective-permute-start.6) | collective-permute-done | bytes 4128 | tf_op jit(solution)/shard_map/ppermute | solution.py:289
  31.0 1.7 %tail.1 = (f32[8,1024]{1,0:T(8,128)}, f32[8,1024]{1,0:T(8,128)}) custom-call(f32[8,128]{1,0:T(8,128)S(1)} %add.15.small, f32[8,1152]{1,0:T(8,128)S(1)} %pairs_0.3.mine, f32[8,1152]{1,0:T(8,128)S(1)} %collective-permute-done.3.other, f32[8,1024]{1,0:T(8,128)S(1)} %copy-done, s32[1]{0:T(128)S(6)} %copy.8.count_hbm.refs_7_), custom_call_target="tpu_custom_call" | custom-call | bytes 131072 | tf_op jit(solution)/shard_map/tail/pallas_call | solution.py:367
  (10 shorter events, 0.0 us)
Async XLA Ops:
  1.3 4.4 %copy-start.1 = (f32[3,1024]{1,0:T(4,128)S(1)}, f32[3,1024]{1,0:T(4,128)}, u32[]{:S(2)}) copy-start(f32[3,1024]{1,0:T(4,128)} %refs_1_.3) | copy-start | bytes 36868
  2.1 5.1 %collective-permute-start = (f32[8,768]{1,0:T(8,128)S(1)}, f32[8,768]{1,0:T(8,128)S(1)}, u32[]{:S(2)}, u32[]{:S(2)}) collective-permute-start(f32[8,768]{1,0:T(8,128)S(1)} %pack.1.refs_0_), channel_id=1, source_target_pairs={{9,0},{8,1},{11,2},{10,3},{13,4},{12,5},{15,6},{14,7},{1,8},{0,9},... | collective-permute-start | bytes 73736 | tf_op jit(solution)/shard_map/ppermute | solution.py:289
  7.3 3.7 %collective-permute-start.1 = (f32[8,1536]{1,0:T(8,128)S(1)}, f32[8,1536]{1,0:T(8,128)S(1)}, u32[]{:S(2)}, u32[]{:S(2)}) collective-permute-start(f32[8,1536]{1,0:T(8,128)S(1)} %constant_dynamic-update-slice_fusion.refs_0_), channel_id=1, source_target_pairs={{5,0},{4,1},{7,2},{6,3},{1,4},{0,5},{3,6},{2,7},{13,8},{12,9},{15,... | collective-permute-start | bytes 147464 | tf_op jit(solution)/shard_map/ppermute | solution.py:289
  11.0 4.7 %collective-permute-start.2 = (f32[8,3072]{1,0:T(8,128)S(1)}, f32[8,3072]{1,0:T(8,128)S(1)}, u32[]{:S(2)}, u32[]{:S(2)}) collective-permute-start(f32[8,3072]{1,0:T(8,128)S(1)} %constant_dynamic-update-slice_fusion.2.refs_0_), channel_id=1, source_target_pairs={{3,0},{2,1},{1,2},{0,3},{7,4},{6,5},{5,6},{4,7},{11,8},{10,9},{9,1... | collective-permute-start | bytes 294920 | tf_op jit(solution)/shard_map/ppermute | solution.py:289
  12.8 2.9 %copy-start = (f32[8,1024]{1,0:T(8,128)S(1)}, f32[8,1024]{1,0:T(8,128)}, u32[]{:S(2)}) copy-start(f32[8,1024]{1,0:T(8,128)} %rhs_hbm.3) | copy-start | bytes 98308
  12.8 2.9 %copy-start.2 = (f32[1024]{0:T(1024)S(1)}, f32[1024]{0:T(1024)}, u32[]{:S(2)}) copy-start(f32[1024]{0:T(1024)} %refs_5_.1) | copy-start | bytes 12292
  17.9 1.9 %collective-permute-start.3 = (f32[8,1152]{1,0:T(8,128)S(1)}, f32[8,1152]{1,0:T(8,128)S(1)}, u32[]{:S(2)}, u32[]{:S(2)}) collective-permute-start(f32[8,1152]{1,0:T(8,128)S(1)} %pairs_0.3.mine), channel_id=1, source_target_pairs={{1,0},{0,1},{3,2},{2,3},{5,4},{4,5},{7,6},{6,7},{9,8},{8,9},{11,10... | collective-permute-start | bytes 110600 | tf_op jit(solution)/shard_map/ppermute | solution.py:289
  19.8 4.5 %collective-permute-start.4 = (f32[8,128]{1,0:T(8,128)S(1)}, f32[8,128]{1,0:T(8,128)S(1)}, u32[]{:S(2)}, u32[]{:S(2)}) collective-permute-start(f32[8,128]{1,0:T(8,128)S(1)} %slice_add_fusion), channel_id=1, source_target_pairs={{9,0},{8,1},{11,2},{10,3},{13,4},{12,5},{15,6},{14,7},{1,8},{0,9},... | collective-permute-start | bytes 12296 | tf_op jit(solution)/shard_map/ppermute | solution.py:289
  24.2 3.2 %collective-permute-start.5 = (f32[8,128]{1,0:T(8,128)S(1)}, f32[8,128]{1,0:T(8,128)S(1)}, u32[]{:S(2)}, u32[]{:S(2)}) collective-permute-start(f32[8,128]{1,0:T(8,128)S(1)} %add.13), channel_id=1, source_target_pairs={{5,0},{4,1},{7,2},{6,3},{1,4},{0,5},{3,6},{2,7},{13,8},{12,9},{15,... | collective-permute-start | bytes 12296 | tf_op jit(solution)/shard_map/ppermute | solution.py:289
  27.4 3.6 %collective-permute-start.6 = (f32[8,128]{1,0:T(8,128)S(1)}, f32[8,128]{1,0:T(8,128)S(1)}, u32[]{:S(2)}, u32[]{:S(2)}) collective-permute-start(f32[8,128]{1,0:T(8,128)S(1)} %add.14), channel_id=1, source_target_pairs={{3,0},{2,1},{1,2},{0,3},{7,4},{6,5},{5,6},{4,7},{11,8},{10,9},{9,1... | collective-permute-start | bytes 12296 | tf_op jit(solution)/shard_map/ppermute | solution.py:289

commit v5 on v4

--- a/solution.py
+++ b/solution.py
@@ -111,9 +111,10 @@
         out[row : row + 4, at : at + LANES] = jnp.concatenate([place, held], axis=0)
 
 
-def pair_kernel(first, last, start, blocks, tiles, *refs):
+def pair_kernel(first, last, keep, taken, tiles, *refs):
     refs = list(refs)
-    packet = refs.pop(0)
+    packets = [refs.pop(0) for _ in taken]
+    packet = packets[0]
     if first or last:
         pos_hbm = refs.pop(0)
     if not first:
@@ -123,7 +124,8 @@
         noise_hbm, rhs_hbm, count_hbm, out = (refs.pop(0) for _ in range(4))
         acc = refs.pop(0)
     else:
-        known_out, acc = refs.pop(0), refs.pop(0)
+        known_out = refs.pop(0) if keep else None
+        acc = refs.pop(0)
         rows_ref = refs.pop(0) if first else rows_in
         if first:
             norm = refs.pop(0)
@@ -143,14 +145,15 @@
         ]
     for copy in copies:
         copy.start()
-    if not last:
+    if keep:
         known_out[...] = packet[...]
 
     width = packet.shape[0]
     half = tiles * LANES
     stride = half + half // 2
     filled = jnp.int32(0)
-    for b in range(start, start + blocks):
+    listed = [(ref, b) for ref, (i, j) in zip(packets, taken) for b in range(i, j)]
+    for packet, b in listed:
         base = b * stride
         for t in range(tiles):
             if t % 2 == 0:
@@ -178,7 +181,7 @@
     if first:
         copies[0].wait()
         rows_ref[...] = row_side(pos[...])
-        norm[...] = gram(packet[:, :half], packet[:, :half], width)
+        norm[...] = gram(packets[0][:, :half], packets[0][:, :half], width)
         acc[...] = jnp.zeros(acc.shape, f32)
     else:
         acc[...] = acc_in[...]
@@ -201,7 +204,7 @@
             part = acc[:, near] + jnp.dot(w, top, preferred_element_type=f32)
             acc[:, near] = part + jnp.dot(w, low, preferred_element_type=f32)
 
-    full = min(STEP, blocks * half)
+    full = min(STEP, len(listed) * half)
     steps = (filled + UNIT - LANES) // full
     rest = filled - steps * full
 
@@ -312,15 +315,16 @@
     acc_shape = shape((6 * width, slots), f32)
     rows_shape = shape((32, slots), bf16)
 
-    def pairs(known, start, count, last, rows=None, acc=None, norm=None):
-        first = rows is None
-        args, specs = [known], [VMEM]
+    def pairs(parts, taken, rows=None, acc=None, norm=None, keep=False):
+        first, last = rows is None, norm is not None
+        args, specs = list(parts), [VMEM] * len(parts)
         if first or last:
             args.append(position)
             specs.append(HBM)
         if not first:
             args += [rows, acc]
             specs += [VMEM] * 2
+        count = sum(stop - start for start, stop in taken)
         scratch = [
             pltpu.VMEM((32, count * half + UNIT), bf16),
             pltpu.VMEM((6 * width, count * half + UNIT), bf16),
@@ -334,28 +338,34 @@
             scratch = [pltpu.VMEM(acc_shape.shape, f32)] + scratch
             scratch += [noise_buf, rhs_buf, count_buf]
         else:
-            outs = (shape(known.shape, f32), acc_shape)
+            outs = (shape(parts[0].shape, f32),) if keep else ()
+            outs += (acc_shape,)
             if first:
                 outs += (rows_shape, shape((width, LANES), f32))
-        kernel = functools.partial(pair_kernel, first, last, start, count, tiles)
+        kernel = functools.partial(pair_kernel, first, last, keep, taken, tiles)
         flops = 2 * slots * count * half * 64
-        specs_out = (VMEM,) * len(outs)
-        return call(kernel, outs, specs, specs_out, scratch, f"pairs_{start}", flops)(*args)
-
-    known, start, count = packet, 0, 1
-    rows = acc = None
-    distance = blocks // 2
-    while distance:
+        name = f"pairs_{count}"
+        return call(kernel, outs, specs, (VMEM,) * len(outs), scratch, name, flops)(*args)
+
+    distances = [blocks >> k for k in range(1, blocks.bit_length())]
+    known, size = packet, 1
+    rows = None
+    for distance in distances[:-2]:
         arrived = exchanged(known, distance)
+        fresh = (size // 2, size)
         if rows is None:
-            known, acc, rows, norm = pairs(known, start, count, False)
+            known, acc, rows, norm = pairs([known], [fresh], keep=True)
         else:
-            known, acc = pairs(known, start, count, False, rows, acc)
-        start += count
-        count = start
+            known, acc = pairs([known], [fresh], rows, acc, keep=True)
         known = jnp.concatenate([known, arrived], axis=1)
-        distance //= 2
-    (mine,) = pairs(arrived, 0, count, True, rows, acc, norm)
+        size *= 2
+    near = exchanged(known, distances[-2])
+    far = exchanged(known, distances[-1])
+    (acc,) = pairs([known], [(size // 2, size)], rows, acc)
+    near, acc = lax.optimization_barrier((near, acc))
+    rest = exchanged(near, distances[-1])
+    (acc,) = pairs([near, far], [(0, size)] * 2, rows, acc)
+    (mine,) = pairs([rest], [(0, size)], rows, acc, norm)
     other = exchanged(mine, 0)
     small = mine[:, slots:] + other[:, slots:]
     distance = blocks // 2

time: 32.9 us -> 31.1 us (0.945)
  starting transfers between devices: 15.5 us -> 14.3 us
  waiting for transfers between devices: 6.56 us -> 5.76 us
  Pallas kernels: 9.22 us -> 9.6 us
    ppermute x7 -> x8, starting transfers between devices: 15.5 us -> 14.3 us  [exchanged(): return lax.ppermute(block, ('blk', 'offs'), route)]
    ppermute x7 -> x8, waiting for transfers between devices: 6.56 us -> 5.76 us  [exchanged(): return lax.ppermute(block, ('blk', 'offs'), route)]
    pallas_call x4, Pallas kernels: 6.73 us -> 7.09 us  [pairs(): call(kernel, outs, specs, (VMEM,) * len(outs), scratch, name, flops)(*args)]
  transfers between devices with their start and end apart: 7 -> 8, of which waited for: 7 -> 5; matrix products, arithmetic and copies ran while one was open for 0% -> 0% of each run, Pallas kernels for 14% -> 17%
where the time goes in v5:
time: 31.1 us
  starting transfers between devices  14.3 us (46%)
  Pallas kernels  9.6 us (31%)
  waiting for transfers between devices  5.76 us (19%)
  between operations  1.39 us (4%)
    ppermute x8, starting transfers between devices, exchanged(): return lax.ppermute(block, ('blk', 'offs'), route)  14.3 us
    pallas_call x4, Pallas kernels, pairs(): call(kernel, outs, specs, (VMEM,) * len(outs), scratch, name, flops)(*args)  7.09 us
    ppermute x8, waiting for transfers between devices, exchanged(): return lax.ppermute(block, ('blk', 'offs'), route)  5.76 us
    pallas_call x1, Pallas kernels, body(): call(tail_kernel, (shape(rhs.shape, f32),) * 2, [VMEM, VMEM, VMEM, HBM, H...  1.66 us
    pallas_call x1, Pallas kernels, body(): call(pack_kernel, shape((width, half + half // 2), f32), [HBM, HBM, HBM],...  0.85 us
  transfers between devices with their start and end apart: 8, of which 5 were waited for; matrix products, arithmetic and copies ran while one was open for 0% of the time, Pallas kernels for 17%

profile of v5, /device:TPU:0, one launch (start us, length us, event | category | flops | bytes accessed | tf_op | source)
XLA Modules:
  0.0 31.1 jit_solution(6401671454858094857)
XLA Ops:
  1.3 0.8 %pack.1.refs_0_ = f32[8,768]{1,0:T(8,128)S(1)} custom-call(f32[3,1024]{1,0:T(4,128)} %refs_1_.3, f32[8,1024]{1,0:T(8,128)} %rhs_hbm.3, s32[1]{0:T(128)S(6)} %copy.7.count_hbm.refs_7_), custom_call_target="tpu_custom_call" | custom-call | bytes 131072 | tf_op jit(solution)/shard_map/pack/pallas_call | solution.py:306
  2.1 3.5 %collective-permute-start = (f32[8,768]{1,0:T(8,128)S(1)}, f32[8,768]{1,0:T(8,128)S(1)}, u32[]{:S(2)}, u32[]{:S(2)}) collective-permute-start(f32[8,768]{1,0:T(8,128)S(1)} %pack.1.refs_0_), channel_id=1, source_target_pairs={{9,0},{8,1},{11,2},{10,3},{13,4},{12,5},{15,6},{14,7},{1,8},{0,9},... | collective-permute-start | bytes 73736 | tf_op jit(solution)/shard_map/ppermute | solution.py:292
  5.7 1.3 %pairs_1.2 = (f32[8,768]{1,0:T(8,128)S(1)}, f32[48,1024]{1,0:T(8,128)S(1)}, bf16[32,1024]{1,0:T(8,128)(2,1)S(1)}, f32[8,128]{1,0:T(8,128)S(1)}) custom-call(f32[8,768]{1,0:T(8,128)S(1)} %pack.1.refs_0_, f32[3,1024]{1,0:T(4,128)S(1)} %copy-done.1), custom_call_target="tpu_custom_call" | custom-call | flops 67108864 | bytes 131072 | tf_op jit(solution)/shard_map/pairs_1/pallas_call | solution.py:348
  7.0 0.3 collective-permute-done
  7.3 1.8 %collective-permute-start.1 = (f32[8,1536]{1,0:T(8,128)S(1)}, f32[8,1536]{1,0:T(8,128)S(1)}, u32[]{:S(2)}, u32[]{:S(2)}) collective-permute-start(f32[8,1536]{1,0:T(8,128)S(1)} %constant_dynamic-update-slice_fusion.refs_0_), channel_id=1, source_target_pairs={{5,0},{4,1},{7,2},{6,3},{1,4},{0,5},{3,6},{2,7},{13,8},{12,9},{15,... | collective-permute-start | bytes 147464 | tf_op jit(solution)/shard_map/ppermute | solution.py:292
  9.1 1.6 %collective-permute-start.3 = (f32[8,1536]{1,0:T(8,128)S(1)}, f32[8,1536]{1,0:T(8,128)S(1)}, u32[]{:S(2)}, u32[]{:S(2)}) collective-permute-start(f32[8,1536]{1,0:T(8,128)S(1)} %constant_dynamic-update-slice_fusion.refs_0_), channel_id=1, source_target_pairs={{3,0},{2,1},{1,2},{0,3},{7,4},{6,5},{5,6},{4,7},{11,8},{10,9},{9,1... | collective-permute-start | bytes 147464 | tf_op jit(solution)/shard_map/ppermute | solution.py:292
  10.7 1.1 %pairs_1.3.refs_3_ = f32[48,1024]{1,0:T(8,128)S(1)} custom-call(f32[8,1536]{1,0:T(8,128)S(1)} %constant_dynamic-update-slice_fusion.refs_0_, bf16[32,1024]{1,0:T(8,128)(2,1)S(1)} %get-tuple-element.9.refs_1_.refs_2_, f32[48,1024]{1,0:T(8,128)S(1)} %get-tuple-element.10.refs_2_), custom_call_target="tpu_custom_call" | custom-call | flops 67108864 | bytes 131072 | tf_op jit(solution)/shard_map/pairs_1/pallas_call | solution.py:348
  11.8 0.0 copy-start
  11.8 0.0 copy-start.2
  11.8 0.0 collective-permute-done.1.refs_0_
  11.8 1.0 %collective-permute-start.2 = (f32[8,1536]{1,0:T(8,128)S(1)}, f32[8,1536]{1,0:T(8,128)S(1)}, u32[]{:S(2)}, u32[]{:S(2)}) collective-permute-start(f32[8,1536]{1,0:T(8,128)S(1)} %collective-permute-done.1.refs_0_), channel_id=1, source_target_pairs={{3,0},{2,1},{1,2},{0,3},{7,4},{6,5},{5,6},{4,7},{11,8},{10,9},{9,1... | collective-permute-start | bytes 147464 | tf_op jit(solution)/shard_map/ppermute | solution.py:292
  12.8 0.0 collective-permute-done.3.refs_1_
  12.8 2.9 %pairs_4.1.refs_3_ = f32[48,1024]{1,0:T(8,128)S(1)} custom-call(f32[8,1536]{1,0:T(8,128)S(1)} %collective-permute-done.1.refs_0_, f32[8,1536]{1,0:T(8,128)S(1)} %collective-permute-done.3.refs_1_, bf16[32,1024]{1,0:T(8,128)(2,1)S(1)} %get-tuple-element.9.refs_1_.refs_2_, f32[48,1024]{1,0:T(8,128)S(1)} %pairs_1.3.refs_3_), custom_call_target="tpu_custom_call" | custom-call | flops 268435456 | bytes 131072 | tf_op jit(solution)/shard_map/pairs_4/pallas_call | solution.py:348
  15.7 0.0 collective-permute-done.2.refs_0_
  15.8 1.8 %pairs_2.1.mine = f32[8,1152]{1,0:T(8,128)S(1)} custom-call(f32[8,1536]{1,0:T(8,128)S(1)} %collective-permute-done.2.refs_0_, f32[3,1024]{1,0:T(4,128)S(1)} %copy-done.1, bf16[32,1024]{1,0:T(8,128)(2,1)S(1)} %get-tuple-element.9.refs_1_.refs_2_, f32[48,1024]{1,0:T(8,128)S(1)} %pairs_4.1.refs_3_, f32[8,128]{1,0:T(8,128)S(1)} %get-tuple-element.13.refs_4_, ...), custom_call_target="tpu_custom_call" | custom-call | flops 134217728 | bytes 131072 | tf_op jit(solution)/shard_map/pairs_2/pallas_call | solution.py:348
  17.6 0.1 collective-permute-start.4
  17.7 1.2 %collective-permute-done.4.other = f32[8,1152]{1,0:T(8,128)S(1)} collective-permute-done((f32[8,1152]{1,0:T(8,128)S(1)}, f32[8,1152]{1,0:T(8,128)S(1)}, u32[]{:S(2)}, u32[]{:S(2)}) %collective-permute-start.4) | collective-permute-done | bytes 36896 | tf_op jit(solution)/shard_map/ppermute | solution.py:292
  18.8 3.1 %collective-permute-start.5 = (f32[8,128]{1,0:T(8,128)S(1)}, f32[8,128]{1,0:T(8,128)S(1)}, u32[]{:S(2)}, u32[]{:S(2)}) collective-permute-start(f32[8,128]{1,0:T(8,128)S(1)} %slice_add_fusion), channel_id=1, source_target_pairs={{9,0},{8,1},{11,2},{10,3},{13,4},{12,5},{15,6},{14,7},{1,8},{0,9},... | collective-permute-start | bytes 12296 | tf_op jit(solution)/shard_map/ppermute | solution.py:292
  21.9 1.3 %collective-permute-done.5 = f32[8,128]{1,0:T(8,128)S(1)} collective-permute-done((f32[8,128]{1,0:T(8,128)S(1)}, f32[8,128]{1,0:T(8,128)S(1)}, u32[]{:S(2)}, u32[]{:S(2)}) %collective-permute-start.5) | collective-permute-done | bytes 4128 | tf_op jit(solution)/shard_map/ppermute | solution.py:292
  23.3 1.8 %collective-permute-start.6 = (f32[8,128]{1,0:T(8,128)S(1)}, f32[8,128]{1,0:T(8,128)S(1)}, u32[]{:S(2)}, u32[]{:S(2)}) collective-permute-start(f32[8,128]{1,0:T(8,128)S(1)} %add.13), channel_id=1, source_target_pairs={{5,0},{4,1},{7,2},{6,3},{1,4},{0,5},{3,6},{2,7},{13,8},{12,9},{15,... | collective-permute-start | bytes 12296 | tf_op jit(solution)/shard_map/ppermute | solution.py:292
  25.1 1.3 %collective-permute-done.6 = f32[8,128]{1,0:T(8,128)S(1)} collective-permute-done((f32[8,128]{1,0:T(8,128)S(1)}, f32[8,128]{1,0:T(8,128)S(1)}, u32[]{:S(2)}, u32[]{:S(2)}) %collective-permute-start.6) | collective-permute-done | bytes 4128 | tf_op jit(solution)/shard_map/ppermute | solution.py:292
  26.4 1.4 %collective-permute-start.7 = (f32[8,128]{1,0:T(8,128)S(1)}, f32[8,128]{1,0:T(8,128)S(1)}, u32[]{:S(2)}, u32[]{:S(2)}) collective-permute-start(f32[8,128]{1,0:T(8,128)S(1)} %add.14), channel_id=1, source_target_pairs={{3,0},{2,1},{1,2},{0,3},{7,4},{6,5},{5,6},{4,7},{11,8},{10,9},{9,1... | collective-permute-start | bytes 12296 | tf_op jit(solution)/shard_map/ppermute | solution.py:292
  27.8 1.6 %collective-permute-done.7 = f32[8,128]{1,0:T(8,128)S(1)} collective-permute-done((f32[8,128]{1,0:T(8,128)S(1)}, f32[8,128]{1,0:T(8,128)S(1)}, u32[]{:S(2)}, u32[]{:S(2)}) %collective-permute-start.7) | collective-permute-done | bytes 4128 | tf_op jit(solution)/shard_map/ppermute | solution.py:292
  29.5 1.7 %tail.1 = (f32[8,1024]{1,0:T(8,128)}, f32[8,1024]{1,0:T(8,128)}) custom-call(f32[8,128]{1,0:T(8,128)S(1)} %add.15.small, f32[8,1152]{1,0:T(8,128)S(1)} %pairs_2.1.mine, f32[8,1152]{1,0:T(8,128)S(1)} %collective-permute-done.4.other, f32[8,1024]{1,0:T(8,128)S(1)} %copy-done, s32[1]{0:T(128)S(6)} %copy.7.count_hbm.refs_7_), custom_call_target="tpu_custom_call" | custom-call | bytes 131072 | tf_op jit(solution)/shard_map/tail/pallas_call | solution.py:377
  (10 shorter events, 0.0 us)
Async XLA Ops:
  1.3 4.4 %copy-start.1 = (f32[3,1024]{1,0:T(4,128)S(1)}, f32[3,1024]{1,0:T(4,128)}, u32[]{:S(2)}) copy-start(f32[3,1024]{1,0:T(4,128)} %refs_1_.3) | copy-start | bytes 36868
  2.1 5.1 %collective-permute-start = (f32[8,768]{1,0:T(8,128)S(1)}, f32[8,768]{1,0:T(8,128)S(1)}, u32[]{:S(2)}, u32[]{:S(2)}) collective-permute-start(f32[8,768]{1,0:T(8,128)S(1)} %pack.1.refs_0_), channel_id=1, source_target_pairs={{9,0},{8,1},{11,2},{10,3},{13,4},{12,5},{15,6},{14,7},{1,8},{0,9},... | collective-permute-start | bytes 73736 | tf_op jit(solution)/shard_map/ppermute | solution.py:292
  7.3 4.5 %collective-permute-start.1 = (f32[8,1536]{1,0:T(8,128)S(1)}, f32[8,1536]{1,0:T(8,128)S(1)}, u32[]{:S(2)}, u32[]{:S(2)}) collective-permute-start(f32[8,1536]{1,0:T(8,128)S(1)} %constant_dynamic-update-slice_fusion.refs_0_), channel_id=1, source_target_pairs={{5,0},{4,1},{7,2},{6,3},{1,4},{0,5},{3,6},{2,7},{13,8},{12,9},{15,... | collective-permute-start | bytes 147464 | tf_op jit(solution)/shard_map/ppermute | solution.py:292
  9.1 3.7 %collective-permute-start.3 = (f32[8,1536]{1,0:T(8,128)S(1)}, f32[8,1536]{1,0:T(8,128)S(1)}, u32[]{:S(2)}, u32[]{:S(2)}) collective-permute-start(f32[8,1536]{1,0:T(8,128)S(1)} %constant_dynamic-update-slice_fusion.refs_0_), channel_id=1, source_target_pairs={{3,0},{2,1},{1,2},{0,3},{7,4},{6,5},{5,6},{4,7},{11,8},{10,9},{9,1... | collective-permute-start | bytes 147464 | tf_op jit(solution)/shard_map/ppermute | solution.py:292
  11.8 4.0 %copy-start = (f32[8,1024]{1,0:T(8,128)S(1)}, f32[8,1024]{1,0:T(8,128)}, u32[]{:S(2)}) copy-start(f32[8,1024]{1,0:T(8,128)} %rhs_hbm.3) | copy-start | bytes 98308
  11.8 4.0 %copy-start.2 = (f32[1024]{0:T(1024)S(1)}, f32[1024]{0:T(1024)}, u32[]{:S(2)}) copy-start(f32[1024]{0:T(1024)} %refs_5_.1) | copy-start | bytes 12292
  11.8 3.9 %collective-permute-start.2 = (f32[8,1536]{1,0:T(8,128)S(1)}, f32[8,1536]{1,0:T(8,128)S(1)}, u32[]{:S(2)}, u32[]{:S(2)}) collective-permute-start(f32[8,1536]{1,0:T(8,128)S(1)} %collective-permute-done.1.refs_0_), channel_id=1, source_target_pairs={{3,0},{2,1},{1,2},{0,3},{7,4},{6,5},{5,6},{4,7},{11,8},{10,9},{9,1... | collective-permute-start | bytes 147464 | tf_op jit(solution)/shard_map/ppermute | solution.py:292
  17.6 1.3 %collective-permute-start.4 = (f32[8,1152]{1,0:T(8,128)S(1)}, f32[8,1152]{1,0:T(8,128)S(1)}, u32[]{:S(2)}, u32[]{:S(2)}) collective-permute-start(f32[8,1152]{1,0:T(8,128)S(1)} %pairs_2.1.mine), channel_id=1, source_target_pairs={{1,0},{0,1},{3,2},{2,3},{5,4},{4,5},{7,6},{6,7},{9,8},{8,9},{11,10... | collective-permute-start | bytes 110600 | tf_op jit(solution)/shard_map/ppermute | solution.py:292
  18.8 4.4 %collective-permute-start.5 = (f32[8,128]{1,0:T(8,128)S(1)}, f32[8,128]{1,0:T(8,128)S(1)}, u32[]{:S(2)}, u32[]{:S(2)}) collective-permute-start(f32[8,128]{1,0:T(8,128)S(1)} %slice_add_fusion), channel_id=1, source_target_pairs={{9,0},{8,1},{11,2},{10,3},{13,4},{12,5},{15,6},{14,7},{1,8},{0,9},... | collective-permute-start | bytes 12296 | tf_op jit(solution)/shard_map/ppermute | solution.py:292
  23.3 3.1 %collective-permute-start.6 = (f32[8,128]{1,0:T(8,128)S(1)}, f32[8,128]{1,0:T(8,128)S(1)}, u32[]{:S(2)}, u32[]{:S(2)}) collective-permute-start(f32[8,128]{1,0:T(8,128)S(1)} %add.13), channel_id=1, source_target_pairs={{5,0},{4,1},{7,2},{6,3},{1,4},{0,5},{3,6},{2,7},{13,8},{12,9},{15,... | collective-permute-start | bytes 12296 | tf_op jit(solution)/shard_map/ppermute | solution.py:292
  26.4 3.0 %collective-permute-start.7 = (f32[8,128]{1,0:T(8,128)S(1)}, f32[8,128]{1,0:T(8,128)S(1)}, u32[]{:S(2)}, u32[]{:S(2)}) collective-permute-start(f32[8,128]{1,0:T(8,128)S(1)} %add.14), channel_id=1, source_target_pairs={{3,0},{2,1},{1,2},{0,3},{7,4},{6,5},{5,6},{4,7},{11,8},{10,9},{9,1... | collective-permute-start | bytes 12296 | tf_op jit(solution)/shard_map/ppermute | solution.py:292

commit v6 on v5

--- a/solution.py
+++ b/solution.py
@@ -25,7 +25,6 @@
 VMEM = pl.BlockSpec(memory_space=pltpu.VMEM)
 HBM = pl.BlockSpec(memory_space=pltpu.HBM)
 LIMIT = 24 * 2**20
-highest = lax.Precision.HIGHEST
 
 
 def split3(x):
@@ -121,7 +120,8 @@
         rows_in, acc_in = refs.pop(0), refs.pop(0)
     if last:
         norm = refs.pop(0)
-        noise_hbm, rhs_hbm, count_hbm, out = (refs.pop(0) for _ in range(4))
+        noise_hbm, rhs_hbm, count_hbm = (refs.pop(0) for _ in range(3))
+        out, direction_out = refs.pop(0), refs.pop(0)
         acc = refs.pop(0)
     else:
         known_out = refs.pop(0) if keep else None
@@ -231,6 +231,7 @@
         pulled = acc[at : at + width] + acc[at + width : at + 2 * width]
         image += unit[k : k + 1] * pulled
     direction = rhs[...] * live
+    direction_out[...] = direction
     mine = (lax.axis_index("offs") == 0).astype(f32)
     noise_row = noise[...].reshape(1, slots)
     image = image + (mine * noise_row * live) * direction
@@ -238,33 +239,40 @@
     out[:, slots:] = norm[...] + gram(direction, image, 0)
 
 
-def tail_kernel(small, mine, other, rhs_hbm, count_hbm, sol, res, rhs, count, sems):
-    copies = [
-        pltpu.make_async_copy(rhs_hbm, rhs, sems.at[0]),
-        pltpu.make_async_copy(count_hbm, count, sems.at[1]),
+def solved(small):
+    width = small.shape[0]
+    shape = small.shape
+    c = [jnp.broadcast_to(small[:, j : j + 1], shape) for j in range(width)]
+    r = [
+        jnp.broadcast_to(small[:, j : j + 1], shape) for j in range(width, 2 * width)
     ]
-    for copy in copies:
-        copy.start()
-    a = small[...]
-    width = a.shape[0]
-    row = lax.broadcasted_iota(jnp.int32, a.shape, 0)
     for k in range(width):
-        pivot = a[k : k + 1] / a[k : k + 1, k : k + 1]
-        a = jnp.where(row == k, pivot, a - a[:, k : k + 1] * pivot)
-    alpha = a[:, width : 2 * width]
-    for copy in copies:
-        copy.wait()
-    slots = rhs.shape[1]
-    lane = lax.broadcasted_iota(jnp.int32, (1, slots), 1)
-    direction = rhs[...] * (lane < count[0]).astype(f32)
+        inverse = pl.reciprocal(c[k], approx=True)[k : k + 1]
+        ck, rk = c[k], r[k]
+        for j in range(width):
+            if j != k:
+                factor = c[j][k : k + 1] * inverse
+                c[j] = c[j] - ck * factor
+                r[j] = r[j] - rk * factor
+        c[k], r[k] = ck * inverse, rk * inverse
+    return r
+
+
+def combined(columns, x):
+    parts = []
+    for t in range(0, x.shape[1], LANES):
+        tile = x[:, t : t + LANES]
+        parts.append(sum(col * tile[m : m + 1] for m, col in enumerate(columns)))
+    return jnp.concatenate(parts, axis=1)
+
+
+def tail_kernel(small, mine, other, direction_ref, sol, res):
+    columns = solved(small[...])
+    direction = direction_ref[...]
+    slots = direction.shape[1]
     image = mine[:, :slots] + other[:, :slots]
-    dims = (((0,), (0,)), ((), ()))
-    sol[...] = lax.dot_general(
-        alpha, direction, dims, precision=highest, preferred_element_type=f32
-    )
-    res[...] = direction - lax.dot_general(
-        alpha, image, dims, precision=highest, preferred_element_type=f32
-    )
+    sol[...] = combined(columns, direction)
+    res[...] = direction - combined(columns, image)
 
 
 def call(kernel, out_shape, in_specs, out_specs, scratch, name, flops=0):
@@ -334,7 +342,7 @@
         if last:
             args += [norm, noise_var, rhs, block_count]
             specs += [VMEM] + [HBM] * 3
-            outs = (shape((width, slots + LANES), f32),)
+            outs = (shape((width, slots + LANES), f32), shape((width, slots), f32))
             scratch = [pltpu.VMEM(acc_shape.shape, f32)] + scratch
             scratch += [noise_buf, rhs_buf, count_buf]
         else:
@@ -365,7 +373,7 @@
     near, acc = lax.optimization_barrier((near, acc))
     rest = exchanged(near, distances[-1])
     (acc,) = pairs([near, far], [(0, size)] * 2, rows, acc)
-    (mine,) = pairs([rest], [(0, size)], rows, acc, norm)
+    mine, direction = pairs([rest], [(0, size)], rows, acc, norm)
     other = exchanged(mine, 0)
     small = mine[:, slots:] + other[:, slots:]
     distance = blocks // 2
@@ -377,11 +385,11 @@
         call(
             tail_kernel,
             (shape(rhs.shape, f32),) * 2,
-            [VMEM, VMEM, VMEM, HBM, HBM],
+            [VMEM] * 4,
             (VMEM, VMEM),
-            [rhs_buf, count_buf, pltpu.SemaphoreType.DMA((2,))],
+            [],
             "tail",
-        )(small, mine, other, rhs, block_count)
+        )(small, mine, other, direction)
     )
 
 

time: 31.1 us -> 30.1 us (0.968)
  Pallas kernels: 9.6 us -> 7.73 us
  waiting for transfers between devices: 5.76 us -> 6.74 us
    pallas_call x4, Pallas kernels: 7.09 us -> 6.07 us  [pairs(): call(kernel, outs, specs, (VMEM,) * len(outs), scratch, name, flops)(*args)]
    ppermute x8, waiting for transfers between devices: 5.76 us -> 6.74 us  [exchanged(): return lax.ppermute(block, ('blk', 'offs'), route)]
    pallas_call x1, Pallas kernels: 1.66 us -> 0.81 us  [body(): call(tail_kernel, (shape(rhs.shape, f32),) * 2, [VMEM] * 4, (VMEM, VMEM),...]
  transfers between devices with their start and end apart: 8 -> 8, of which waited for: 5 -> 6; matrix products, arithmetic and copies ran while one was open for 0% -> 0% of each run, Pallas kernels for 17% -> 13%
where the time goes in v6:
time: 30.1 us
  starting transfers between devices  14.2 us (47%)
  Pallas kernels  7.73 us (26%)
  waiting for transfers between devices  6.74 us (22%)
  between operations  1.37 us (5%)
    ppermute x8, starting transfers between devices, exchanged(): return lax.ppermute(block, ('blk', 'offs'), route)  14.2 us
    ppermute x8, waiting for transfers between devices, exchanged(): return lax.ppermute(block, ('blk', 'offs'), route)  6.74 us
    pallas_call x4, Pallas kernels, pairs(): call(kernel, outs, specs, (VMEM,) * len(outs), scratch, name, flops)(*args)  6.07 us
    pallas_call x1, Pallas kernels, body(): call(pack_kernel, shape((width, half + half // 2), f32), [HBM, HBM, HBM],...  0.85 us
    pallas_call x1, Pallas kernels, body(): call(tail_kernel, (shape(rhs.shape, f32),) * 2, [VMEM] * 4, (VMEM, VMEM),...  0.81 us
  transfers between devices with their start and end apart: 8, of which 6 were waited for; matrix products, arithmetic and copies ran while one was open for 0% of the time, Pallas kernels for 13%

profile of v6, /device:TPU:0, one launch (start us, length us, event | category | flops | bytes accessed | tf_op | source)
XLA Modules:
  0.0 30.1 jit_solution(9939725771117938793)
XLA Ops:
  1.3 0.8 %pack.1.refs_0_ = f32[8,768]{1,0:T(8,128)S(1)} custom-call(f32[3,1024]{1,0:T(4,128)} %refs_1_.3, f32[8,1024]{1,0:T(8,128)} %refs_6_.1, s32[1]{0:T(128)S(6)} %copy.7.count_hbm.refs_7_), custom_call_target="tpu_custom_call" | custom-call | bytes 131072 | tf_op jit(solution)/shard_map/pack/pallas_call | solution.py:314
  2.1 3.5 %collective-permute-start = (f32[8,768]{1,0:T(8,128)S(1)}, f32[8,768]{1,0:T(8,128)S(1)}, u32[]{:S(2)}, u32[]{:S(2)}) collective-permute-start(f32[8,768]{1,0:T(8,128)S(1)} %pack.1.refs_0_), channel_id=1, source_target_pairs={{9,0},{8,1},{11,2},{10,3},{13,4},{12,5},{15,6},{14,7},{1,8},{0,9},... | collective-permute-start | bytes 73736 | tf_op jit(solution)/shard_map/ppermute | solution.py:300
  5.7 0.9 %pairs_1.2 = (f32[8,768]{1,0:T(8,128)S(1)}, f32[48,1024]{1,0:T(8,128)S(1)}, bf16[32,1024]{1,0:T(8,128)(2,1)S(1)}, f32[8,128]{1,0:T(8,128)S(1)}) custom-call(f32[8,768]{1,0:T(8,128)S(1)} %pack.1.refs_0_, f32[3,1024]{1,0:T(4,128)S(1)} %copy-done.1), custom_call_target="tpu_custom_call" | custom-call | flops 67108864 | bytes 131072 | tf_op jit(solution)/shard_map/pairs_1/pallas_call | solution.py:356
  6.7 0.6 %collective-permute-done = f32[8,768]{1,0:T(8,128)S(1)} collective-permute-done((f32[8,768]{1,0:T(8,128)S(1)}, f32[8,768]{1,0:T(8,128)S(1)}, u32[]{:S(2)}, u32[]{:S(2)}) %collective-permute-start) | collective-permute-done | bytes 24608 | tf_op jit(solution)/shard_map/ppermute | solution.py:300
  7.3 1.8 %collective-permute-start.1 = (f32[8,1536]{1,0:T(8,128)S(1)}, f32[8,1536]{1,0:T(8,128)S(1)}, u32[]{:S(2)}, u32[]{:S(2)}) collective-permute-start(f32[8,1536]{1,0:T(8,128)S(1)} %constant_dynamic-update-slice_fusion.refs_0_), channel_id=1, source_target_pairs={{5,0},{4,1},{7,2},{6,3},{1,4},{0,5},{3,6},{2,7},{13,8},{12,9},{15,... | collective-permute-start | bytes 147464 | tf_op jit(solution)/shard_map/ppermute | solution.py:300
  9.1 1.6 %collective-permute-start.3 = (f32[8,1536]{1,0:T(8,128)S(1)}, f32[8,1536]{1,0:T(8,128)S(1)}, u32[]{:S(2)}, u32[]{:S(2)}) collective-permute-start(f32[8,1536]{1,0:T(8,128)S(1)} %constant_dynamic-update-slice_fusion.refs_0_), channel_id=1, source_target_pairs={{3,0},{2,1},{1,2},{0,3},{7,4},{6,5},{5,6},{4,7},{11,8},{10,9},{9,1... | collective-permute-start | bytes 147464 | tf_op jit(solution)/shard_map/ppermute | solution.py:300
  10.7 1.1 %pairs_1.3.refs_3_ = f32[48,1024]{1,0:T(8,128)S(1)} custom-call(f32[8,1536]{1,0:T(8,128)S(1)} %constant_dynamic-update-slice_fusion.refs_0_, bf16[32,1024]{1,0:T(8,128)(2,1)S(1)} %get-tuple-element.11.refs_1_.refs_2_, f32[48,1024]{1,0:T(8,128)S(1)} %get-tuple-element.12.refs_2_), custom_call_target="tpu_custom_call" | custom-call | flops 67108864 | bytes 131072 | tf_op jit(solution)/shard_map/pairs_1/pallas_call | solution.py:356
  11.8 0.0 copy-start
  11.8 0.0 copy-start.2
  11.8 0.0 collective-permute-done.1.refs_0_
  11.8 1.0 %collective-permute-start.2 = (f32[8,1536]{1,0:T(8,128)S(1)}, f32[8,1536]{1,0:T(8,128)S(1)}, u32[]{:S(2)}, u32[]{:S(2)}) collective-permute-start(f32[8,1536]{1,0:T(8,128)S(1)} %collective-permute-done.1.refs_0_), channel_id=1, source_target_pairs={{3,0},{2,1},{1,2},{0,3},{7,4},{6,5},{5,6},{4,7},{11,8},{10,9},{9,1... | collective-permute-start | bytes 147464 | tf_op jit(solution)/shard_map/ppermute | solution.py:300
  12.8 0.0 collective-permute-done.3.refs_1_
  12.8 1.9 %pairs_4.1.refs_3_ = f32[48,1024]{1,0:T(8,128)S(1)} custom-call(f32[8,1536]{1,0:T(8,128)S(1)} %collective-permute-done.1.refs_0_, f32[8,1536]{1,0:T(8,128)S(1)} %collective-permute-done.3.refs_1_, bf16[32,1024]{1,0:T(8,128)(2,1)S(1)} %get-tuple-element.11.refs_1_.refs_2_, f32[48,1024]{1,0:T(8,128)S(1)} %pairs_1.3.refs_3_), custom_call_target="tpu_custom_call" | custom-call | flops 268435456 | bytes 131072 | tf_op jit(solution)/shard_map/pairs_4/pallas_call | solution.py:356
  14.7 1.0 %collective-permute-done.2.refs_0_ = f32[8,1536]{1,0:T(8,128)S(1)} collective-permute-done((f32[8,1536]{1,0:T(8,128)S(1)}, f32[8,1536]{1,0:T(8,128)S(1)}, u32[]{:S(2)}, u32[]{:S(2)}) %collective-permute-start.2) | collective-permute-done | bytes 49184 | tf_op jit(solution)/shard_map/ppermute | solution.py:300
  15.7 2.1 %pairs_2.1 = (f32[8,1152]{1,0:T(8,128)S(1)}, f32[8,1024]{1,0:T(8,128)S(1)}) custom-call(f32[8,1536]{1,0:T(8,128)S(1)} %collective-permute-done.2.refs_0_, f32[3,1024]{1,0:T(4,128)S(1)} %copy-done.1, bf16[32,1024]{1,0:T(8,128)(2,1)S(1)} %get-tuple-element.11.refs_1_.refs_2_, f32[48,1024]{1,0:T(8,128)S(1)} %pairs_4.1.refs_3_, ...), custom_call_target="tpu_custom_call" | custom-call | flops 134217728 | bytes 131072 | tf_op jit(solution)/shard_map/pairs_2/pallas_call | solution.py:356
  17.8 0.2 collective-permute-start.4
  18.0 1.1 %collective-permute-done.4.other = f32[8,1152]{1,0:T(8,128)S(1)} collective-permute-done((f32[8,1152]{1,0:T(8,128)S(1)}, f32[8,1152]{1,0:T(8,128)S(1)}, u32[]{:S(2)}, u32[]{:S(2)}) %collective-permute-start.4) | collective-permute-done | bytes 36896 | tf_op jit(solution)/shard_map/ppermute | solution.py:300
  19.1 2.7 %collective-permute-start.5 = (f32[8,128]{1,0:T(8,128)S(1)}, f32[8,128]{1,0:T(8,128)S(1)}, u32[]{:S(2)}, u32[]{:S(2)}) collective-permute-start(f32[8,128]{1,0:T(8,128)S(1)} %slice_add_fusion), channel_id=1, source_target_pairs={{9,0},{8,1},{11,2},{10,3},{13,4},{12,5},{15,6},{14,7},{1,8},{0,9},... | collective-permute-start | bytes 12296 | tf_op jit(solution)/shard_map/ppermute | solution.py:300
  21.8 1.3 %collective-permute-done.5 = f32[8,128]{1,0:T(8,128)S(1)} collective-permute-done((f32[8,128]{1,0:T(8,128)S(1)}, f32[8,128]{1,0:T(8,128)S(1)}, u32[]{:S(2)}, u32[]{:S(2)}) %collective-permute-start.5) | collective-permute-done | bytes 4128 | tf_op jit(solution)/shard_map/ppermute | solution.py:300
  23.1 1.6 %collective-permute-start.6 = (f32[8,128]{1,0:T(8,128)S(1)}, f32[8,128]{1,0:T(8,128)S(1)}, u32[]{:S(2)}, u32[]{:S(2)}) collective-permute-start(f32[8,128]{1,0:T(8,128)S(1)} %add.13), channel_id=1, source_target_pairs={{5,0},{4,1},{7,2},{6,3},{1,4},{0,5},{3,6},{2,7},{13,8},{12,9},{15,... | collective-permute-start | bytes 12296 | tf_op jit(solution)/shard_map/ppermute | solution.py:300
  24.7 1.4 %collective-permute-done.6 = f32[8,128]{1,0:T(8,128)S(1)} collective-permute-done((f32[8,128]{1,0:T(8,128)S(1)}, f32[8,128]{1,0:T(8,128)S(1)}, u32[]{:S(2)}, u32[]{:S(2)}) %collective-permute-start.6) | collective-permute-done | bytes 4128 | tf_op jit(solution)/shard_map/ppermute | solution.py:300
  26.1 1.8 %collective-permute-start.7 = (f32[8,128]{1,0:T(8,128)S(1)}, f32[8,128]{1,0:T(8,128)S(1)}, u32[]{:S(2)}, u32[]{:S(2)}) collective-permute-start(f32[8,128]{1,0:T(8,128)S(1)} %add.14), channel_id=1, source_target_pairs={{3,0},{2,1},{1,2},{0,3},{7,4},{6,5},{5,6},{4,7},{11,8},{10,9},{9,1... | collective-permute-start | bytes 12296 | tf_op jit(solution)/shard_map/ppermute | solution.py:300
  27.9 1.3 %collective-permute-done.7 = f32[8,128]{1,0:T(8,128)S(1)} collective-permute-done((f32[8,128]{1,0:T(8,128)S(1)}, f32[8,128]{1,0:T(8,128)S(1)}, u32[]{:S(2)}, u32[]{:S(2)}) %collective-permute-start.7) | collective-permute-done | bytes 4128 | tf_op jit(solution)/shard_map/ppermute | solution.py:300
  29.3 0.8 %tail.1 = (f32[8,1024]{1,0:T(8,128)}, f32[8,1024]{1,0:T(8,128)}) custom-call(f32[8,128]{1,0:T(8,128)S(1)} %add.15.small, f32[8,1152]{1,0:T(8,128)S(1)} %get-tuple-element.16.mine, f32[8,1152]{1,0:T(8,128)S(1)} %collective-permute-done.4.other, f32[8,1024]{1,0:T(8,128)S(1)} %get-tuple-element.17.direction_ref), custom_call_target="tpu_custom_call" | custom-call | bytes 131072 | tf_op jit(solution)/shard_map/tail/pallas_call | solution.py:385
  (10 shorter events, 0.0 us)
Async XLA Ops:
  1.3 4.4 %copy-start.1 = (f32[3,1024]{1,0:T(4,128)S(1)}, f32[3,1024]{1,0:T(4,128)}, u32[]{:S(2)}) copy-start(f32[3,1024]{1,0:T(4,128)} %refs_1_.3) | copy-start | bytes 36868
  2.1 5.1 %collective-permute-start = (f32[8,768]{1,0:T(8,128)S(1)}, f32[8,768]{1,0:T(8,128)S(1)}, u32[]{:S(2)}, u32[]{:S(2)}) collective-permute-start(f32[8,768]{1,0:T(8,128)S(1)} %pack.1.refs_0_), channel_id=1, source_target_pairs={{9,0},{8,1},{11,2},{10,3},{13,4},{12,5},{15,6},{14,7},{1,8},{0,9},... | collective-permute-start | bytes 73736 | tf_op jit(solution)/shard_map/ppermute | solution.py:300
  7.3 4.5 %collective-permute-start.1 = (f32[8,1536]{1,0:T(8,128)S(1)}, f32[8,1536]{1,0:T(8,128)S(1)}, u32[]{:S(2)}, u32[]{:S(2)}) collective-permute-start(f32[8,1536]{1,0:T(8,128)S(1)} %constant_dynamic-update-slice_fusion.refs_0_), channel_id=1, source_target_pairs={{5,0},{4,1},{7,2},{6,3},{1,4},{0,5},{3,6},{2,7},{13,8},{12,9},{15,... | collective-permute-start | bytes 147464 | tf_op jit(solution)/shard_map/ppermute | solution.py:300
  9.1 3.7 %collective-permute-start.3 = (f32[8,1536]{1,0:T(8,128)S(1)}, f32[8,1536]{1,0:T(8,128)S(1)}, u32[]{:S(2)}, u32[]{:S(2)}) collective-permute-start(f32[8,1536]{1,0:T(8,128)S(1)} %constant_dynamic-update-slice_fusion.refs_0_), channel_id=1, source_target_pairs={{3,0},{2,1},{1,2},{0,3},{7,4},{6,5},{5,6},{4,7},{11,8},{10,9},{9,1... | collective-permute-start | bytes 147464 | tf_op jit(solution)/shard_map/ppermute | solution.py:300
  11.8 3.9 %copy-start = (f32[8,1024]{1,0:T(8,128)S(1)}, f32[8,1024]{1,0:T(8,128)}, u32[]{:S(2)}) copy-start(f32[8,1024]{1,0:T(8,128)} %refs_6_.1) | copy-start | bytes 98308
  11.8 3.9 %copy-start.2 = (f32[1024]{0:T(1024)S(1)}, f32[1024]{0:T(1024)}, u32[]{:S(2)}) copy-start(f32[1024]{0:T(1024)} %refs_5_.1) | copy-start | bytes 12292
  11.8 3.8 %collective-permute-start.2 = (f32[8,1536]{1,0:T(8,128)S(1)}, f32[8,1536]{1,0:T(8,128)S(1)}, u32[]{:S(2)}, u32[]{:S(2)}) collective-permute-start(f32[8,1536]{1,0:T(8,128)S(1)} %collective-permute-done.1.refs_0_), channel_id=1, source_target_pairs={{3,0},{2,1},{1,2},{0,3},{7,4},{6,5},{5,6},{4,7},{11,8},{10,9},{9,1... | collective-permute-start | bytes 147464 | tf_op jit(solution)/shard_map/ppermute | solution.py:300
  17.8 1.3 %collective-permute-start.4 = (f32[8,1152]{1,0:T(8,128)S(1)}, f32[8,1152]{1,0:T(8,128)S(1)}, u32[]{:S(2)}, u32[]{:S(2)}) collective-permute-start(f32[8,1152]{1,0:T(8,128)S(1)} %get-tuple-element.16.mine), channel_id=1, source_target_pairs={{1,0},{0,1},{3,2},{2,3},{5,4},{4,5},{7,6},{6,7},{9,8},{8,9},{11,10... | collective-permute-start | bytes 110600 | tf_op jit(solution)/shard_map/ppermute | solution.py:300
  19.1 4.0 %collective-permute-start.5 = (f32[8,128]{1,0:T(8,128)S(1)}, f32[8,128]{1,0:T(8,128)S(1)}, u32[]{:S(2)}, u32[]{:S(2)}) collective-permute-start(f32[8,128]{1,0:T(8,128)S(1)} %slice_add_fusion), channel_id=1, source_target_pairs={{9,0},{8,1},{11,2},{10,3},{13,4},{12,5},{15,6},{14,7},{1,8},{0,9},... | collective-permute-start | bytes 12296 | tf_op jit(solution)/shard_map/ppermute | solution.py:300
  23.1 3.0 %collective-permute-start.6 = (f32[8,128]{1,0:T(8,128)S(1)}, f32[8,128]{1,0:T(8,128)S(1)}, u32[]{:S(2)}, u32[]{:S(2)}) collective-permute-start(f32[8,128]{1,0:T(8,128)S(1)} %add.13), channel_id=1, source_target_pairs={{5,0},{4,1},{7,2},{6,3},{1,4},{0,5},{3,6},{2,7},{13,8},{12,9},{15,... | collective-permute-start | bytes 12296 | tf_op jit(solution)/shard_map/ppermute | solution.py:300
  26.1 3.1 %collective-permute-start.7 = (f32[8,128]{1,0:T(8,128)S(1)}, f32[8,128]{1,0:T(8,128)S(1)}, u32[]{:S(2)}, u32[]{:S(2)}) collective-permute-start(f32[8,128]{1,0:T(8,128)S(1)} %add.14), channel_id=1, source_target_pairs={{3,0},{2,1},{1,2},{0,3},{7,4},{6,5},{5,6},{4,7},{11,8},{10,9},{9,1... | collective-permute-start | bytes 12296 | tf_op jit(solution)/shard_map/ppermute | solution.py:300

commit v7 on v6

--- a/solution.py
+++ b/solution.py
@@ -173,9 +173,6 @@
             weights[:, at] = jnp.concatenate(rows, axis=0).astype(bf16)
         held = jnp.max(packet[3:4, base + half : base + half + LANES])
         filled = filled + held.astype(jnp.int32) * LANES
-    at = pl.ds(pl.multiple_of(filled, LANES), UNIT)
-    cols[:, at] = jnp.zeros((cols.shape[0], UNIT), bf16)
-    weights[:, at] = jnp.zeros((weights.shape[0], UNIT), bf16)
 
     slots = acc.shape[1]
     if first:
@@ -205,16 +202,16 @@
             acc[:, near] = part + jnp.dot(w, low, preferred_element_type=f32)
 
     full = min(STEP, len(listed) * half)
-    steps = (filled + UNIT - LANES) // full
+    steps = filled // full
     rest = filled - steps * full
 
     @pl.loop(0, steps)
     def _(i):
         step(i * full, full)
 
-    for size in range(UNIT, full, UNIT):
-
-        @pl.when((rest > size - UNIT) & (rest <= size))
+    for size in range(LANES, full, LANES):
+
+        @pl.when(rest == size)
         def _(size=size):
             step(steps * full, size)
 
@@ -334,8 +331,8 @@
             specs += [VMEM] * 2
         count = sum(stop - start for start, stop in taken)
         scratch = [
-            pltpu.VMEM((32, count * half + UNIT), bf16),
-            pltpu.VMEM((6 * width, count * half + UNIT), bf16),
+            pltpu.VMEM((32, count * half), bf16),
+            pltpu.VMEM((6 * width, count * half), bf16),
         ]
         if first or last:
             scratch += [pltpu.SemaphoreType.DMA((4,)), pos_buf]

time: 30.1 us -> 30.5 us (1.013)
  starting transfers between devices: 14.2 us -> 15.2 us
  waiting for transfers between devices: 6.74 us -> 6 us
    ppermute x8, starting transfers between devices: 14.2 us -> 15.2 us  [exchanged(): return lax.ppermute(block, ('blk', 'offs'), route)]
    ppermute x8, waiting for transfers between devices: 6.74 us -> 6 us  [exchanged(): return lax.ppermute(block, ('blk', 'offs'), route)]
  transfers between devices with their start and end apart: 8 -> 8, of which waited for: 6 -> 6; matrix products, arithmetic and copies ran while one was open for 0% -> 0% of each run, Pallas kernels for 13% -> 14%
where the time goes in v7:
time: 30.5 us; the launch traced here: 30.3 us
  starting transfers between devices  15.2 us (50%)
  Pallas kernels  7.8 us (26%)
  waiting for transfers between devices  6 us (20%)
  between operations  1.35 us (4%)
    ppermute x8, starting transfers between devices, exchanged(): return lax.ppermute(block, ('blk', 'offs'), route)  15.2 us
    pallas_call x4, Pallas kernels, pairs(): call(kernel, outs, specs, (VMEM,) * len(outs), scratch, name, flops)(*args)  6.15 us
    ppermute x8, waiting for transfers between devices, exchanged(): return lax.ppermute(block, ('blk', 'offs'), route)  6 us
    pallas_call x1, Pallas kernels, body(): call(pack_kernel, shape((width, half + half // 2), f32), [HBM, HBM, HBM],...  0.85 us
    pallas_call x1, Pallas kernels, body(): call(tail_kernel, (shape(rhs.shape, f32),) * 2, [VMEM] * 4, (VMEM, VMEM),...  0.81 us
  transfers between devices with their start and end apart: 8, of which 6 were waited for; matrix products, arithmetic and copies ran while one was open for 0% of the time, Pallas kernels for 14%

profile of v7, /device:TPU:0, one launch (start us, length us, event | category | flops | bytes accessed | tf_op | source)
XLA Modules:
  0.0 30.3 jit_solution(3149105139052423730)
XLA Ops:
  1.3 0.0 copy-start.1
  1.3 0.8 %pack.1.refs_0_ = f32[8,768]{1,0:T(8,128)S(1)} custom-call(f32[3,1024]{1,0:T(4,128)} %refs_1_.3, f32[8,1024]{1,0:T(8,128)} %refs_6_.1, s32[1]{0:T(128)S(6)} %copy.7.count_hbm.refs_7_), custom_call_target="tpu_custom_call" | custom-call | bytes 131072 | tf_op jit(solution)/shard_map/pack/pallas_call | solution.py:311
  2.1 3.5 %collective-permute-start = (f32[8,768]{1,0:T(8,128)S(1)}, f32[8,768]{1,0:T(8,128)S(1)}, u32[]{:S(2)}, u32[]{:S(2)}) collective-permute-start(f32[8,768]{1,0:T(8,128)S(1)} %pack.1.refs_0_), channel_id=1, source_target_pairs={{9,0},{8,1},{11,2},{10,3},{13,4},{12,5},{15,6},{14,7},{1,8},{0,9},... | collective-permute-start | bytes 73736 | tf_op jit(solution)/shard_map/ppermute | solution.py:297
  5.7 1.3 %pairs_1.2 = (f32[8,768]{1,0:T(8,128)S(1)}, f32[48,1024]{1,0:T(8,128)S(1)}, bf16[32,1024]{1,0:T(8,128)(2,1)S(1)}, f32[8,128]{1,0:T(8,128)S(1)}) custom-call(f32[8,768]{1,0:T(8,128)S(1)} %pack.1.refs_0_, f32[3,1024]{1,0:T(4,128)S(1)} %copy-done.1), custom_call_target="tpu_custom_call" | custom-call | flops 67108864 | bytes 131072 | tf_op jit(solution)/shard_map/pairs_1/pallas_call | solution.py:353
  7.0 0.3 collective-permute-done
  7.3 1.8 %collective-permute-start.1 = (f32[8,1536]{1,0:T(8,128)S(1)}, f32[8,1536]{1,0:T(8,128)S(1)}, u32[]{:S(2)}, u32[]{:S(2)}) collective-permute-start(f32[8,1536]{1,0:T(8,128)S(1)} %constant_dynamic-update-slice_fusion.refs_0_), channel_id=1, source_target_pairs={{5,0},{4,1},{7,2},{6,3},{1,4},{0,5},{3,6},{2,7},{13,8},{12,9},{15,... | collective-permute-start | bytes 147464 | tf_op jit(solution)/shard_map/ppermute | solution.py:297
  9.1 1.6 %collective-permute-start.3 = (f32[8,1536]{1,0:T(8,128)S(1)}, f32[8,1536]{1,0:T(8,128)S(1)}, u32[]{:S(2)}, u32[]{:S(2)}) collective-permute-start(f32[8,1536]{1,0:T(8,128)S(1)} %constant_dynamic-update-slice_fusion.refs_0_), channel_id=1, source_target_pairs={{3,0},{2,1},{1,2},{0,3},{7,4},{6,5},{5,6},{4,7},{11,8},{10,9},{9,1... | collective-permute-start | bytes 147464 | tf_op jit(solution)/shard_map/ppermute | solution.py:297
  10.7 0.8 %pairs_1.3.refs_3_ = f32[48,1024]{1,0:T(8,128)S(1)} custom-call(f32[8,1536]{1,0:T(8,128)S(1)} %constant_dynamic-update-slice_fusion.refs_0_, bf16[32,1024]{1,0:T(8,128)(2,1)S(1)} %get-tuple-element.11.refs_1_.refs_2_, f32[48,1024]{1,0:T(8,128)S(1)} %get-tuple-element.12.refs_2_), custom_call_target="tpu_custom_call" | custom-call | flops 67108864 | bytes 131072 | tf_op jit(solution)/shard_map/pairs_1/pallas_call | solution.py:353
  11.5 0.0 copy-start.2
  11.5 0.0 collective-permute-done.1.refs_0_
  11.5 1.3 %collective-permute-start.2 = (f32[8,1536]{1,0:T(8,128)S(1)}, f32[8,1536]{1,0:T(8,128)S(1)}, u32[]{:S(2)}, u32[]{:S(2)}) collective-permute-start(f32[8,1536]{1,0:T(8,128)S(1)} %collective-permute-done.1.refs_0_), channel_id=1, source_target_pairs={{3,0},{2,1},{1,2},{0,3},{7,4},{6,5},{5,6},{4,7},{11,8},{10,9},{9,1... | collective-permute-start | bytes 147464 | tf_op jit(solution)/shard_map/ppermute | solution.py:297
  12.8 0.0 collective-permute-done.3.refs_1_
  12.8 2.1 %pairs_4.1.refs_3_ = f32[48,1024]{1,0:T(8,128)S(1)} custom-call(f32[8,1536]{1,0:T(8,128)S(1)} %collective-permute-done.1.refs_0_, f32[8,1536]{1,0:T(8,128)S(1)} %collective-permute-done.3.refs_1_, bf16[32,1024]{1,0:T(8,128)(2,1)S(1)} %get-tuple-element.11.refs_1_.refs_2_, f32[48,1024]{1,0:T(8,128)S(1)} %pairs_1.3.refs_3_), custom_call_target="tpu_custom_call" | custom-call | flops 268435456 | bytes 131072 | tf_op jit(solution)/shard_map/pairs_4/pallas_call | solution.py:353
  14.9 0.3 %collective-permute-done.2.refs_0_ = f32[8,1536]{1,0:T(8,128)S(1)} collective-permute-done((f32[8,1536]{1,0:T(8,128)S(1)}, f32[8,1536]{1,0:T(8,128)S(1)}, u32[]{:S(2)}, u32[]{:S(2)}) %collective-permute-start.2) | collective-permute-done | bytes 49184 | tf_op jit(solution)/shard_map/ppermute | solution.py:297
  15.2 2.0 %pairs_2.1 = (f32[8,1152]{1,0:T(8,128)S(1)}, f32[8,1024]{1,0:T(8,128)S(1)}) custom-call(f32[8,1536]{1,0:T(8,128)S(1)} %collective-permute-done.2.refs_0_, f32[3,1024]{1,0:T(4,128)S(1)} %copy-done.1, bf16[32,1024]{1,0:T(8,128)(2,1)S(1)} %get-tuple-element.11.refs_1_.refs_2_, f32[48,1024]{1,0:T(8,128)S(1)} %pairs_4.1.refs_3_, ...), custom_call_target="tpu_custom_call" | custom-call | flops 134217728 | bytes 131072 | tf_op jit(solution)/shard_map/pairs_2/pallas_call | solution.py:353
  17.2 0.4 %collective-permute-start.4 = (f32[8,1152]{1,0:T(8,128)S(1)}, f32[8,1152]{1,0:T(8,128)S(1)}, u32[]{:S(2)}, u32[]{:S(2)}) collective-permute-start(f32[8,1152]{1,0:T(8,128)S(1)} %get-tuple-element.16.mine), channel_id=1, source_target_pairs={{1,0},{0,1},{3,2},{2,3},{5,4},{4,5},{7,6},{6,7},{9,8},{8,9},{11,10... | collective-permute-start | bytes 110600 | tf_op jit(solution)/shard_map/ppermute | solution.py:297
  17.6 0.9 %collective-permute-done.4.other = f32[8,1152]{1,0:T(8,128)S(1)} collective-permute-done((f32[8,1152]{1,0:T(8,128)S(1)}, f32[8,1152]{1,0:T(8,128)S(1)}, u32[]{:S(2)}, u32[]{:S(2)}) %collective-permute-start.4) | collective-permute-done | bytes 36896 | tf_op jit(solution)/shard_map/ppermute | solution.py:297
  18.5 3.6 %collective-permute-start.5 = (f32[8,128]{1,0:T(8,128)S(1)}, f32[8,128]{1,0:T(8,128)S(1)}, u32[]{:S(2)}, u32[]{:S(2)}) collective-permute-start(f32[8,128]{1,0:T(8,128)S(1)} %slice_add_fusion), channel_id=1, source_target_pairs={{9,0},{8,1},{11,2},{10,3},{13,4},{12,5},{15,6},{14,7},{1,8},{0,9},... | collective-permute-start | bytes 12296 | tf_op jit(solution)/shard_map/ppermute | solution.py:297
  22.1 1.3 %collective-permute-done.5 = f32[8,128]{1,0:T(8,128)S(1)} collective-permute-done((f32[8,128]{1,0:T(8,128)S(1)}, f32[8,128]{1,0:T(8,128)S(1)}, u32[]{:S(2)}, u32[]{:S(2)}) %collective-permute-start.5) | collective-permute-done | bytes 4128 | tf_op jit(solution)/shard_map/ppermute | solution.py:297
  23.5 1.3 %collective-permute-start.6 = (f32[8,128]{1,0:T(8,128)S(1)}, f32[8,128]{1,0:T(8,128)S(1)}, u32[]{:S(2)}, u32[]{:S(2)}) collective-permute-start(f32[8,128]{1,0:T(8,128)S(1)} %add.13), channel_id=1, source_target_pairs={{5,0},{4,1},{7,2},{6,3},{1,4},{0,5},{3,6},{2,7},{13,8},{12,9},{15,... | collective-permute-start | bytes 12296 | tf_op jit(solution)/shard_map/ppermute | solution.py:297
  24.7 1.8 %collective-permute-done.6 = f32[8,128]{1,0:T(8,128)S(1)} collective-permute-done((f32[8,128]{1,0:T(8,128)S(1)}, f32[8,128]{1,0:T(8,128)S(1)}, u32[]{:S(2)}, u32[]{:S(2)}) %collective-permute-start.6) | collective-permute-done | bytes 4128 | tf_op jit(solution)/shard_map/ppermute | solution.py:297
  26.5 1.6 %collective-permute-start.7 = (f32[8,128]{1,0:T(8,128)S(1)}, f32[8,128]{1,0:T(8,128)S(1)}, u32[]{:S(2)}, u32[]{:S(2)}) collective-permute-start(f32[8,128]{1,0:T(8,128)S(1)} %add.14), channel_id=1, source_target_pairs={{3,0},{2,1},{1,2},{0,3},{7,4},{6,5},{5,6},{4,7},{11,8},{10,9},{9,1... | collective-permute-start | bytes 12296 | tf_op jit(solution)/shard_map/ppermute | solution.py:297
  28.1 1.4 %collective-permute-done.7 = f32[8,128]{1,0:T(8,128)S(1)} collective-permute-done((f32[8,128]{1,0:T(8,128)S(1)}, f32[8,128]{1,0:T(8,128)S(1)}, u32[]{:S(2)}, u32[]{:S(2)}) %collective-permute-start.7) | collective-permute-done | bytes 4128 | tf_op jit(solution)/shard_map/ppermute | solution.py:297
  29.5 0.8 %tail.1 = (f32[8,1024]{1,0:T(8,128)}, f32[8,1024]{1,0:T(8,128)}) custom-call(f32[8,128]{1,0:T(8,128)S(1)} %add.15.small, f32[8,1152]{1,0:T(8,128)S(1)} %get-tuple-element.16.mine, f32[8,1152]{1,0:T(8,128)S(1)} %collective-permute-done.4.other, f32[8,1024]{1,0:T(8,128)S(1)} %get-tuple-element.17.direction_ref), custom_call_target="tpu_custom_call" | custom-call | bytes 131072 | tf_op jit(solution)/shard_map/tail/pallas_call | solution.py:382
  (10 shorter events, 0.0 us)
Async XLA Ops:
  1.3 4.4 %copy-start.1 = (f32[3,1024]{1,0:T(4,128)S(1)}, f32[3,1024]{1,0:T(4,128)}, u32[]{:S(2)}) copy-start(f32[3,1024]{1,0:T(4,128)} %refs_1_.3) | copy-start | bytes 36868
  2.1 5.1 %collective-permute-start = (f32[8,768]{1,0:T(8,128)S(1)}, f32[8,768]{1,0:T(8,128)S(1)}, u32[]{:S(2)}, u32[]{:S(2)}) collective-permute-start(f32[8,768]{1,0:T(8,128)S(1)} %pack.1.refs_0_), channel_id=1, source_target_pairs={{9,0},{8,1},{11,2},{10,3},{13,4},{12,5},{15,6},{14,7},{1,8},{0,9},... | collective-permute-start | bytes 73736 | tf_op jit(solution)/shard_map/ppermute | solution.py:297
  7.3 4.2 %collective-permute-start.1 = (f32[8,1536]{1,0:T(8,128)S(1)}, f32[8,1536]{1,0:T(8,128)S(1)}, u32[]{:S(2)}, u32[]{:S(2)}) collective-permute-start(f32[8,1536]{1,0:T(8,128)S(1)} %constant_dynamic-update-slice_fusion.refs_0_), channel_id=1, source_target_pairs={{5,0},{4,1},{7,2},{6,3},{1,4},{0,5},{3,6},{2,7},{13,8},{12,9},{15,... | collective-permute-start | bytes 147464 | tf_op jit(solution)/shard_map/ppermute | solution.py:297
  9.1 3.7 %collective-permute-start.3 = (f32[8,1536]{1,0:T(8,128)S(1)}, f32[8,1536]{1,0:T(8,128)S(1)}, u32[]{:S(2)}, u32[]{:S(2)}) collective-permute-start(f32[8,1536]{1,0:T(8,128)S(1)} %constant_dynamic-update-slice_fusion.refs_0_), channel_id=1, source_target_pairs={{3,0},{2,1},{1,2},{0,3},{7,4},{6,5},{5,6},{4,7},{11,8},{10,9},{9,1... | collective-permute-start | bytes 147464 | tf_op jit(solution)/shard_map/ppermute | solution.py:297
  11.5 3.8 %copy-start = (f32[8,1024]{1,0:T(8,128)S(1)}, f32[8,1024]{1,0:T(8,128)}, u32[]{:S(2)}) copy-start(f32[8,1024]{1,0:T(8,128)} %refs_6_.1) | copy-start | bytes 98308
  11.5 3.8 %copy-start.2 = (f32[1024]{0:T(1024)S(1)}, f32[1024]{0:T(1024)}, u32[]{:S(2)}) copy-start(f32[1024]{0:T(1024)} %refs_5_.1) | copy-start | bytes 12292
  11.5 3.7 %collective-permute-start.2 = (f32[8,1536]{1,0:T(8,128)S(1)}, f32[8,1536]{1,0:T(8,128)S(1)}, u32[]{:S(2)}, u32[]{:S(2)}) collective-permute-start(f32[8,1536]{1,0:T(8,128)S(1)} %collective-permute-done.1.refs_0_), channel_id=1, source_target_pairs={{3,0},{2,1},{1,2},{0,3},{7,4},{6,5},{5,6},{4,7},{11,8},{10,9},{9,1... | collective-permute-start | bytes 147464 | tf_op jit(solution)/shard_map/ppermute | solution.py:297
  17.2 1.3 %collective-permute-start.4 = (f32[8,1152]{1,0:T(8,128)S(1)}, f32[8,1152]{1,0:T(8,128)S(1)}, u32[]{:S(2)}, u32[]{:S(2)}) collective-permute-start(f32[8,1152]{1,0:T(8,128)S(1)} %get-tuple-element.16.mine), channel_id=1, source_target_pairs={{1,0},{0,1},{3,2},{2,3},{5,4},{4,5},{7,6},{6,7},{9,8},{8,9},{11,10... | collective-permute-start | bytes 110600 | tf_op jit(solution)/shard_map/ppermute | solution.py:297
  18.5 5.0 %collective-permute-start.5 = (f32[8,128]{1,0:T(8,128)S(1)}, f32[8,128]{1,0:T(8,128)S(1)}, u32[]{:S(2)}, u32[]{:S(2)}) collective-permute-start(f32[8,128]{1,0:T(8,128)S(1)} %slice_add_fusion), channel_id=1, source_target_pairs={{9,0},{8,1},{11,2},{10,3},{13,4},{12,5},{15,6},{14,7},{1,8},{0,9},... | collective-permute-start | bytes 12296 | tf_op jit(solution)/shard_map/ppermute | solution.py:297
  23.5 3.0 %collective-permute-start.6 = (f32[8,128]{1,0:T(8,128)S(1)}, f32[8,128]{1,0:T(8,128)S(1)}, u32[]{:S(2)}, u32[]{:S(2)}) collective-permute-start(f32[8,128]{1,0:T(8,128)S(1)} %add.13), channel_id=1, source_target_pairs={{5,0},{4,1},{7,2},{6,3},{1,4},{0,5},{3,6},{2,7},{13,8},{12,9},{15,... | collective-permute-start | bytes 12296 | tf_op jit(solution)/shard_map/ppermute | solution.py:297
  26.5 3.0 %collective-permute-start.7 = (f32[8,128]{1,0:T(8,128)S(1)}, f32[8,128]{1,0:T(8,128)S(1)}, u32[]{:S(2)}, u32[]{:S(2)}) collective-permute-start(f32[8,128]{1,0:T(8,128)S(1)} %add.14), channel_id=1, source_target_pairs={{3,0},{2,1},{1,2},{0,3},{7,4},{6,5},{5,6},{4,7},{11,8},{10,9},{9,1... | collective-permute-start | bytes 12296 | tf_op jit(solution)/shard_map/ppermute | solution.py:297

commit v8 on v7

--- a/solution.py
+++ b/solution.py
@@ -80,24 +80,23 @@
     return out
 
 
-def pack_kernel(pos_hbm, rhs_hbm, count_hbm, out, pos, rhs, count, sems):
-    copies = [
-        pltpu.make_async_copy(pos_hbm, pos, sems.at[0]),
-        pltpu.make_async_copy(rhs_hbm, rhs, sems.at[1]),
-        pltpu.make_async_copy(count_hbm, count, sems.at[2]),
-    ]
-    for copy in copies:
-        copy.start()
-    for copy in copies:
-        copy.wait()
+def first_kernel(out):
+    out[...] = jnp.zeros(out.shape, jnp.int32)
+
+
+def count_kernel(count, first, out):
+    out[...] = jnp.full(out.shape, count[0], jnp.int32) + first[...]
+
+
+def pack_kernel(pos, rhs, count, out):
     width, slots = rhs.shape
     tiles = slots // LANES // 2
     side = (lax.axis_index("offs") + lax.axis_index("blk")) % 2
     odd = side == 1
-    n = count[0]
+    n = count[...]
     lane = lax.broadcasted_iota(jnp.int32, (1, LANES), 1)
     held = jnp.clip((n + LANES - 1 - side * LANES + LANES) // (2 * LANES), 0, tiles)
-    held = jnp.full((1, LANES), held.astype(f32))
+    held = held.astype(f32)
     for t in range(tiles):
         even_at = slice(2 * t * LANES, (2 * t + 1) * LANES)
         odd_at = slice((2 * t + 1) * LANES, (2 * t + 2) * LANES)
@@ -308,14 +307,27 @@
     noise_buf = pltpu.VMEM(noise_var.shape, f32)
     count_buf = pltpu.SMEM((1,), jnp.int32)
 
+    first = call(
+        first_kernel, shape((1, LANES), jnp.int32), [], VMEM, [], "first", 1 << 30
+    )()
+    block_count, first = lax.optimization_barrier((block_count, first))
+    counted = call(
+        count_kernel,
+        shape((1, LANES), jnp.int32),
+        [pl.BlockSpec(memory_space=pltpu.SMEM), VMEM],
+        VMEM,
+        [],
+        "count",
+        0,
+    )(block_count, first)
     packet = call(
         pack_kernel,
         shape((width, half + half // 2), f32),
-        [HBM, HBM, HBM],
+        [VMEM] * 3,
         VMEM,
-        [pos_buf, rhs_buf, count_buf, pltpu.SemaphoreType.DMA((3,))],
+        [],
         "pack",
-    )(*(pltpu.with_memory_space_constraint(x, pltpu.HBM) for x in (position, rhs)), block_count)
+    )(position, rhs, counted)
 
     acc_shape = shape((6 * width, slots), f32)
     rows_shape = shape((32, slots), bf16)

time: 30.5 us -> 29.8 us (0.977); the launches traced: 30.3 us -> 29.3 us
  waiting for transfers between devices: 6 us -> 5.32 us
  Pallas kernels: 7.8 us -> 7.24 us
    pallas_call x1 -> x3, Pallas kernels: 0.85 us -> 0.03 us  [the longest x1 0.02 us: body(): call(pack_kernel, shape((width, half + half // 2), f32), [VMEM] * 3, VMEM...]
    ppermute x8, waiting for transfers between devices: 6 us -> 5.32 us  [exchanged(): return lax.ppermute(block, ('blk', 'offs'), route)]
  transfers between devices with their start and end apart: 8 -> 8, of which waited for: 6 -> 5; matrix products, arithmetic and copies ran while one was open for 0% -> 0% of each run, Pallas kernels for 14% -> 16%
where the time goes in v8:
time: 29.8 us; the launch traced here: 29.3 us
  starting transfers between devices  15.2 us (51%)
  Pallas kernels  7.24 us (24%)
  waiting for transfers between devices  5.32 us (18%)
  between operations  1.4 us (5%)
    ppermute x8, starting transfers between devices, exchanged(): return lax.ppermute(block, ('blk', 'offs'), route)  15.2 us
    pallas_call x4, Pallas kernels, pairs(): call(kernel, outs, specs, (VMEM,) * len(outs), scratch, name, flops)(*args)  6.4 us
    ppermute x8, waiting for transfers between devices, exchanged(): return lax.ppermute(block, ('blk', 'offs'), route)  5.32 us
    pallas_call x1, Pallas kernels, body(): call(tail_kernel, (shape(rhs.shape, f32),) * 2, [VMEM] * 4, (VMEM, VMEM),...  0.81 us
  transfers between devices with their start and end apart: 8, of which 5 were waited for; matrix products, arithmetic and copies ran while one was open for 0% of the time, Pallas kernels for 16%

profile of v8, /device:TPU:0, one launch (start us, length us, event | category | flops | bytes accessed | tf_op | source)
XLA Modules:
  0.0 29.3 jit_solution(1708655703378775993)
XLA Ops:
  1.3 0.0 copy-done.1
  1.3 0.1 copy-done
  1.4 3.5 %collective-permute-start = (f32[8,768]{1,0:T(8,128)S(1)}, f32[8,768]{1,0:T(8,128)S(1)}, u32[]{:S(2)}, u32[]{:S(2)}) collective-permute-start(f32[8,768]{1,0:T(8,128)S(1)} %pack.1.refs_0_), channel_id=1, source_target_pairs={{9,0},{8,1},{11,2},{10,3},{13,4},{12,5},{15,6},{14,7},{1,8},{0,9},... | collective-permute-start | bytes 73736 | tf_op jit(solution)/shard_map/ppermute | solution.py:296
  5.0 1.3 %pairs_1.2 = (f32[8,768]{1,0:T(8,128)S(1)}, f32[48,1024]{1,0:T(8,128)S(1)}, bf16[32,1024]{1,0:T(8,128)(2,1)S(1)}, f32[8,128]{1,0:T(8,128)S(1)}) custom-call(f32[8,768]{1,0:T(8,128)S(1)} %pack.1.refs_0_, f32[3,1024]{1,0:T(4,128)S(1)} %copy-done.1), custom_call_target="tpu_custom_call" | custom-call | flops 67108864 | bytes 131072 | tf_op jit(solution)/shard_map/pairs_1/pallas_call | solution.py:365
  6.3 0.3 collective-permute-done
  6.6 1.8 %collective-permute-start.1 = (f32[8,1536]{1,0:T(8,128)S(1)}, f32[8,1536]{1,0:T(8,128)S(1)}, u32[]{:S(2)}, u32[]{:S(2)}) collective-permute-start(f32[8,1536]{1,0:T(8,128)S(1)} %constant_dynamic-update-slice_fusion.refs_0_), channel_id=1, source_target_pairs={{5,0},{4,1},{7,2},{6,3},{1,4},{0,5},{3,6},{2,7},{13,8},{12,9},{15,... | collective-permute-start | bytes 147464 | tf_op jit(solution)/shard_map/ppermute | solution.py:296
  8.4 1.6 %collective-permute-start.3 = (f32[8,1536]{1,0:T(8,128)S(1)}, f32[8,1536]{1,0:T(8,128)S(1)}, u32[]{:S(2)}, u32[]{:S(2)}) collective-permute-start(f32[8,1536]{1,0:T(8,128)S(1)} %constant_dynamic-update-slice_fusion.refs_0_), channel_id=1, source_target_pairs={{3,0},{2,1},{1,2},{0,3},{7,4},{6,5},{5,6},{4,7},{11,8},{10,9},{9,1... | collective-permute-start | bytes 147464 | tf_op jit(solution)/shard_map/ppermute | solution.py:296
  10.0 0.6 %pairs_1.3.refs_3_ = f32[48,1024]{1,0:T(8,128)S(1)} custom-call(f32[8,1536]{1,0:T(8,128)S(1)} %constant_dynamic-update-slice_fusion.refs_0_, bf16[32,1024]{1,0:T(8,128)(2,1)S(1)} %get-tuple-element.15.refs_1_.refs_2_, f32[48,1024]{1,0:T(8,128)S(1)} %get-tuple-element.16.refs_2_), custom_call_target="tpu_custom_call" | custom-call | flops 67108864 | bytes 131072 | tf_op jit(solution)/shard_map/pairs_1/pallas_call | solution.py:365
  10.6 0.0 copy-start.2
  10.6 0.0 collective-permute-done.1.refs_0_
  10.6 1.5 %collective-permute-start.2 = (f32[8,1536]{1,0:T(8,128)S(1)}, f32[8,1536]{1,0:T(8,128)S(1)}, u32[]{:S(2)}, u32[]{:S(2)}) collective-permute-start(f32[8,1536]{1,0:T(8,128)S(1)} %collective-permute-done.1.refs_0_), channel_id=1, source_target_pairs={{3,0},{2,1},{1,2},{0,3},{7,4},{6,5},{5,6},{4,7},{11,8},{10,9},{9,1... | collective-permute-start | bytes 147464 | tf_op jit(solution)/shard_map/ppermute | solution.py:296
  12.1 0.0 collective-permute-done.3.refs_1_
  12.1 2.9 %pairs_4.1.refs_3_ = f32[48,1024]{1,0:T(8,128)S(1)} custom-call(f32[8,1536]{1,0:T(8,128)S(1)} %collective-permute-done.1.refs_0_, f32[8,1536]{1,0:T(8,128)S(1)} %collective-permute-done.3.refs_1_, bf16[32,1024]{1,0:T(8,128)(2,1)S(1)} %get-tuple-element.15.refs_1_.refs_2_, f32[48,1024]{1,0:T(8,128)S(1)} %pairs_1.3.refs_3_), custom_call_target="tpu_custom_call" | custom-call | flops 268435456 | bytes 131072 | tf_op jit(solution)/shard_map/pairs_4/pallas_call | solution.py:365
  15.0 0.0 collective-permute-done.2.refs_0_
  15.0 1.6 %pairs_2.1 = (f32[8,1152]{1,0:T(8,128)S(1)}, f32[8,1024]{1,0:T(8,128)S(1)}) custom-call(f32[8,1536]{1,0:T(8,128)S(1)} %collective-permute-done.2.refs_0_, f32[3,1024]{1,0:T(4,128)S(1)} %copy-done.1, bf16[32,1024]{1,0:T(8,128)(2,1)S(1)} %get-tuple-element.15.refs_1_.refs_2_, f32[48,1024]{1,0:T(8,128)S(1)} %pairs_4.1.refs_3_, ...), custom_call_target="tpu_custom_call" | custom-call | flops 134217728 | bytes 131072 | tf_op jit(solution)/shard_map/pairs_2/pallas_call | solution.py:365
  16.6 0.7 %collective-permute-start.4 = (f32[8,1152]{1,0:T(8,128)S(1)}, f32[8,1152]{1,0:T(8,128)S(1)}, u32[]{:S(2)}, u32[]{:S(2)}) collective-permute-start(f32[8,1152]{1,0:T(8,128)S(1)} %get-tuple-element.20.mine), channel_id=1, source_target_pairs={{1,0},{0,1},{3,2},{2,3},{5,4},{4,5},{7,6},{6,7},{9,8},{8,9},{11,10... | collective-permute-start | bytes 110600 | tf_op jit(solution)/shard_map/ppermute | solution.py:296
  17.3 0.9 %collective-permute-done.4.other = f32[8,1152]{1,0:T(8,128)S(1)} collective-permute-done((f32[8,1152]{1,0:T(8,128)S(1)}, f32[8,1152]{1,0:T(8,128)S(1)}, u32[]{:S(2)}, u32[]{:S(2)}) %collective-permute-start.4) | collective-permute-done | bytes 36896 | tf_op jit(solution)/shard_map/ppermute | solution.py:296
  18.2 2.9 %collective-permute-start.5 = (f32[8,128]{1,0:T(8,128)S(1)}, f32[8,128]{1,0:T(8,128)S(1)}, u32[]{:S(2)}, u32[]{:S(2)}) collective-permute-start(f32[8,128]{1,0:T(8,128)S(1)} %slice_add_fusion), channel_id=1, source_target_pairs={{9,0},{8,1},{11,2},{10,3},{13,4},{12,5},{15,6},{14,7},{1,8},{0,9},... | collective-permute-start | bytes 12296 | tf_op jit(solution)/shard_map/ppermute | solution.py:296
  21.0 1.3 %collective-permute-done.5 = f32[8,128]{1,0:T(8,128)S(1)} collective-permute-done((f32[8,128]{1,0:T(8,128)S(1)}, f32[8,128]{1,0:T(8,128)S(1)}, u32[]{:S(2)}, u32[]{:S(2)}) %collective-permute-start.5) | collective-permute-done | bytes 4128 | tf_op jit(solution)/shard_map/ppermute | solution.py:296
  22.4 1.6 %collective-permute-start.6 = (f32[8,128]{1,0:T(8,128)S(1)}, f32[8,128]{1,0:T(8,128)S(1)}, u32[]{:S(2)}, u32[]{:S(2)}) collective-permute-start(f32[8,128]{1,0:T(8,128)S(1)} %add.13), channel_id=1, source_target_pairs={{5,0},{4,1},{7,2},{6,3},{1,4},{0,5},{3,6},{2,7},{13,8},{12,9},{15,... | collective-permute-start | bytes 12296 | tf_op jit(solution)/shard_map/ppermute | solution.py:296
  24.0 1.4 %collective-permute-done.6 = f32[8,128]{1,0:T(8,128)S(1)} collective-permute-done((f32[8,128]{1,0:T(8,128)S(1)}, f32[8,128]{1,0:T(8,128)S(1)}, u32[]{:S(2)}, u32[]{:S(2)}) %collective-permute-start.6) | collective-permute-done | bytes 4128 | tf_op jit(solution)/shard_map/ppermute | solution.py:296
  25.4 1.6 %collective-permute-start.7 = (f32[8,128]{1,0:T(8,128)S(1)}, f32[8,128]{1,0:T(8,128)S(1)}, u32[]{:S(2)}, u32[]{:S(2)}) collective-permute-start(f32[8,128]{1,0:T(8,128)S(1)} %add.14), channel_id=1, source_target_pairs={{3,0},{2,1},{1,2},{0,3},{7,4},{6,5},{5,6},{4,7},{11,8},{10,9},{9,1... | collective-permute-start | bytes 12296 | tf_op jit(solution)/shard_map/ppermute | solution.py:296
  27.0 1.4 %collective-permute-done.7 = f32[8,128]{1,0:T(8,128)S(1)} collective-permute-done((f32[8,128]{1,0:T(8,128)S(1)}, f32[8,128]{1,0:T(8,128)S(1)}, u32[]{:S(2)}, u32[]{:S(2)}) %collective-permute-start.7) | collective-permute-done | bytes 4128 | tf_op jit(solution)/shard_map/ppermute | solution.py:296
  28.5 0.8 %tail.1 = (f32[8,1024]{1,0:T(8,128)}, f32[8,1024]{1,0:T(8,128)}) custom-call(f32[8,128]{1,0:T(8,128)S(1)} %add.15.small, f32[8,1152]{1,0:T(8,128)S(1)} %get-tuple-element.20.mine, f32[8,1152]{1,0:T(8,128)S(1)} %collective-permute-done.4.other, f32[8,1024]{1,0:T(8,128)S(1)} %get-tuple-element.21.direction_ref), custom_call_target="tpu_custom_call" | custom-call | bytes 131072 | tf_op jit(solution)/shard_map/tail/pallas_call | solution.py:394
  (12 shorter events, 0.1 us)
Async XLA Ops:
  0.6 0.7 %copy-start.1 = (f32[3,1024]{1,0:T(4,128)S(1)}, f32[3,1024]{1,0:T(4,128)}, u32[]{:S(2)}) copy-start(f32[3,1024]{1,0:T(4,128)} %refs_1_.3) | copy-start | bytes 36868
  0.6 0.8 %copy-start = (f32[8,1024]{1,0:T(8,128)S(1)}, f32[8,1024]{1,0:T(8,128)}, u32[]{:S(2)}) copy-start(f32[8,1024]{1,0:T(8,128)} %refs_6_.1) | copy-start | bytes 98308
  1.4 5.1 %collective-permute-start = (f32[8,768]{1,0:T(8,128)S(1)}, f32[8,768]{1,0:T(8,128)S(1)}, u32[]{:S(2)}, u32[]{:S(2)}) collective-permute-start(f32[8,768]{1,0:T(8,128)S(1)} %pack.1.refs_0_), channel_id=1, source_target_pairs={{9,0},{8,1},{11,2},{10,3},{13,4},{12,5},{15,6},{14,7},{1,8},{0,9},... | collective-permute-start | bytes 73736 | tf_op jit(solution)/shard_map/ppermute | solution.py:296
  6.6 4.0 %collective-permute-start.1 = (f32[8,1536]{1,0:T(8,128)S(1)}, f32[8,1536]{1,0:T(8,128)S(1)}, u32[]{:S(2)}, u32[]{:S(2)}) collective-permute-start(f32[8,1536]{1,0:T(8,128)S(1)} %constant_dynamic-update-slice_fusion.refs_0_), channel_id=1, source_target_pairs={{5,0},{4,1},{7,2},{6,3},{1,4},{0,5},{3,6},{2,7},{13,8},{12,9},{15,... | collective-permute-start | bytes 147464 | tf_op jit(solution)/shard_map/ppermute | solution.py:296
  8.4 3.7 %collective-permute-start.3 = (f32[8,1536]{1,0:T(8,128)S(1)}, f32[8,1536]{1,0:T(8,128)S(1)}, u32[]{:S(2)}, u32[]{:S(2)}) collective-permute-start(f32[8,1536]{1,0:T(8,128)S(1)} %constant_dynamic-update-slice_fusion.refs_0_), channel_id=1, source_target_pairs={{3,0},{2,1},{1,2},{0,3},{7,4},{6,5},{5,6},{4,7},{11,8},{10,9},{9,1... | collective-permute-start | bytes 147464 | tf_op jit(solution)/shard_map/ppermute | solution.py:296
  10.6 4.5 %copy-start.2 = (f32[1024]{0:T(1024)S(1)}, f32[1024]{0:T(1024)}, u32[]{:S(2)}) copy-start(f32[1024]{0:T(1024)} %refs_5_.1) | copy-start | bytes 12292
  10.6 4.4 %collective-permute-start.2 = (f32[8,1536]{1,0:T(8,128)S(1)}, f32[8,1536]{1,0:T(8,128)S(1)}, u32[]{:S(2)}, u32[]{:S(2)}) collective-permute-start(f32[8,1536]{1,0:T(8,128)S(1)} %collective-permute-done.1.refs_0_), channel_id=1, source_target_pairs={{3,0},{2,1},{1,2},{0,3},{7,4},{6,5},{5,6},{4,7},{11,8},{10,9},{9,1... | collective-permute-start | bytes 147464 | tf_op jit(solution)/shard_map/ppermute | solution.py:296
  16.6 1.5 %collective-permute-start.4 = (f32[8,1152]{1,0:T(8,128)S(1)}, f32[8,1152]{1,0:T(8,128)S(1)}, u32[]{:S(2)}, u32[]{:S(2)}) collective-permute-start(f32[8,1152]{1,0:T(8,128)S(1)} %get-tuple-element.20.mine), channel_id=1, source_target_pairs={{1,0},{0,1},{3,2},{2,3},{5,4},{4,5},{7,6},{6,7},{9,8},{8,9},{11,10... | collective-permute-start | bytes 110600 | tf_op jit(solution)/shard_map/ppermute | solution.py:296
  18.2 4.2 %collective-permute-start.5 = (f32[8,128]{1,0:T(8,128)S(1)}, f32[8,128]{1,0:T(8,128)S(1)}, u32[]{:S(2)}, u32[]{:S(2)}) collective-permute-start(f32[8,128]{1,0:T(8,128)S(1)} %slice_add_fusion), channel_id=1, source_target_pairs={{9,0},{8,1},{11,2},{10,3},{13,4},{12,5},{15,6},{14,7},{1,8},{0,9},... | collective-permute-start | bytes 12296 | tf_op jit(solution)/shard_map/ppermute | solution.py:296
  22.4 3.0 %collective-permute-start.6 = (f32[8,128]{1,0:T(8,128)S(1)}, f32[8,128]{1,0:T(8,128)S(1)}, u32[]{:S(2)}, u32[]{:S(2)}) collective-permute-start(f32[8,128]{1,0:T(8,128)S(1)} %add.13), channel_id=1, source_target_pairs={{5,0},{4,1},{7,2},{6,3},{1,4},{0,5},{3,6},{2,7},{13,8},{12,9},{15,... | collective-permute-start | bytes 12296 | tf_op jit(solution)/shard_map/ppermute | solution.py:296
  25.4 3.0 %collective-permute-start.7 = (f32[8,128]{1,0:T(8,128)S(1)}, f32[8,128]{1,0:T(8,128)S(1)}, u32[]{:S(2)}, u32[]{:S(2)}) collective-permute-start(f32[8,128]{1,0:T(8,128)S(1)} %add.14), channel_id=1, source_target_pairs={{3,0},{2,1},{1,2},{0,3},{7,4},{6,5},{5,6},{4,7},{11,8},{10,9},{9,1... | collective-permute-start | bytes 12296 | tf_op jit(solution)/shard_map/ppermute | solution.py:296

commit v9 on v8

--- a/solution.py
+++ b/solution.py
@@ -208,11 +208,23 @@
     def _(i):
         step(i * full, full)
 
-    for size in range(LANES, full, LANES):
+    begin, longest = steps * full, full
+    if len(listed) * half > full:
+        longest = full // 2
+        more = rest >= longest
+
+        @pl.when(more)
+        def _(begin=begin):
+            step(begin, longest)
+
+        begin = jnp.where(more, begin + longest, begin)
+        rest = jnp.where(more, rest - longest, rest)
+
+    for size in range(LANES, longest, LANES):
 
         @pl.when(rest == size)
-        def _(size=size):
-            step(steps * full, size)
+        def _(size=size, begin=begin):
+            step(begin, size)
 
     if not last:
         return

time: 29.8 us -> 30 us (level)
  waiting for transfers between devices: 5.32 us -> 6.49 us
  starting transfers between devices: 15.2 us -> 14.7 us
    ppermute x8, waiting for transfers between devices: 5.32 us -> 6.49 us  [exchanged(): return lax.ppermute(block, ('blk', 'offs'), route)]
    ppermute x8, starting transfers between devices: 15.2 us -> 14.7 us  [exchanged(): return lax.ppermute(block, ('blk', 'offs'), route)]
  transfers between devices with their start and end apart: 8 -> 8, of which waited for: 5 -> 6; matrix products, arithmetic and copies ran while one was open for 0% -> 0% of each run, Pallas kernels for 16% -> 13%
where the time goes in v9:
time: 30 us; the launch traced here: 29.6 us
  starting transfers between devices  14.7 us (49%)
  Pallas kernels  6.97 us (23%)
  waiting for transfers between devices  6.49 us (22%)
  between operations  1.38 us (5%)
    ppermute x8, starting transfers between devices, exchanged(): return lax.ppermute(block, ('blk', 'offs'), route)  14.7 us
    ppermute x8, waiting for transfers between devices, exchanged(): return lax.ppermute(block, ('blk', 'offs'), route)  6.49 us
    pallas_call x4, Pallas kernels, pairs(): call(kernel, outs, specs, (VMEM,) * len(outs), scratch, name, flops)(*args)  6.14 us
    pallas_call x1, Pallas kernels, body(): call(tail_kernel, (shape(rhs.shape, f32),) * 2, [VMEM] * 4, (VMEM, VMEM),...  0.81 us
  transfers between devices with their start and end apart: 8, of which 6 were waited for; matrix products, arithmetic and copies ran while one was open for 0% of the time, Pallas kernels for 13%

profile of v9, /device:TPU:0, one launch (start us, length us, event | category | flops | bytes accessed | tf_op | source)
XLA Modules:
  0.0 29.6 jit_solution(11126859507522465559)
XLA Ops:
  1.3 0.0 copy-done.1
  1.3 0.1 copy-done
  1.4 3.5 %collective-permute-start = (f32[8,768]{1,0:T(8,128)S(1)}, f32[8,768]{1,0:T(8,128)S(1)}, u32[]{:S(2)}, u32[]{:S(2)}) collective-permute-start(f32[8,768]{1,0:T(8,128)S(1)} %pack.1.refs_0_), channel_id=1, source_target_pairs={{9,0},{8,1},{11,2},{10,3},{13,4},{12,5},{15,6},{14,7},{1,8},{0,9},... | collective-permute-start | bytes 73736 | tf_op jit(solution)/shard_map/ppermute | solution.py:308
  5.0 1.1 %pairs_1.2 = (f32[8,768]{1,0:T(8,128)S(1)}, f32[48,1024]{1,0:T(8,128)S(1)}, bf16[32,1024]{1,0:T(8,128)(2,1)S(1)}, f32[8,128]{1,0:T(8,128)S(1)}) custom-call(f32[8,768]{1,0:T(8,128)S(1)} %pack.1.refs_0_, f32[3,1024]{1,0:T(4,128)S(1)} %copy-done.1), custom_call_target="tpu_custom_call" | custom-call | flops 67108864 | bytes 131072 | tf_op jit(solution)/shard_map/pairs_1/pallas_call | solution.py:377
  6.1 0.5 %collective-permute-done = f32[8,768]{1,0:T(8,128)S(1)} collective-permute-done((f32[8,768]{1,0:T(8,128)S(1)}, f32[8,768]{1,0:T(8,128)S(1)}, u32[]{:S(2)}, u32[]{:S(2)}) %collective-permute-start) | collective-permute-done | bytes 24608 | tf_op jit(solution)/shard_map/ppermute | solution.py:308
  6.6 1.8 %collective-permute-start.1 = (f32[8,1536]{1,0:T(8,128)S(1)}, f32[8,1536]{1,0:T(8,128)S(1)}, u32[]{:S(2)}, u32[]{:S(2)}) collective-permute-start(f32[8,1536]{1,0:T(8,128)S(1)} %constant_dynamic-update-slice_fusion.refs_0_), channel_id=1, source_target_pairs={{5,0},{4,1},{7,2},{6,3},{1,4},{0,5},{3,6},{2,7},{13,8},{12,9},{15,... | collective-permute-start | bytes 147464 | tf_op jit(solution)/shard_map/ppermute | solution.py:308
  8.4 1.6 %collective-permute-start.3 = (f32[8,1536]{1,0:T(8,128)S(1)}, f32[8,1536]{1,0:T(8,128)S(1)}, u32[]{:S(2)}, u32[]{:S(2)}) collective-permute-start(f32[8,1536]{1,0:T(8,128)S(1)} %constant_dynamic-update-slice_fusion.refs_0_), channel_id=1, source_target_pairs={{3,0},{2,1},{1,2},{0,3},{7,4},{6,5},{5,6},{4,7},{11,8},{10,9},{9,1... | collective-permute-start | bytes 147464 | tf_op jit(solution)/shard_map/ppermute | solution.py:308
  10.0 0.1 pairs_1.3.refs_3_
  10.1 0.0 copy-start.2
  10.1 0.1 collective-permute-done.1.refs_0_
  10.2 1.8 %collective-permute-start.2 = (f32[8,1536]{1,0:T(8,128)S(1)}, f32[8,1536]{1,0:T(8,128)S(1)}, u32[]{:S(2)}, u32[]{:S(2)}) collective-permute-start(f32[8,1536]{1,0:T(8,128)S(1)} %collective-permute-done.1.refs_0_), channel_id=1, source_target_pairs={{3,0},{2,1},{1,2},{0,3},{7,4},{6,5},{5,6},{4,7},{11,8},{10,9},{9,1... | collective-permute-start | bytes 147464 | tf_op jit(solution)/shard_map/ppermute | solution.py:308
  12.1 0.0 collective-permute-done.3.refs_1_
  12.1 2.6 %pairs_4.1.refs_3_ = f32[48,1024]{1,0:T(8,128)S(1)} custom-call(f32[8,1536]{1,0:T(8,128)S(1)} %collective-permute-done.1.refs_0_, f32[8,1536]{1,0:T(8,128)S(1)} %collective-permute-done.3.refs_1_, bf16[32,1024]{1,0:T(8,128)(2,1)S(1)} %get-tuple-element.15.refs_1_.refs_2_, f32[48,1024]{1,0:T(8,128)S(1)} %pairs_1.3.refs_3_), custom_call_target="tpu_custom_call" | custom-call | flops 268435456 | bytes 131072 | tf_op jit(solution)/shard_map/pairs_4/pallas_call | solution.py:377
  14.7 0.0 collective-permute-done.2.refs_0_
  14.7 2.3 %pairs_2.1 = (f32[8,1152]{1,0:T(8,128)S(1)}, f32[8,1024]{1,0:T(8,128)S(1)}) custom-call(f32[8,1536]{1,0:T(8,128)S(1)} %collective-permute-done.2.refs_0_, f32[3,1024]{1,0:T(4,128)S(1)} %copy-done.1, bf16[32,1024]{1,0:T(8,128)(2,1)S(1)} %get-tuple-element.15.refs_1_.refs_2_, f32[48,1024]{1,0:T(8,128)S(1)} %pairs_4.1.refs_3_, ...), custom_call_target="tpu_custom_call" | custom-call | flops 134217728 | bytes 131072 | tf_op jit(solution)/shard_map/pairs_2/pallas_call | solution.py:377
  17.0 0.5 %collective-permute-start.4 = (f32[8,1152]{1,0:T(8,128)S(1)}, f32[8,1152]{1,0:T(8,128)S(1)}, u32[]{:S(2)}, u32[]{:S(2)}) collective-permute-start(f32[8,1152]{1,0:T(8,128)S(1)} %get-tuple-element.20.mine), channel_id=1, source_target_pairs={{1,0},{0,1},{3,2},{2,3},{5,4},{4,5},{7,6},{6,7},{9,8},{8,9},{11,10... | collective-permute-start | bytes 110600 | tf_op jit(solution)/shard_map/ppermute | solution.py:308
  17.5 0.9 %collective-permute-done.4.other = f32[8,1152]{1,0:T(8,128)S(1)} collective-permute-done((f32[8,1152]{1,0:T(8,128)S(1)}, f32[8,1152]{1,0:T(8,128)S(1)}, u32[]{:S(2)}, u32[]{:S(2)}) %collective-permute-start.4) | collective-permute-done | bytes 36896 | tf_op jit(solution)/shard_map/ppermute | solution.py:308
  18.3 3.1 %collective-permute-start.5 = (f32[8,128]{1,0:T(8,128)S(1)}, f32[8,128]{1,0:T(8,128)S(1)}, u32[]{:S(2)}, u32[]{:S(2)}) collective-permute-start(f32[8,128]{1,0:T(8,128)S(1)} %slice_add_fusion), channel_id=1, source_target_pairs={{9,0},{8,1},{11,2},{10,3},{13,4},{12,5},{15,6},{14,7},{1,8},{0,9},... | collective-permute-start | bytes 12296 | tf_op jit(solution)/shard_map/ppermute | solution.py:308
  21.4 1.3 %collective-permute-done.5 = f32[8,128]{1,0:T(8,128)S(1)} collective-permute-done((f32[8,128]{1,0:T(8,128)S(1)}, f32[8,128]{1,0:T(8,128)S(1)}, u32[]{:S(2)}, u32[]{:S(2)}) %collective-permute-start.5) | collective-permute-done | bytes 4128 | tf_op jit(solution)/shard_map/ppermute | solution.py:308
  22.7 1.1 %collective-permute-start.6 = (f32[8,128]{1,0:T(8,128)S(1)}, f32[8,128]{1,0:T(8,128)S(1)}, u32[]{:S(2)}, u32[]{:S(2)}) collective-permute-start(f32[8,128]{1,0:T(8,128)S(1)} %add.13), channel_id=1, source_target_pairs={{5,0},{4,1},{7,2},{6,3},{1,4},{0,5},{3,6},{2,7},{13,8},{12,9},{15,... | collective-permute-start | bytes 12296 | tf_op jit(solution)/shard_map/ppermute | solution.py:308
  23.8 1.9 %collective-permute-done.6 = f32[8,128]{1,0:T(8,128)S(1)} collective-permute-done((f32[8,128]{1,0:T(8,128)S(1)}, f32[8,128]{1,0:T(8,128)S(1)}, u32[]{:S(2)}, u32[]{:S(2)}) %collective-permute-start.6) | collective-permute-done | bytes 4128 | tf_op jit(solution)/shard_map/ppermute | solution.py:308
  25.8 1.3 %collective-permute-start.7 = (f32[8,128]{1,0:T(8,128)S(1)}, f32[8,128]{1,0:T(8,128)S(1)}, u32[]{:S(2)}, u32[]{:S(2)}) collective-permute-start(f32[8,128]{1,0:T(8,128)S(1)} %add.14), channel_id=1, source_target_pairs={{3,0},{2,1},{1,2},{0,3},{7,4},{6,5},{5,6},{4,7},{11,8},{10,9},{9,1... | collective-permute-start | bytes 12296 | tf_op jit(solution)/shard_map/ppermute | solution.py:308
  27.0 1.8 %collective-permute-done.7 = f32[8,128]{1,0:T(8,128)S(1)} collective-permute-done((f32[8,128]{1,0:T(8,128)S(1)}, f32[8,128]{1,0:T(8,128)S(1)}, u32[]{:S(2)}, u32[]{:S(2)}) %collective-permute-start.7) | collective-permute-done | bytes 4128 | tf_op jit(solution)/shard_map/ppermute | solution.py:308
  28.8 0.8 %tail.1 = (f32[8,1024]{1,0:T(8,128)}, f32[8,1024]{1,0:T(8,128)}) custom-call(f32[8,128]{1,0:T(8,128)S(1)} %add.15.small, f32[8,1152]{1,0:T(8,128)S(1)} %get-tuple-element.20.mine, f32[8,1152]{1,0:T(8,128)S(1)} %collective-permute-done.4.other, f32[8,1024]{1,0:T(8,128)S(1)} %get-tuple-element.21.direction_ref), custom_call_target="tpu_custom_call" | custom-call | bytes 131072 | tf_op jit(solution)/shard_map/tail/pallas_call | solution.py:406
  (12 shorter events, 0.1 us)
Async XLA Ops:
  0.6 0.7 %copy-start.1 = (f32[3,1024]{1,0:T(4,128)S(1)}, f32[3,1024]{1,0:T(4,128)}, u32[]{:S(2)}) copy-start(f32[3,1024]{1,0:T(4,128)} %refs_1_.3) | copy-start | bytes 36868
  0.6 0.8 %copy-start = (f32[8,1024]{1,0:T(8,128)S(1)}, f32[8,1024]{1,0:T(8,128)}, u32[]{:S(2)}) copy-start(f32[8,1024]{1,0:T(8,128)} %refs_6_.1) | copy-start | bytes 98308
  1.4 5.1 %collective-permute-start = (f32[8,768]{1,0:T(8,128)S(1)}, f32[8,768]{1,0:T(8,128)S(1)}, u32[]{:S(2)}, u32[]{:S(2)}) collective-permute-start(f32[8,768]{1,0:T(8,128)S(1)} %pack.1.refs_0_), channel_id=1, source_target_pairs={{9,0},{8,1},{11,2},{10,3},{13,4},{12,5},{15,6},{14,7},{1,8},{0,9},... | collective-permute-start | bytes 73736 | tf_op jit(solution)/shard_map/ppermute | solution.py:308
  6.6 3.7 %collective-permute-start.1 = (f32[8,1536]{1,0:T(8,128)S(1)}, f32[8,1536]{1,0:T(8,128)S(1)}, u32[]{:S(2)}, u32[]{:S(2)}) collective-permute-start(f32[8,1536]{1,0:T(8,128)S(1)} %constant_dynamic-update-slice_fusion.refs_0_), channel_id=1, source_target_pairs={{5,0},{4,1},{7,2},{6,3},{1,4},{0,5},{3,6},{2,7},{13,8},{12,9},{15,... | collective-permute-start | bytes 147464 | tf_op jit(solution)/shard_map/ppermute | solution.py:308
  8.4 3.7 %collective-permute-start.3 = (f32[8,1536]{1,0:T(8,128)S(1)}, f32[8,1536]{1,0:T(8,128)S(1)}, u32[]{:S(2)}, u32[]{:S(2)}) collective-permute-start(f32[8,1536]{1,0:T(8,128)S(1)} %constant_dynamic-update-slice_fusion.refs_0_), channel_id=1, source_target_pairs={{3,0},{2,1},{1,2},{0,3},{7,4},{6,5},{5,6},{4,7},{11,8},{10,9},{9,1... | collective-permute-start | bytes 147464 | tf_op jit(solution)/shard_map/ppermute | solution.py:308
  10.1 4.6 %copy-start.2 = (f32[1024]{0:T(1024)S(1)}, f32[1024]{0:T(1024)}, u32[]{:S(2)}) copy-start(f32[1024]{0:T(1024)} %refs_5_.1) | copy-start | bytes 12292
  10.2 4.4 %collective-permute-start.2 = (f32[8,1536]{1,0:T(8,128)S(1)}, f32[8,1536]{1,0:T(8,128)S(1)}, u32[]{:S(2)}, u32[]{:S(2)}) collective-permute-start(f32[8,1536]{1,0:T(8,128)S(1)} %collective-permute-done.1.refs_0_), channel_id=1, source_target_pairs={{3,0},{2,1},{1,2},{0,3},{7,4},{6,5},{5,6},{4,7},{11,8},{10,9},{9,1... | collective-permute-start | bytes 147464 | tf_op jit(solution)/shard_map/ppermute | solution.py:308
  17.0 1.3 %collective-permute-start.4 = (f32[8,1152]{1,0:T(8,128)S(1)}, f32[8,1152]{1,0:T(8,128)S(1)}, u32[]{:S(2)}, u32[]{:S(2)}) collective-permute-start(f32[8,1152]{1,0:T(8,128)S(1)} %get-tuple-element.20.mine), channel_id=1, source_target_pairs={{1,0},{0,1},{3,2},{2,3},{5,4},{4,5},{7,6},{6,7},{9,8},{8,9},{11,10... | collective-permute-start | bytes 110600 | tf_op jit(solution)/shard_map/ppermute | solution.py:308
  18.3 4.4 %collective-permute-start.5 = (f32[8,128]{1,0:T(8,128)S(1)}, f32[8,128]{1,0:T(8,128)S(1)}, u32[]{:S(2)}, u32[]{:S(2)}) collective-permute-start(f32[8,128]{1,0:T(8,128)S(1)} %slice_add_fusion), channel_id=1, source_target_pairs={{9,0},{8,1},{11,2},{10,3},{13,4},{12,5},{15,6},{14,7},{1,8},{0,9},... | collective-permute-start | bytes 12296 | tf_op jit(solution)/shard_map/ppermute | solution.py:308
  22.7 3.0 %collective-permute-start.6 = (f32[8,128]{1,0:T(8,128)S(1)}, f32[8,128]{1,0:T(8,128)S(1)}, u32[]{:S(2)}, u32[]{:S(2)}) collective-permute-start(f32[8,128]{1,0:T(8,128)S(1)} %add.13), channel_id=1, source_target_pairs={{5,0},{4,1},{7,2},{6,3},{1,4},{0,5},{3,6},{2,7},{13,8},{12,9},{15,... | collective-permute-start | bytes 12296 | tf_op jit(solution)/shard_map/ppermute | solution.py:308
  25.8 3.0 %collective-permute-start.7 = (f32[8,128]{1,0:T(8,128)S(1)}, f32[8,128]{1,0:T(8,128)S(1)}, u32[]{:S(2)}, u32[]{:S(2)}) collective-permute-start(f32[8,128]{1,0:T(8,128)S(1)} %add.14), channel_id=1, source_target_pairs={{3,0},{2,1},{1,2},{0,3},{7,4},{6,5},{5,6},{4,7},{11,8},{10,9},{9,1... | collective-permute-start | bytes 12296 | tf_op jit(solution)/shard_map/ppermute | solution.py:308

commit v10 on v9

--- a/solution.py
+++ b/solution.py
@@ -113,34 +113,26 @@
     refs = list(refs)
     packets = [refs.pop(0) for _ in taken]
     packet = packets[0]
-    if first or last:
-        pos_hbm = refs.pop(0)
-    if not first:
-        rows_in, acc_in = refs.pop(0), refs.pop(0)
+    if first:
+        hbm = [refs.pop(0) for _ in range(4)]
+    else:
+        rows_ref, acc_in = refs.pop(0), refs.pop(0)
     if last:
-        norm = refs.pop(0)
-        noise_hbm, rhs_hbm, count_hbm = (refs.pop(0) for _ in range(3))
-        out, direction_out = refs.pop(0), refs.pop(0)
-        acc = refs.pop(0)
+        norm, lead, direction_ref, own = (refs.pop(0) for _ in range(4))
+        out, acc = refs.pop(0), refs.pop(0)
     else:
         known_out = refs.pop(0) if keep else None
         acc = refs.pop(0)
-        rows_ref = refs.pop(0) if first else rows_in
-        if first:
-            norm = refs.pop(0)
-    if last:
-        rows_ref = rows_in
+    if first:
+        rows_ref, norm, lead, direction_ref, own = (refs.pop(0) for _ in range(5))
     cols, weights = refs.pop(0), refs.pop(0)
     copies = []
-    if first or last:
-        sems, pos = refs.pop(0), refs.pop(0)
-        copies.append(pltpu.make_async_copy(pos_hbm, pos, sems.at[0]))
-    if last:
-        noise, rhs, count = (refs.pop(0) for _ in range(3))
-        copies += [
-            pltpu.make_async_copy(noise_hbm, noise, sems.at[1]),
-            pltpu.make_async_copy(rhs_hbm, rhs, sems.at[2]),
-            pltpu.make_async_copy(count_hbm, count, sems.at[3]),
+    if first:
+        sems, *held_here = refs
+        pos, noise, rhs, count = held_here
+        copies = [
+            pltpu.make_async_copy(source, target, sems.at[i])
+            for i, (source, target) in enumerate(zip(hbm, held_here))
         ]
     for copy in copies:
         copy.start()
@@ -226,25 +218,24 @@
         def _(size=size, begin=begin):
             step(begin, size)
 
-    if not last:
-        return
-    for copy in copies:
-        copy.wait()
-    lane = lax.broadcasted_iota(jnp.int32, (1, slots), 1)
-    live = (lane < count[0]).astype(f32)
-    unit = unit_of(pos[...]) * (live * scale)
-    image = jnp.zeros((width, slots), f32)
-    for k in range(3):
-        at = 2 * k * width
-        pulled = acc[at : at + width] + acc[at + width : at + 2 * width]
-        image += unit[k : k + 1] * pulled
-    direction = rhs[...] * live
-    direction_out[...] = direction
-    mine = (lax.axis_index("offs") == 0).astype(f32)
-    noise_row = noise[...].reshape(1, slots)
-    image = image + (mine * noise_row * live) * direction
-    out[:, :slots] = image
-    out[:, slots:] = norm[...] + gram(direction, image, 0)
+    if first:
+        for copy in copies[1:]:
+            copy.wait()
+        lane = lax.broadcasted_iota(jnp.int32, (1, slots), 1)
+        live = (lane < count[0]).astype(f32)
+        lead[...] = unit_of(pos[...]) * (live * scale)
+        direction = rhs[...] * live
+        direction_ref[...] = direction
+        mine = (lax.axis_index("offs") == 0).astype(f32)
+        own[...] = (mine * noise[...].reshape(1, slots) * live) * direction
+    if last:
+        image = own[...]
+        for k in range(3):
+            at = 2 * k * width
+            pulled = acc[at : at + width] + acc[at + width : at + 2 * width]
+            image += lead[k : k + 1] * pulled
+        out[:, :slots] = image
+        out[:, slots:] = norm[...] + gram(direction_ref[...], image, 0)
 
 
 def solved(small):
@@ -344,33 +335,31 @@
     acc_shape = shape((6 * width, slots), f32)
     rows_shape = shape((32, slots), bf16)
 
-    def pairs(parts, taken, rows=None, acc=None, norm=None, keep=False):
-        first, last = rows is None, norm is not None
+    def pairs(parts, taken, rows=None, acc=None, ready=(), keep=False):
+        first, last = rows is None, bool(ready)
         args, specs = list(parts), [VMEM] * len(parts)
-        if first or last:
-            args.append(position)
-            specs.append(HBM)
-        if not first:
-            args += [rows, acc]
-            specs += [VMEM] * 2
+        if first:
+            args += [position, noise_var, rhs, block_count]
+            specs += [HBM] * 4
+        else:
+            args += [rows, acc, *ready]
+            specs += [VMEM] * (2 + len(ready))
         count = sum(stop - start for start, stop in taken)
         scratch = [
             pltpu.VMEM((32, count * half), bf16),
             pltpu.VMEM((6 * width, count * half), bf16),
         ]
-        if first or last:
-            scratch += [pltpu.SemaphoreType.DMA((4,)), pos_buf]
         if last:
-            args += [norm, noise_var, rhs, block_count]
-            specs += [VMEM] + [HBM] * 3
-            outs = (shape((width, slots + LANES), f32), shape((width, slots), f32))
+            outs = (shape((width, slots + LANES), f32),)
             scratch = [pltpu.VMEM(acc_shape.shape, f32)] + scratch
-            scratch += [noise_buf, rhs_buf, count_buf]
         else:
             outs = (shape(parts[0].shape, f32),) if keep else ()
             outs += (acc_shape,)
-            if first:
-                outs += (rows_shape, shape((width, LANES), f32))
+        if first:
+            outs += (rows_shape, shape((width, LANES), f32))
+            outs += (shape(position.shape, f32),) + (shape(rhs.shape, f32),) * 2
+            scratch += [pltpu.SemaphoreType.DMA((4,))]
+            scratch += [pos_buf, noise_buf, rhs_buf, count_buf]
         kernel = functools.partial(pair_kernel, first, last, keep, taken, tiles)
         flops = 2 * slots * count * half * 64
         name = f"pairs_{count}"
@@ -383,7 +372,7 @@
         arrived = exchanged(known, distance)
         fresh = (size // 2, size)
         if rows is None:
-            known, acc, rows, norm = pairs([known], [fresh], keep=True)
+            known, acc, rows, *ready = pairs([known], [fresh], keep=True)
         else:
             known, acc = pairs([known], [fresh], rows, acc, keep=True)
         known = jnp.concatenate([known, arrived], axis=1)
@@ -394,7 +383,8 @@
     near, acc = lax.optimization_barrier((near, acc))
     rest = exchanged(near, distances[-1])
     (acc,) = pairs([near, far], [(0, size)] * 2, rows, acc)
-    mine, direction = pairs([rest], [(0, size)], rows, acc, norm)
+    (mine,) = pairs([rest], [(0, size)], rows, acc, ready)
+    direction = ready[2]
     other = exchanged(mine, 0)
     small = mine[:, slots:] + other[:, slots:]
     distance = blocks // 2

time: 30 us -> 29.5 us (0.983)
  starting transfers between devices: 14.7 us -> 14.1 us
  waiting for transfers between devices: 6.49 us -> 6.9 us
    ppermute x8, starting transfers between devices: 14.7 us -> 14.1 us  [exchanged(): return lax.ppermute(block, ('blk', 'offs'), route)]
    ppermute x8, waiting for transfers between devices: 6.49 us -> 6.9 us  [exchanged(): return lax.ppermute(block, ('blk', 'offs'), route)]
  transfers between devices with their start and end apart: 8 -> 8, of which waited for: 6 -> 6; matrix products, arithmetic and copies ran while one was open for 0% -> 0% of each run, Pallas kernels for 13% -> 14%
where the time goes in v10:
time: 29.5 us; the launch traced here: 29.3 us
  starting transfers between devices  14.1 us (48%)
  Pallas kernels  6.9 us (23%)
  waiting for transfers between devices  6.9 us (23%)
  between operations  1.37 us (5%)
    ppermute x8, starting transfers between devices, exchanged(): return lax.ppermute(block, ('blk', 'offs'), route)  14.1 us
    ppermute x8, waiting for transfers between devices, exchanged(): return lax.ppermute(block, ('blk', 'offs'), route)  6.9 us
    pallas_call x4, Pallas kernels, pairs(): call(kernel, outs, specs, (VMEM,) * len(outs), scratch, name, flops)(*args)  6.06 us
    pallas_call x1, Pallas kernels, body(): call(tail_kernel, (shape(rhs.shape, f32),) * 2, [VMEM] * 4, (VMEM, VMEM),...  0.81 us
  transfers between devices with their start and end apart: 8, of which 6 were waited for; matrix products, arithmetic and copies ran while one was open for 0% of the time, Pallas kernels for 14%

profile of v10, /device:TPU:0, one launch (start us, length us, event | category | flops | bytes accessed | tf_op | source)
XLA Modules:
  0.0 29.3 jit_solution(17017279996573949435)
XLA Ops:
  0.6 0.0 copy-start
  0.6 0.0 copy-start.1
  1.3 0.1 copy-done
  1.4 3.5 %collective-permute-start = (f32[8,768]{1,0:T(8,128)S(1)}, f32[8,768]{1,0:T(8,128)S(1)}, u32[]{:S(2)}, u32[]{:S(2)}) collective-permute-start(f32[8,768]{1,0:T(8,128)S(1)} %pack.1.refs_0_), channel_id=1, source_target_pairs={{9,0},{8,1},{11,2},{10,3},{13,4},{12,5},{15,6},{14,7},{1,8},{0,9},... | collective-permute-start | bytes 73736 | tf_op jit(solution)/shard_map/ppermute | solution.py:299
  5.0 1.0 %pairs_1.2 = (f32[8,768]{1,0:T(8,128)S(1)}, f32[48,1024]{1,0:T(8,128)S(1)}, bf16[32,1024]{1,0:T(8,128)(2,1)S(1)}, f32[8,128]{1,0:T(8,128)S(1)}, f32[3,1024]{1,0:...) custom-call(f32[8,768]{1,0:T(8,128)S(1)} %pack.1.refs_0_, f32[3,1024]{1,0:T(4,128)S(1)} %copy-done.1, ...), custom_call_target="tpu_custom_call" | custom-call | flops 67108864 | bytes 131072 | tf_op jit(solution)/shard_map/pairs_1/pallas_call | solution.py:366
  6.0 0.6 %collective-permute-done = f32[8,768]{1,0:T(8,128)S(1)} collective-permute-done((f32[8,768]{1,0:T(8,128)S(1)}, f32[8,768]{1,0:T(8,128)S(1)}, u32[]{:S(2)}, u32[]{:S(2)}) %collective-permute-start) | collective-permute-done | bytes 24608 | tf_op jit(solution)/shard_map/ppermute | solution.py:299
  6.6 1.8 %collective-permute-start.1 = (f32[8,1536]{1,0:T(8,128)S(1)}, f32[8,1536]{1,0:T(8,128)S(1)}, u32[]{:S(2)}, u32[]{:S(2)}) collective-permute-start(f32[8,1536]{1,0:T(8,128)S(1)} %constant_dynamic-update-slice_fusion.refs_0_), channel_id=1, source_target_pairs={{5,0},{4,1},{7,2},{6,3},{1,4},{0,5},{3,6},{2,7},{13,8},{12,9},{15,... | collective-permute-start | bytes 147464 | tf_op jit(solution)/shard_map/ppermute | solution.py:299
  8.4 1.6 %collective-permute-start.3 = (f32[8,1536]{1,0:T(8,128)S(1)}, f32[8,1536]{1,0:T(8,128)S(1)}, u32[]{:S(2)}, u32[]{:S(2)}) collective-permute-start(f32[8,1536]{1,0:T(8,128)S(1)} %constant_dynamic-update-slice_fusion.refs_0_), channel_id=1, source_target_pairs={{3,0},{2,1},{1,2},{0,3},{7,4},{6,5},{5,6},{4,7},{11,8},{10,9},{9,1... | collective-permute-start | bytes 147464 | tf_op jit(solution)/shard_map/ppermute | solution.py:299
  10.0 1.1 %pairs_1.3.refs_3_ = f32[48,1024]{1,0:T(8,128)S(1)} custom-call(f32[8,1536]{1,0:T(8,128)S(1)} %constant_dynamic-update-slice_fusion.refs_0_, bf16[32,1024]{1,0:T(8,128)(2,1)S(1)} %get-tuple-element.16.refs_1_.refs_2_, f32[48,1024]{1,0:T(8,128)S(1)} %get-tuple-element.17.refs_2_), custom_call_target="tpu_custom_call" | custom-call | flops 67108864 | bytes 131072 | tf_op jit(solution)/shard_map/pairs_1/pallas_call | solution.py:366
  11.1 0.0 collective-permute-done.1.refs_0_
  11.1 1.0 %collective-permute-start.2 = (f32[8,1536]{1,0:T(8,128)S(1)}, f32[8,1536]{1,0:T(8,128)S(1)}, u32[]{:S(2)}, u32[]{:S(2)}) collective-permute-start(f32[8,1536]{1,0:T(8,128)S(1)} %collective-permute-done.1.refs_0_), channel_id=1, source_target_pairs={{3,0},{2,1},{1,2},{0,3},{7,4},{6,5},{5,6},{4,7},{11,8},{10,9},{9,1... | collective-permute-start | bytes 147464 | tf_op jit(solution)/shard_map/ppermute | solution.py:299
  12.1 0.0 collective-permute-done.3.refs_1_
  12.1 1.9 %pairs_4.1.refs_2_ = f32[48,1024]{1,0:T(8,128)S(1)} custom-call(f32[8,1536]{1,0:T(8,128)S(1)} %collective-permute-done.1.refs_0_, f32[8,1536]{1,0:T(8,128)S(1)} %collective-permute-done.3.refs_1_, bf16[32,1024]{1,0:T(8,128)(2,1)S(1)} %get-tuple-element.16.refs_1_.refs_2_, f32[48,1024]{1,0:T(8,128)S(1)} %pairs_1.3.refs_3_), custom_call_target="tpu_custom_call" | custom-call | flops 268435456 | bytes 131072 | tf_op jit(solution)/shard_map/pairs_4/pallas_call | solution.py:366
  14.0 0.9 %collective-permute-done.2.refs_0_ = f32[8,1536]{1,0:T(8,128)S(1)} collective-permute-done((f32[8,1536]{1,0:T(8,128)S(1)}, f32[8,1536]{1,0:T(8,128)S(1)}, u32[]{:S(2)}, u32[]{:S(2)}) %collective-permute-start.2) | collective-permute-done | bytes 49184 | tf_op jit(solution)/shard_map/ppermute | solution.py:299
  14.9 2.0 %pairs_2.1.mine = f32[8,1152]{1,0:T(8,128)S(1)} custom-call(f32[8,1536]{1,0:T(8,128)S(1)} %collective-permute-done.2.refs_0_, bf16[32,1024]{1,0:T(8,128)(2,1)S(1)} %get-tuple-element.16.refs_1_.refs_2_, f32[48,1024]{1,0:T(8,128)S(1)} %pairs_4.1.refs_2_, f32[8,128]{1,0:T(8,128)S(1)} %get-tuple-element.20.refs_3_, f32[3,1024]{1,0:T(4,128)S(1)} %get-tuple-element.21.refs_4_, ...), custom_call_target="tpu_custom_call" | custom-call | flops 134217728 | bytes 131072 | tf_op jit(solution)/shard_map/pairs_2/pallas_call | solution.py:366
  17.0 0.2 collective-permute-start.4
  17.1 1.1 %collective-permute-done.4.other = f32[8,1152]{1,0:T(8,128)S(1)} collective-permute-done((f32[8,1152]{1,0:T(8,128)S(1)}, f32[8,1152]{1,0:T(8,128)S(1)}, u32[]{:S(2)}, u32[]{:S(2)}) %collective-permute-start.4) | collective-permute-done | bytes 36896 | tf_op jit(solution)/shard_map/ppermute | solution.py:299
  18.2 2.6 %collective-permute-start.5 = (f32[8,128]{1,0:T(8,128)S(1)}, f32[8,128]{1,0:T(8,128)S(1)}, u32[]{:S(2)}, u32[]{:S(2)}) collective-permute-start(f32[8,128]{1,0:T(8,128)S(1)} %slice_add_fusion), channel_id=1, source_target_pairs={{9,0},{8,1},{11,2},{10,3},{13,4},{12,5},{15,6},{14,7},{1,8},{0,9},... | collective-permute-start | bytes 12296 | tf_op jit(solution)/shard_map/ppermute | solution.py:299
  20.8 1.4 %collective-permute-done.5 = f32[8,128]{1,0:T(8,128)S(1)} collective-permute-done((f32[8,128]{1,0:T(8,128)S(1)}, f32[8,128]{1,0:T(8,128)S(1)}, u32[]{:S(2)}, u32[]{:S(2)}) %collective-permute-start.5) | collective-permute-done | bytes 4128 | tf_op jit(solution)/shard_map/ppermute | solution.py:299
  22.2 2.0 %collective-permute-start.6 = (f32[8,128]{1,0:T(8,128)S(1)}, f32[8,128]{1,0:T(8,128)S(1)}, u32[]{:S(2)}, u32[]{:S(2)}) collective-permute-start(f32[8,128]{1,0:T(8,128)S(1)} %add.13), channel_id=1, source_target_pairs={{5,0},{4,1},{7,2},{6,3},{1,4},{0,5},{3,6},{2,7},{13,8},{12,9},{15,... | collective-permute-start | bytes 12296 | tf_op jit(solution)/shard_map/ppermute | solution.py:299
  24.1 1.3 %collective-permute-done.6 = f32[8,128]{1,0:T(8,128)S(1)} collective-permute-done((f32[8,128]{1,0:T(8,128)S(1)}, f32[8,128]{1,0:T(8,128)S(1)}, u32[]{:S(2)}, u32[]{:S(2)}) %collective-permute-start.6) | collective-permute-done | bytes 4128 | tf_op jit(solution)/shard_map/ppermute | solution.py:299
  25.5 1.4 %collective-permute-start.7 = (f32[8,128]{1,0:T(8,128)S(1)}, f32[8,128]{1,0:T(8,128)S(1)}, u32[]{:S(2)}, u32[]{:S(2)}) collective-permute-start(f32[8,128]{1,0:T(8,128)S(1)} %add.14), channel_id=1, source_target_pairs={{3,0},{2,1},{1,2},{0,3},{7,4},{6,5},{5,6},{4,7},{11,8},{10,9},{9,1... | collective-permute-start | bytes 12296 | tf_op jit(solution)/shard_map/ppermute | solution.py:299
  26.9 1.6 %collective-permute-done.7 = f32[8,128]{1,0:T(8,128)S(1)} collective-permute-done((f32[8,128]{1,0:T(8,128)S(1)}, f32[8,128]{1,0:T(8,128)S(1)}, u32[]{:S(2)}, u32[]{:S(2)}) %collective-permute-start.7) | collective-permute-done | bytes 4128 | tf_op jit(solution)/shard_map/ppermute | solution.py:299
  28.5 0.8 %tail.1 = (f32[8,1024]{1,0:T(8,128)}, f32[8,1024]{1,0:T(8,128)}) custom-call(f32[8,128]{1,0:T(8,128)S(1)} %add.15.small, f32[8,1152]{1,0:T(8,128)S(1)} %pairs_2.1.mine, f32[8,1152]{1,0:T(8,128)S(1)} %collective-permute-done.4.other, f32[8,1024]{1,0:T(8,128)S(1)} %get-tuple-element.22.refs_5_.direction_ref), custom_call_target="tpu_custom_call" | custom-call | bytes 131072 | tf_op jit(solution)/shard_map/tail/pallas_call | solution.py:396
  (12 shorter events, 0.1 us)
Async XLA Ops:
  0.6 0.8 %copy-start = (f32[8,1024]{1,0:T(8,128)S(1)}, f32[8,1024]{1,0:T(8,128)}, u32[]{:S(2)}) copy-start(f32[8,1024]{1,0:T(8,128)} %refs_3_.1) | copy-start | bytes 98308
  0.6 0.8 %copy-start.1 = (f32[3,1024]{1,0:T(4,128)S(1)}, f32[3,1024]{1,0:T(4,128)}, u32[]{:S(2)}) copy-start(f32[3,1024]{1,0:T(4,128)} %refs_1_.1) | copy-start | bytes 36868
  1.4 3.6 %copy-start.2 = (f32[1024]{0:T(1024)S(1)}, f32[1024]{0:T(1024)}, u32[]{:S(2)}) copy-start(f32[1024]{0:T(1024)} %refs_2_.1) | copy-start | bytes 12292
  1.4 5.1 %collective-permute-start = (f32[8,768]{1,0:T(8,128)S(1)}, f32[8,768]{1,0:T(8,128)S(1)}, u32[]{:S(2)}, u32[]{:S(2)}) collective-permute-start(f32[8,768]{1,0:T(8,128)S(1)} %pack.1.refs_0_), channel_id=1, source_target_pairs={{9,0},{8,1},{11,2},{10,3},{13,4},{12,5},{15,6},{14,7},{1,8},{0,9},... | collective-permute-start | bytes 73736 | tf_op jit(solution)/shard_map/ppermute | solution.py:299
  6.6 4.5 %collective-permute-start.1 = (f32[8,1536]{1,0:T(8,128)S(1)}, f32[8,1536]{1,0:T(8,128)S(1)}, u32[]{:S(2)}, u32[]{:S(2)}) collective-permute-start(f32[8,1536]{1,0:T(8,128)S(1)} %constant_dynamic-update-slice_fusion.refs_0_), channel_id=1, source_target_pairs={{5,0},{4,1},{7,2},{6,3},{1,4},{0,5},{3,6},{2,7},{13,8},{12,9},{15,... | collective-permute-start | bytes 147464 | tf_op jit(solution)/shard_map/ppermute | solution.py:299
  8.4 3.7 %collective-permute-start.3 = (f32[8,1536]{1,0:T(8,128)S(1)}, f32[8,1536]{1,0:T(8,128)S(1)}, u32[]{:S(2)}, u32[]{:S(2)}) collective-permute-start(f32[8,1536]{1,0:T(8,128)S(1)} %constant_dynamic-update-slice_fusion.refs_0_), channel_id=1, source_target_pairs={{3,0},{2,1},{1,2},{0,3},{7,4},{6,5},{5,6},{4,7},{11,8},{10,9},{9,1... | collective-permute-start | bytes 147464 | tf_op jit(solution)/shard_map/ppermute | solution.py:299
  11.1 3.8 %collective-permute-start.2 = (f32[8,1536]{1,0:T(8,128)S(1)}, f32[8,1536]{1,0:T(8,128)S(1)}, u32[]{:S(2)}, u32[]{:S(2)}) collective-permute-start(f32[8,1536]{1,0:T(8,128)S(1)} %collective-permute-done.1.refs_0_), channel_id=1, source_target_pairs={{3,0},{2,1},{1,2},{0,3},{7,4},{6,5},{5,6},{4,7},{11,8},{10,9},{9,1... | collective-permute-start | bytes 147464 | tf_op jit(solution)/shard_map/ppermute | solution.py:299
  17.0 1.3 %collective-permute-start.4 = (f32[8,1152]{1,0:T(8,128)S(1)}, f32[8,1152]{1,0:T(8,128)S(1)}, u32[]{:S(2)}, u32[]{:S(2)}) collective-permute-start(f32[8,1152]{1,0:T(8,128)S(1)} %pairs_2.1.mine), channel_id=1, source_target_pairs={{1,0},{0,1},{3,2},{2,3},{5,4},{4,5},{7,6},{6,7},{9,8},{8,9},{11,10... | collective-permute-start | bytes 110600 | tf_op jit(solution)/shard_map/ppermute | solution.py:299
  18.2 3.9 %collective-permute-start.5 = (f32[8,128]{1,0:T(8,128)S(1)}, f32[8,128]{1,0:T(8,128)S(1)}, u32[]{:S(2)}, u32[]{:S(2)}) collective-permute-start(f32[8,128]{1,0:T(8,128)S(1)} %slice_add_fusion), channel_id=1, source_target_pairs={{9,0},{8,1},{11,2},{10,3},{13,4},{12,5},{15,6},{14,7},{1,8},{0,9},... | collective-permute-start | bytes 12296 | tf_op jit(solution)/shard_map/ppermute | solution.py:299
  22.2 3.3 %collective-permute-start.6 = (f32[8,128]{1,0:T(8,128)S(1)}, f32[8,128]{1,0:T(8,128)S(1)}, u32[]{:S(2)}, u32[]{:S(2)}) collective-permute-start(f32[8,128]{1,0:T(8,128)S(1)} %add.13), channel_id=1, source_target_pairs={{5,0},{4,1},{7,2},{6,3},{1,4},{0,5},{3,6},{2,7},{13,8},{12,9},{15,... | collective-permute-start | bytes 12296 | tf_op jit(solution)/shard_map/ppermute | solution.py:299
  25.5 3.0 %collective-permute-start.7 = (f32[8,128]{1,0:T(8,128)S(1)}, f32[8,128]{1,0:T(8,128)S(1)}, u32[]{:S(2)}, u32[]{:S(2)}) collective-permute-start(f32[8,128]{1,0:T(8,128)S(1)} %add.14), channel_id=1, source_target_pairs={{3,0},{2,1},{1,2},{0,3},{7,4},{6,5},{5,6},{4,7},{11,8},{10,9},{9,1... | collective-permute-start | bytes 12296 | tf_op jit(solution)/shard_map/ppermute | solution.py:299

commit v11 on v10

--- a/solution.py
+++ b/solution.py
@@ -192,7 +192,8 @@
             part = acc[:, near] + jnp.dot(w, top, preferred_element_type=f32)
             acc[:, near] = part + jnp.dot(w, low, preferred_element_type=f32)
 
-    full = min(STEP, len(listed) * half)
+    most = len(listed) * half
+    full = STEP * 3 // 4 if most == STEP else min(STEP, most)
     steps = filled // full
     rest = filled - steps * full
 
@@ -201,7 +202,7 @@
         step(i * full, full)
 
     begin, longest = steps * full, full
-    if len(listed) * half > full:
+    if most > STEP:
         longest = full // 2
         more = rest >= longest
 

time: 29.5 us -> 29.5 us (level)
  starting transfers between devices: 14.1 us -> 12.8 us
  Pallas kernels: 6.9 us -> 7.67 us
  waiting for transfers between devices: 6.9 us -> 7.6 us
    ppermute x8, starting transfers between devices: 14.1 us -> 12.8 us  [exchanged(): return lax.ppermute(block, ('blk', 'offs'), route)]
    pallas_call x4, Pallas kernels: 6.06 us -> 6.83 us  [pairs(): call(kernel, outs, specs, (VMEM,) * len(outs), scratch, name, flops)(*args)]
    ppermute x8, waiting for transfers between devices: 6.9 us -> 7.6 us  [exchanged(): return lax.ppermute(block, ('blk', 'offs'), route)]
  transfers between devices with their start and end apart: 8 -> 8, of which waited for: 6 -> 5; matrix products, arithmetic and copies ran while one was open for 0% -> 0% of each run, Pallas kernels for 14% -> 18%
where the time goes in v11:
time: 29.5 us; the launch traced here: 29.6 us
  starting transfers between devices  12.8 us (43%)
  Pallas kernels  7.67 us (26%)
  waiting for transfers between devices  7.6 us (26%)
  between operations  1.38 us (5%)
    ppermute x8, starting transfers between devices, exchanged(): return lax.ppermute(block, ('blk', 'offs'), route)  12.8 us
    ppermute x8, waiting for transfers between devices, exchanged(): return lax.ppermute(block, ('blk', 'offs'), route)  7.6 us
    pallas_call x4, Pallas kernels, pairs(): call(kernel, outs, specs, (VMEM,) * len(outs), scratch, name, flops)(*args)  6.83 us
    pallas_call x1, Pallas kernels, body(): call(tail_kernel, (shape(rhs.shape, f32),) * 2, [VMEM] * 4, (VMEM, VMEM),...  0.81 us
  transfers between devices with their start and end apart: 8, of which 5 were waited for; matrix products, arithmetic and copies ran while one was open for 0% of the time, Pallas kernels for 18%

profile of v11, /device:TPU:0, one launch (start us, length us, event | category | flops | bytes accessed | tf_op | source)
XLA Modules:
  0.0 29.6 jit_solution(4596149763038160098)
XLA Ops:
  0.6 0.0 copy-start
  0.6 0.0 copy-start.1
  1.3 0.1 copy-done
  1.4 3.5 %collective-permute-start = (f32[8,768]{1,0:T(8,128)S(1)}, f32[8,768]{1,0:T(8,128)S(1)}, u32[]{:S(2)}, u32[]{:S(2)}) collective-permute-start(f32[8,768]{1,0:T(8,128)S(1)} %pack.1.refs_0_), channel_id=1, source_target_pairs={{9,0},{8,1},{11,2},{10,3},{13,4},{12,5},{15,6},{14,7},{1,8},{0,9},... | collective-permute-start | bytes 73736 | tf_op jit(solution)/shard_map/ppermute | solution.py:300
  5.0 0.8 %pairs_1.2 = (f32[8,768]{1,0:T(8,128)S(1)}, f32[48,1024]{1,0:T(8,128)S(1)}, bf16[32,1024]{1,0:T(8,128)(2,1)S(1)}, f32[8,128]{1,0:T(8,128)S(1)}, f32[3,1024]{1,0:...) custom-call(f32[8,768]{1,0:T(8,128)S(1)} %pack.1.refs_0_, f32[3,1024]{1,0:T(4,128)S(1)} %copy-done.1, ...), custom_call_target="tpu_custom_call" | custom-call | flops 67108864 | bytes 131072 | tf_op jit(solution)/shard_map/pairs_1/pallas_call | solution.py:367
  5.8 0.7 %collective-permute-done = f32[8,768]{1,0:T(8,128)S(1)} collective-permute-done((f32[8,768]{1,0:T(8,128)S(1)}, f32[8,768]{1,0:T(8,128)S(1)}, u32[]{:S(2)}, u32[]{:S(2)}) %collective-permute-start) | collective-permute-done | bytes 24608 | tf_op jit(solution)/shard_map/ppermute | solution.py:300
  6.6 1.8 %collective-permute-start.1 = (f32[8,1536]{1,0:T(8,128)S(1)}, f32[8,1536]{1,0:T(8,128)S(1)}, u32[]{:S(2)}, u32[]{:S(2)}) collective-permute-start(f32[8,1536]{1,0:T(8,128)S(1)} %constant_dynamic-update-slice_fusion.refs_0_), channel_id=1, source_target_pairs={{5,0},{4,1},{7,2},{6,3},{1,4},{0,5},{3,6},{2,7},{13,8},{12,9},{15,... | collective-permute-start | bytes 147464 | tf_op jit(solution)/shard_map/ppermute | solution.py:300
  8.4 1.6 %collective-permute-start.3 = (f32[8,1536]{1,0:T(8,128)S(1)}, f32[8,1536]{1,0:T(8,128)S(1)}, u32[]{:S(2)}, u32[]{:S(2)}) collective-permute-start(f32[8,1536]{1,0:T(8,128)S(1)} %constant_dynamic-update-slice_fusion.refs_0_), channel_id=1, source_target_pairs={{3,0},{2,1},{1,2},{0,3},{7,4},{6,5},{5,6},{4,7},{11,8},{10,9},{9,1... | collective-permute-start | bytes 147464 | tf_op jit(solution)/shard_map/ppermute | solution.py:300
  10.0 1.1 %pairs_1.3.refs_3_ = f32[48,1024]{1,0:T(8,128)S(1)} custom-call(f32[8,1536]{1,0:T(8,128)S(1)} %constant_dynamic-update-slice_fusion.refs_0_, bf16[32,1024]{1,0:T(8,128)(2,1)S(1)} %get-tuple-element.16.refs_1_.refs_2_, f32[48,1024]{1,0:T(8,128)S(1)} %get-tuple-element.17.refs_2_), custom_call_target="tpu_custom_call" | custom-call | flops 67108864 | bytes 131072 | tf_op jit(solution)/shard_map/pairs_1/pallas_call | solution.py:367
  11.1 0.0 collective-permute-done.1.refs_0_
  11.1 1.0 %collective-permute-start.2 = (f32[8,1536]{1,0:T(8,128)S(1)}, f32[8,1536]{1,0:T(8,128)S(1)}, u32[]{:S(2)}, u32[]{:S(2)}) collective-permute-start(f32[8,1536]{1,0:T(8,128)S(1)} %collective-permute-done.1.refs_0_), channel_id=1, source_target_pairs={{3,0},{2,1},{1,2},{0,3},{7,4},{6,5},{5,6},{4,7},{11,8},{10,9},{9,1... | collective-permute-start | bytes 147464 | tf_op jit(solution)/shard_map/ppermute | solution.py:300
  12.1 0.0 collective-permute-done.3.refs_1_
  12.1 3.4 %pairs_4.1.refs_2_ = f32[48,1024]{1,0:T(8,128)S(1)} custom-call(f32[8,1536]{1,0:T(8,128)S(1)} %collective-permute-done.1.refs_0_, f32[8,1536]{1,0:T(8,128)S(1)} %collective-permute-done.3.refs_1_, bf16[32,1024]{1,0:T(8,128)(2,1)S(1)} %get-tuple-element.16.refs_1_.refs_2_, f32[48,1024]{1,0:T(8,128)S(1)} %pairs_1.3.refs_3_), custom_call_target="tpu_custom_call" | custom-call | flops 268435456 | bytes 131072 | tf_op jit(solution)/shard_map/pairs_4/pallas_call | solution.py:367
  15.5 0.0 collective-permute-done.2.refs_0_
  15.5 1.5 %pairs_2.1.mine = f32[8,1152]{1,0:T(8,128)S(1)} custom-call(f32[8,1536]{1,0:T(8,128)S(1)} %collective-permute-done.2.refs_0_, bf16[32,1024]{1,0:T(8,128)(2,1)S(1)} %get-tuple-element.16.refs_1_.refs_2_, f32[48,1024]{1,0:T(8,128)S(1)} %pairs_4.1.refs_2_, f32[8,128]{1,0:T(8,128)S(1)} %get-tuple-element.20.refs_3_, f32[3,1024]{1,0:T(4,128)S(1)} %get-tuple-element.21.refs_4_, ...), custom_call_target="tpu_custom_call" | custom-call | flops 134217728 | bytes 131072 | tf_op jit(solution)/shard_map/pairs_2/pallas_call | solution.py:367
  17.0 0.1 collective-permute-start.4
  17.1 1.2 %collective-permute-done.4.other = f32[8,1152]{1,0:T(8,128)S(1)} collective-permute-done((f32[8,1152]{1,0:T(8,128)S(1)}, f32[8,1152]{1,0:T(8,128)S(1)}, u32[]{:S(2)}, u32[]{:S(2)}) %collective-permute-start.4) | collective-permute-done | bytes 36896 | tf_op jit(solution)/shard_map/ppermute | solution.py:300
  18.3 3.1 %collective-permute-start.5 = (f32[8,128]{1,0:T(8,128)S(1)}, f32[8,128]{1,0:T(8,128)S(1)}, u32[]{:S(2)}, u32[]{:S(2)}) collective-permute-start(f32[8,128]{1,0:T(8,128)S(1)} %slice_add_fusion), channel_id=1, source_target_pairs={{9,0},{8,1},{11,2},{10,3},{13,4},{12,5},{15,6},{14,7},{1,8},{0,9},... | collective-permute-start | bytes 12296 | tf_op jit(solution)/shard_map/ppermute | solution.py:300
  21.4 1.3 %collective-permute-done.5 = f32[8,128]{1,0:T(8,128)S(1)} collective-permute-done((f32[8,128]{1,0:T(8,128)S(1)}, f32[8,128]{1,0:T(8,128)S(1)}, u32[]{:S(2)}, u32[]{:S(2)}) %collective-permute-start.5) | collective-permute-done | bytes 4128 | tf_op jit(solution)/shard_map/ppermute | solution.py:300
  22.7 0.6 %collective-permute-start.6 = (f32[8,128]{1,0:T(8,128)S(1)}, f32[8,128]{1,0:T(8,128)S(1)}, u32[]{:S(2)}, u32[]{:S(2)}) collective-permute-start(f32[8,128]{1,0:T(8,128)S(1)} %add.13), channel_id=1, source_target_pairs={{5,0},{4,1},{7,2},{6,3},{1,4},{0,5},{3,6},{2,7},{13,8},{12,9},{15,... | collective-permute-start | bytes 12296 | tf_op jit(solution)/shard_map/ppermute | solution.py:300
  23.3 2.4 %collective-permute-done.6 = f32[8,128]{1,0:T(8,128)S(1)} collective-permute-done((f32[8,128]{1,0:T(8,128)S(1)}, f32[8,128]{1,0:T(8,128)S(1)}, u32[]{:S(2)}, u32[]{:S(2)}) %collective-permute-start.6) | collective-permute-done | bytes 4128 | tf_op jit(solution)/shard_map/ppermute | solution.py:300
  25.7 1.2 %collective-permute-start.7 = (f32[8,128]{1,0:T(8,128)S(1)}, f32[8,128]{1,0:T(8,128)S(1)}, u32[]{:S(2)}, u32[]{:S(2)}) collective-permute-start(f32[8,128]{1,0:T(8,128)S(1)} %add.14), channel_id=1, source_target_pairs={{3,0},{2,1},{1,2},{0,3},{7,4},{6,5},{5,6},{4,7},{11,8},{10,9},{9,1... | collective-permute-start | bytes 12296 | tf_op jit(solution)/shard_map/ppermute | solution.py:300
  26.9 1.9 %collective-permute-done.7 = f32[8,128]{1,0:T(8,128)S(1)} collective-permute-done((f32[8,128]{1,0:T(8,128)S(1)}, f32[8,128]{1,0:T(8,128)S(1)}, u32[]{:S(2)}, u32[]{:S(2)}) %collective-permute-start.7) | collective-permute-done | bytes 4128 | tf_op jit(solution)/shard_map/ppermute | solution.py:300
  28.8 0.8 %tail.1 = (f32[8,1024]{1,0:T(8,128)}, f32[8,1024]{1,0:T(8,128)}) custom-call(f32[8,128]{1,0:T(8,128)S(1)} %add.15.small, f32[8,1152]{1,0:T(8,128)S(1)} %pairs_2.1.mine, f32[8,1152]{1,0:T(8,128)S(1)} %collective-permute-done.4.other, f32[8,1024]{1,0:T(8,128)S(1)} %get-tuple-element.22.refs_5_.direction_ref), custom_call_target="tpu_custom_call" | custom-call | bytes 131072 | tf_op jit(solution)/shard_map/tail/pallas_call | solution.py:397
  (12 shorter events, 0.1 us)
Async XLA Ops:
  0.6 0.8 %copy-start = (f32[8,1024]{1,0:T(8,128)S(1)}, f32[8,1024]{1,0:T(8,128)}, u32[]{:S(2)}) copy-start(f32[8,1024]{1,0:T(8,128)} %refs_3_.1) | copy-start | bytes 98308
  0.6 0.8 %copy-start.1 = (f32[3,1024]{1,0:T(4,128)S(1)}, f32[3,1024]{1,0:T(4,128)}, u32[]{:S(2)}) copy-start(f32[3,1024]{1,0:T(4,128)} %refs_1_.1) | copy-start | bytes 36868
  1.4 3.6 %copy-start.2 = (f32[1024]{0:T(1024)S(1)}, f32[1024]{0:T(1024)}, u32[]{:S(2)}) copy-start(f32[1024]{0:T(1024)} %refs_2_.1) | copy-start | bytes 12292
  1.4 5.1 %collective-permute-start = (f32[8,768]{1,0:T(8,128)S(1)}, f32[8,768]{1,0:T(8,128)S(1)}, u32[]{:S(2)}, u32[]{:S(2)}) collective-permute-start(f32[8,768]{1,0:T(8,128)S(1)} %pack.1.refs_0_), channel_id=1, source_target_pairs={{9,0},{8,1},{11,2},{10,3},{13,4},{12,5},{15,6},{14,7},{1,8},{0,9},... | collective-permute-start | bytes 73736 | tf_op jit(solution)/shard_map/ppermute | solution.py:300
  6.6 4.5 %collective-permute-start.1 = (f32[8,1536]{1,0:T(8,128)S(1)}, f32[8,1536]{1,0:T(8,128)S(1)}, u32[]{:S(2)}, u32[]{:S(2)}) collective-permute-start(f32[8,1536]{1,0:T(8,128)S(1)} %constant_dynamic-update-slice_fusion.refs_0_), channel_id=1, source_target_pairs={{5,0},{4,1},{7,2},{6,3},{1,4},{0,5},{3,6},{2,7},{13,8},{12,9},{15,... | collective-permute-start | bytes 147464 | tf_op jit(solution)/shard_map/ppermute | solution.py:300
  8.4 3.7 %collective-permute-start.3 = (f32[8,1536]{1,0:T(8,128)S(1)}, f32[8,1536]{1,0:T(8,128)S(1)}, u32[]{:S(2)}, u32[]{:S(2)}) collective-permute-start(f32[8,1536]{1,0:T(8,128)S(1)} %constant_dynamic-update-slice_fusion.refs_0_), channel_id=1, source_target_pairs={{3,0},{2,1},{1,2},{0,3},{7,4},{6,5},{5,6},{4,7},{11,8},{10,9},{9,1... | collective-permute-start | bytes 147464 | tf_op jit(solution)/shard_map/ppermute | solution.py:300
  11.1 4.4 %collective-permute-start.2 = (f32[8,1536]{1,0:T(8,128)S(1)}, f32[8,1536]{1,0:T(8,128)S(1)}, u32[]{:S(2)}, u32[]{:S(2)}) collective-permute-start(f32[8,1536]{1,0:T(8,128)S(1)} %collective-permute-done.1.refs_0_), channel_id=1, source_target_pairs={{3,0},{2,1},{1,2},{0,3},{7,4},{6,5},{5,6},{4,7},{11,8},{10,9},{9,1... | collective-permute-start | bytes 147464 | tf_op jit(solution)/shard_map/ppermute | solution.py:300
  17.0 1.3 %collective-permute-start.4 = (f32[8,1152]{1,0:T(8,128)S(1)}, f32[8,1152]{1,0:T(8,128)S(1)}, u32[]{:S(2)}, u32[]{:S(2)}) collective-permute-start(f32[8,1152]{1,0:T(8,128)S(1)} %pairs_2.1.mine), channel_id=1, source_target_pairs={{1,0},{0,1},{3,2},{2,3},{5,4},{4,5},{7,6},{6,7},{9,8},{8,9},{11,10... | collective-permute-start | bytes 110600 | tf_op jit(solution)/shard_map/ppermute | solution.py:300
  18.3 4.4 %collective-permute-start.5 = (f32[8,128]{1,0:T(8,128)S(1)}, f32[8,128]{1,0:T(8,128)S(1)}, u32[]{:S(2)}, u32[]{:S(2)}) collective-permute-start(f32[8,128]{1,0:T(8,128)S(1)} %slice_add_fusion), channel_id=1, source_target_pairs={{9,0},{8,1},{11,2},{10,3},{13,4},{12,5},{15,6},{14,7},{1,8},{0,9},... | collective-permute-start | bytes 12296 | tf_op jit(solution)/shard_map/ppermute | solution.py:300
  22.7 3.0 %collective-permute-start.6 = (f32[8,128]{1,0:T(8,128)S(1)}, f32[8,128]{1,0:T(8,128)S(1)}, u32[]{:S(2)}, u32[]{:S(2)}) collective-permute-start(f32[8,128]{1,0:T(8,128)S(1)} %add.13), channel_id=1, source_target_pairs={{5,0},{4,1},{7,2},{6,3},{1,4},{0,5},{3,6},{2,7},{13,8},{12,9},{15,... | collective-permute-start | bytes 12296 | tf_op jit(solution)/shard_map/ppermute | solution.py:300
  25.7 3.0 %collective-permute-start.7 = (f32[8,128]{1,0:T(8,128)S(1)}, f32[8,128]{1,0:T(8,128)S(1)}, u32[]{:S(2)}, u32[]{:S(2)}) collective-permute-start(f32[8,128]{1,0:T(8,128)S(1)} %add.14), channel_id=1, source_target_pairs={{3,0},{2,1},{1,2},{0,3},{7,4},{6,5},{5,6},{4,7},{11,8},{10,9},{9,1... | collective-permute-start | bytes 12296 | tf_op jit(solution)/shard_map/ppermute | solution.py:300

commit v12 on v11

--- a/solution.py
+++ b/solution.py
@@ -193,7 +193,7 @@
             acc[:, near] = part + jnp.dot(w, low, preferred_element_type=f32)
 
     most = len(listed) * half
-    full = STEP * 3 // 4 if most == STEP else min(STEP, most)
+    full = STEP - LANES if most == STEP else min(STEP, most)
     steps = filled // full
     rest = filled - steps * full
 

time: 29.5 us -> 29.8 us (1.010); the launches traced: 29.6 us -> 29.5 us
  starting transfers between devices: 12.8 us -> 14.5 us
  waiting for transfers between devices: 7.6 us -> 5.96 us
    ppermute x8, starting transfers between devices: 12.8 us -> 14.5 us  [exchanged(): return lax.ppermute(block, ('blk', 'offs'), route)]
    ppermute x8, waiting for transfers between devices: 7.6 us -> 5.96 us  [exchanged(): return lax.ppermute(block, ('blk', 'offs'), route)]
  transfers between devices with their start and end apart: 8 -> 8, of which waited for: 5 -> 6; matrix products, arithmetic and copies ran while one was open for 0% -> 0% of each run, Pallas kernels for 18% -> 17%
where the time goes in v12:
time: 29.8 us; the launch traced here: 29.5 us
  starting transfers between devices  14.5 us (49%)
  Pallas kernels  7.54 us (25%)
  waiting for transfers between devices  5.96 us (20%)
  between operations  1.37 us (5%)
    ppermute x8, starting transfers between devices, exchanged(): return lax.ppermute(block, ('blk', 'offs'), route)  14.5 us
    pallas_call x4, Pallas kernels, pairs(): call(kernel, outs, specs, (VMEM,) * len(outs), scratch, name, flops)(*args)  6.69 us
    ppermute x8, waiting for transfers between devices, exchanged(): return lax.ppermute(block, ('blk', 'offs'), route)  5.96 us
    pallas_call x1, Pallas kernels, body(): call(tail_kernel, (shape(rhs.shape, f32),) * 2, [VMEM] * 4, (VMEM, VMEM),...  0.81 us
  transfers between devices with their start and end apart: 8, of which 6 were waited for; matrix products, arithmetic and copies ran while one was open for 0% of the time, Pallas kernels for 17%

profile of v12, /device:TPU:0, one launch (start us, length us, event | category | flops | bytes accessed | tf_op | source)
XLA Modules:
  0.0 29.5 jit_solution(7332931821871772209)
XLA Ops:
  0.6 0.0 copy-start
  0.6 0.0 copy-start.1
  1.3 0.1 copy-done
  1.4 3.5 %collective-permute-start = (f32[8,768]{1,0:T(8,128)S(1)}, f32[8,768]{1,0:T(8,128)S(1)}, u32[]{:S(2)}, u32[]{:S(2)}) collective-permute-start(f32[8,768]{1,0:T(8,128)S(1)} %pack.1.refs_0_), channel_id=1, source_target_pairs={{9,0},{8,1},{11,2},{10,3},{13,4},{12,5},{15,6},{14,7},{1,8},{0,9},... | collective-permute-start | bytes 73736 | tf_op jit(solution)/shard_map/ppermute | solution.py:300
  5.0 1.4 %pairs_1.2 = (f32[8,768]{1,0:T(8,128)S(1)}, f32[48,1024]{1,0:T(8,128)S(1)}, bf16[32,1024]{1,0:T(8,128)(2,1)S(1)}, f32[8,128]{1,0:T(8,128)S(1)}, f32[3,1024]{1,0:...) custom-call(f32[8,768]{1,0:T(8,128)S(1)} %pack.1.refs_0_, f32[3,1024]{1,0:T(4,128)S(1)} %copy-done.1, ...), custom_call_target="tpu_custom_call" | custom-call | flops 67108864 | bytes 131072 | tf_op jit(solution)/shard_map/pairs_1/pallas_call | solution.py:367
  6.4 0.2 collective-permute-done
  6.6 1.8 %collective-permute-start.1 = (f32[8,1536]{1,0:T(8,128)S(1)}, f32[8,1536]{1,0:T(8,128)S(1)}, u32[]{:S(2)}, u32[]{:S(2)}) collective-permute-start(f32[8,1536]{1,0:T(8,128)S(1)} %constant_dynamic-update-slice_fusion.refs_0_), channel_id=1, source_target_pairs={{5,0},{4,1},{7,2},{6,3},{1,4},{0,5},{3,6},{2,7},{13,8},{12,9},{15,... | collective-permute-start | bytes 147464 | tf_op jit(solution)/shard_map/ppermute | solution.py:300
  8.4 1.6 %collective-permute-start.3 = (f32[8,1536]{1,0:T(8,128)S(1)}, f32[8,1536]{1,0:T(8,128)S(1)}, u32[]{:S(2)}, u32[]{:S(2)}) collective-permute-start(f32[8,1536]{1,0:T(8,128)S(1)} %constant_dynamic-update-slice_fusion.refs_0_), channel_id=1, source_target_pairs={{3,0},{2,1},{1,2},{0,3},{7,4},{6,5},{5,6},{4,7},{11,8},{10,9},{9,1... | collective-permute-start | bytes 147464 | tf_op jit(solution)/shard_map/ppermute | solution.py:300
  10.0 1.1 %pairs_1.3.refs_3_ = f32[48,1024]{1,0:T(8,128)S(1)} custom-call(f32[8,1536]{1,0:T(8,128)S(1)} %constant_dynamic-update-slice_fusion.refs_0_, bf16[32,1024]{1,0:T(8,128)(2,1)S(1)} %get-tuple-element.16.refs_1_.refs_2_, f32[48,1024]{1,0:T(8,128)S(1)} %get-tuple-element.17.refs_2_), custom_call_target="tpu_custom_call" | custom-call | flops 67108864 | bytes 131072 | tf_op jit(solution)/shard_map/pairs_1/pallas_call | solution.py:367
  11.1 0.0 collective-permute-done.1.refs_0_
  11.1 1.0 %collective-permute-start.2 = (f32[8,1536]{1,0:T(8,128)S(1)}, f32[8,1536]{1,0:T(8,128)S(1)}, u32[]{:S(2)}, u32[]{:S(2)}) collective-permute-start(f32[8,1536]{1,0:T(8,128)S(1)} %collective-permute-done.1.refs_0_), channel_id=1, source_target_pairs={{3,0},{2,1},{1,2},{0,3},{7,4},{6,5},{5,6},{4,7},{11,8},{10,9},{9,1... | collective-permute-start | bytes 147464 | tf_op jit(solution)/shard_map/ppermute | solution.py:300
  12.1 0.0 collective-permute-done.3.refs_1_
  12.1 2.6 %pairs_4.1.refs_2_ = f32[48,1024]{1,0:T(8,128)S(1)} custom-call(f32[8,1536]{1,0:T(8,128)S(1)} %collective-permute-done.1.refs_0_, f32[8,1536]{1,0:T(8,128)S(1)} %collective-permute-done.3.refs_1_, bf16[32,1024]{1,0:T(8,128)(2,1)S(1)} %get-tuple-element.16.refs_1_.refs_2_, f32[48,1024]{1,0:T(8,128)S(1)} %pairs_1.3.refs_3_), custom_call_target="tpu_custom_call" | custom-call | flops 268435456 | bytes 131072 | tf_op jit(solution)/shard_map/pairs_4/pallas_call | solution.py:367
  14.7 0.3 collective-permute-done.2.refs_0_
  14.9 1.6 %pairs_2.1.mine = f32[8,1152]{1,0:T(8,128)S(1)} custom-call(f32[8,1536]{1,0:T(8,128)S(1)} %collective-permute-done.2.refs_0_, bf16[32,1024]{1,0:T(8,128)(2,1)S(1)} %get-tuple-element.16.refs_1_.refs_2_, f32[48,1024]{1,0:T(8,128)S(1)} %pairs_4.1.refs_2_, f32[8,128]{1,0:T(8,128)S(1)} %get-tuple-element.20.refs_3_, f32[3,1024]{1,0:T(4,128)S(1)} %get-tuple-element.21.refs_4_, ...), custom_call_target="tpu_custom_call" | custom-call | flops 134217728 | bytes 131072 | tf_op jit(solution)/shard_map/pairs_2/pallas_call | solution.py:367
  16.6 0.1 collective-permute-start.4
  16.6 1.2 %collective-permute-done.4.other = f32[8,1152]{1,0:T(8,128)S(1)} collective-permute-done((f32[8,1152]{1,0:T(8,128)S(1)}, f32[8,1152]{1,0:T(8,128)S(1)}, u32[]{:S(2)}, u32[]{:S(2)}) %collective-permute-start.4) | collective-permute-done | bytes 36896 | tf_op jit(solution)/shard_map/ppermute | solution.py:300
  17.9 3.0 %collective-permute-start.5 = (f32[8,128]{1,0:T(8,128)S(1)}, f32[8,128]{1,0:T(8,128)S(1)}, u32[]{:S(2)}, u32[]{:S(2)}) collective-permute-start(f32[8,128]{1,0:T(8,128)S(1)} %slice_add_fusion), channel_id=1, source_target_pairs={{9,0},{8,1},{11,2},{10,3},{13,4},{12,5},{15,6},{14,7},{1,8},{0,9},... | collective-permute-start | bytes 12296 | tf_op jit(solution)/shard_map/ppermute | solution.py:300
  20.8 1.3 %collective-permute-done.5 = f32[8,128]{1,0:T(8,128)S(1)} collective-permute-done((f32[8,128]{1,0:T(8,128)S(1)}, f32[8,128]{1,0:T(8,128)S(1)}, u32[]{:S(2)}, u32[]{:S(2)}) %collective-permute-start.5) | collective-permute-done | bytes 4128 | tf_op jit(solution)/shard_map/ppermute | solution.py:300
  22.2 2.2 %collective-permute-start.6 = (f32[8,128]{1,0:T(8,128)S(1)}, f32[8,128]{1,0:T(8,128)S(1)}, u32[]{:S(2)}, u32[]{:S(2)}) collective-permute-start(f32[8,128]{1,0:T(8,128)S(1)} %add.13), channel_id=1, source_target_pairs={{5,0},{4,1},{7,2},{6,3},{1,4},{0,5},{3,6},{2,7},{13,8},{12,9},{15,... | collective-permute-start | bytes 12296 | tf_op jit(solution)/shard_map/ppermute | solution.py:300
  24.3 1.3 %collective-permute-done.6 = f32[8,128]{1,0:T(8,128)S(1)} collective-permute-done((f32[8,128]{1,0:T(8,128)S(1)}, f32[8,128]{1,0:T(8,128)S(1)}, u32[]{:S(2)}, u32[]{:S(2)}) %collective-permute-start.6) | collective-permute-done | bytes 4128 | tf_op jit(solution)/shard_map/ppermute | solution.py:300
  25.7 1.4 %collective-permute-start.7 = (f32[8,128]{1,0:T(8,128)S(1)}, f32[8,128]{1,0:T(8,128)S(1)}, u32[]{:S(2)}, u32[]{:S(2)}) collective-permute-start(f32[8,128]{1,0:T(8,128)S(1)} %add.14), channel_id=1, source_target_pairs={{3,0},{2,1},{1,2},{0,3},{7,4},{6,5},{5,6},{4,7},{11,8},{10,9},{9,1... | collective-permute-start | bytes 12296 | tf_op jit(solution)/shard_map/ppermute | solution.py:300
  27.1 1.6 %collective-permute-done.7 = f32[8,128]{1,0:T(8,128)S(1)} collective-permute-done((f32[8,128]{1,0:T(8,128)S(1)}, f32[8,128]{1,0:T(8,128)S(1)}, u32[]{:S(2)}, u32[]{:S(2)}) %collective-permute-start.7) | collective-permute-done | bytes 4128 | tf_op jit(solution)/shard_map/ppermute | solution.py:300
  28.7 0.8 %tail.1 = (f32[8,1024]{1,0:T(8,128)}, f32[8,1024]{1,0:T(8,128)}) custom-call(f32[8,128]{1,0:T(8,128)S(1)} %add.15.small, f32[8,1152]{1,0:T(8,128)S(1)} %pairs_2.1.mine, f32[8,1152]{1,0:T(8,128)S(1)} %collective-permute-done.4.other, f32[8,1024]{1,0:T(8,128)S(1)} %get-tuple-element.22.refs_5_.direction_ref), custom_call_target="tpu_custom_call" | custom-call | bytes 131072 | tf_op jit(solution)/shard_map/tail/pallas_call | solution.py:397
  (12 shorter events, 0.1 us)
Async XLA Ops:
  0.6 0.8 %copy-start = (f32[8,1024]{1,0:T(8,128)S(1)}, f32[8,1024]{1,0:T(8,128)}, u32[]{:S(2)}) copy-start(f32[8,1024]{1,0:T(8,128)} %refs_3_.1) | copy-start | bytes 98308
  0.6 0.8 %copy-start.1 = (f32[3,1024]{1,0:T(4,128)S(1)}, f32[3,1024]{1,0:T(4,128)}, u32[]{:S(2)}) copy-start(f32[3,1024]{1,0:T(4,128)} %refs_1_.1) | copy-start | bytes 36868
  1.4 3.6 %copy-start.2 = (f32[1024]{0:T(1024)S(1)}, f32[1024]{0:T(1024)}, u32[]{:S(2)}) copy-start(f32[1024]{0:T(1024)} %refs_2_.1) | copy-start | bytes 12292
  1.4 5.1 %collective-permute-start = (f32[8,768]{1,0:T(8,128)S(1)}, f32[8,768]{1,0:T(8,128)S(1)}, u32[]{:S(2)}, u32[]{:S(2)}) collective-permute-start(f32[8,768]{1,0:T(8,128)S(1)} %pack.1.refs_0_), channel_id=1, source_target_pairs={{9,0},{8,1},{11,2},{10,3},{13,4},{12,5},{15,6},{14,7},{1,8},{0,9},... | collective-permute-start | bytes 73736 | tf_op jit(solution)/shard_map/ppermute | solution.py:300
  6.6 4.5 %collective-permute-start.1 = (f32[8,1536]{1,0:T(8,128)S(1)}, f32[8,1536]{1,0:T(8,128)S(1)}, u32[]{:S(2)}, u32[]{:S(2)}) collective-permute-start(f32[8,1536]{1,0:T(8,128)S(1)} %constant_dynamic-update-slice_fusion.refs_0_), channel_id=1, source_target_pairs={{5,0},{4,1},{7,2},{6,3},{1,4},{0,5},{3,6},{2,7},{13,8},{12,9},{15,... | collective-permute-start | bytes 147464 | tf_op jit(solution)/shard_map/ppermute | solution.py:300
  8.4 3.7 %collective-permute-start.3 = (f32[8,1536]{1,0:T(8,128)S(1)}, f32[8,1536]{1,0:T(8,128)S(1)}, u32[]{:S(2)}, u32[]{:S(2)}) collective-permute-start(f32[8,1536]{1,0:T(8,128)S(1)} %constant_dynamic-update-slice_fusion.refs_0_), channel_id=1, source_target_pairs={{3,0},{2,1},{1,2},{0,3},{7,4},{6,5},{5,6},{4,7},{11,8},{10,9},{9,1... | collective-permute-start | bytes 147464 | tf_op jit(solution)/shard_map/ppermute | solution.py:300
  11.1 3.8 %collective-permute-start.2 = (f32[8,1536]{1,0:T(8,128)S(1)}, f32[8,1536]{1,0:T(8,128)S(1)}, u32[]{:S(2)}, u32[]{:S(2)}) collective-permute-start(f32[8,1536]{1,0:T(8,128)S(1)} %collective-permute-done.1.refs_0_), channel_id=1, source_target_pairs={{3,0},{2,1},{1,2},{0,3},{7,4},{6,5},{5,6},{4,7},{11,8},{10,9},{9,1... | collective-permute-start | bytes 147464 | tf_op jit(solution)/shard_map/ppermute | solution.py:300
  16.6 1.3 %collective-permute-start.4 = (f32[8,1152]{1,0:T(8,128)S(1)}, f32[8,1152]{1,0:T(8,128)S(1)}, u32[]{:S(2)}, u32[]{:S(2)}) collective-permute-start(f32[8,1152]{1,0:T(8,128)S(1)} %pairs_2.1.mine), channel_id=1, source_target_pairs={{1,0},{0,1},{3,2},{2,3},{5,4},{4,5},{7,6},{6,7},{9,8},{8,9},{11,10... | collective-permute-start | bytes 110600 | tf_op jit(solution)/shard_map/ppermute | solution.py:300
  17.9 4.3 %collective-permute-start.5 = (f32[8,128]{1,0:T(8,128)S(1)}, f32[8,128]{1,0:T(8,128)S(1)}, u32[]{:S(2)}, u32[]{:S(2)}) collective-permute-start(f32[8,128]{1,0:T(8,128)S(1)} %slice_add_fusion), channel_id=1, source_target_pairs={{9,0},{8,1},{11,2},{10,3},{13,4},{12,5},{15,6},{14,7},{1,8},{0,9},... | collective-permute-start | bytes 12296 | tf_op jit(solution)/shard_map/ppermute | solution.py:300
  22.2 3.5 %collective-permute-start.6 = (f32[8,128]{1,0:T(8,128)S(1)}, f32[8,128]{1,0:T(8,128)S(1)}, u32[]{:S(2)}, u32[]{:S(2)}) collective-permute-start(f32[8,128]{1,0:T(8,128)S(1)} %add.13), channel_id=1, source_target_pairs={{5,0},{4,1},{7,2},{6,3},{1,4},{0,5},{3,6},{2,7},{13,8},{12,9},{15,... | collective-permute-start | bytes 12296 | tf_op jit(solution)/shard_map/ppermute | solution.py:300
  25.7 3.0 %collective-permute-start.7 = (f32[8,128]{1,0:T(8,128)S(1)}, f32[8,128]{1,0:T(8,128)S(1)}, u32[]{:S(2)}, u32[]{:S(2)}) collective-permute-start(f32[8,128]{1,0:T(8,128)S(1)} %add.14), channel_id=1, source_target_pairs={{3,0},{2,1},{1,2},{0,3},{7,4},{6,5},{5,6},{4,7},{11,8},{10,9},{9,1... | collective-permute-start | bytes 12296 | tf_op jit(solution)/shard_map/ppermute | solution.py:300

commit v13 on v10

--- a/solution.py
+++ b/solution.py
@@ -387,10 +387,8 @@
     direction = ready[2]
     other = exchanged(mine, 0)
     small = mine[:, slots:] + other[:, slots:]
-    distance = blocks // 2
-    while distance:
+    for distance in reversed(distances):
         small = small + exchanged(small, distance)
-        distance //= 2
 
     return tuple(
         call(

time: 29.5 us -> 29.5 us (level)
  starting transfers between devices: 14.1 us -> 13.5 us
  Pallas kernels: 6.9 us -> 7.37 us
    ppermute x8, starting transfers between devices: 14.1 us -> 13.5 us  [exchanged(): return lax.ppermute(block, ('blk', 'offs'), route)]
    pallas_call x4, Pallas kernels: 6.06 us -> 6.52 us  [pairs(): call(kernel, outs, specs, (VMEM,) * len(outs), scratch, name, flops)(*args)]
  transfers between devices with their start and end apart: 8 -> 8, of which waited for: 6 -> 5; matrix products, arithmetic and copies ran while one was open for 0% -> 0% of each run, Pallas kernels for 14% -> 17%
where the time goes in v13:
time: 29.5 us; the launch traced here: 29.3 us
  starting transfers between devices  13.5 us (46%)
  Pallas kernels  7.37 us (25%)
  waiting for transfers between devices  6.91 us (23%)
  between operations  1.38 us (5%)
    ppermute x8, starting transfers between devices, exchanged(): return lax.ppermute(block, ('blk', 'offs'), route)  13.5 us
    ppermute x8, waiting for transfers between devices, exchanged(): return lax.ppermute(block, ('blk', 'offs'), route)  6.91 us
    pallas_call x4, Pallas kernels, pairs(): call(kernel, outs, specs, (VMEM,) * len(outs), scratch, name, flops)(*args)  6.52 us
    pallas_call x1, Pallas kernels, body(): call(tail_kernel, (shape(rhs.shape, f32),) * 2, [VMEM] * 4, (VMEM, VMEM),...  0.81 us
  transfers between devices with their start and end apart: 8, of which 5 were waited for; matrix products, arithmetic and copies ran while one was open for 0% of the time, Pallas kernels for 17%

profile of v13, /device:TPU:0, one launch (start us, length us, event | category | flops | bytes accessed | tf_op | source)
XLA Modules:
  0.0 29.3 jit_solution(14279274767300465678)
XLA Ops:
  1.3 0.1 copy-done
  1.4 0.0 copy-done.1
  1.4 3.5 %collective-permute-start = (f32[8,768]{1,0:T(8,128)S(1)}, f32[8,768]{1,0:T(8,128)S(1)}, u32[]{:S(2)}, u32[]{:S(2)}) collective-permute-start(f32[8,768]{1,0:T(8,128)S(1)} %pack.1.refs_0_), channel_id=1, source_target_pairs={{9,0},{8,1},{11,2},{10,3},{13,4},{12,5},{15,6},{14,7},{1,8},{0,9},... | collective-permute-start | bytes 73736 | tf_op jit(solution)/shard_map/ppermute | solution.py:299
  5.0 0.0 copy-done.2
  5.0 0.8 %pairs_1.2 = (f32[8,768]{1,0:T(8,128)S(1)}, f32[48,1024]{1,0:T(8,128)S(1)}, bf16[32,1024]{1,0:T(8,128)(2,1)S(1)}, f32[8,128]{1,0:T(8,128)S(1)}, f32[3,1024]{1,0:...) custom-call(f32[8,768]{1,0:T(8,128)S(1)} %pack.1.refs_0_, f32[3,1024]{1,0:T(4,128)S(1)} %copy-done.1, ...), custom_call_target="tpu_custom_call" | custom-call | flops 67108864 | bytes 131072 | tf_op jit(solution)/shard_map/pairs_1/pallas_call | solution.py:366
  5.8 0.7 %collective-permute-done = f32[8,768]{1,0:T(8,128)S(1)} collective-permute-done((f32[8,768]{1,0:T(8,128)S(1)}, f32[8,768]{1,0:T(8,128)S(1)}, u32[]{:S(2)}, u32[]{:S(2)}) %collective-permute-start) | collective-permute-done | bytes 24608 | tf_op jit(solution)/shard_map/ppermute | solution.py:299
  6.6 1.8 %collective-permute-start.1 = (f32[8,1536]{1,0:T(8,128)S(1)}, f32[8,1536]{1,0:T(8,128)S(1)}, u32[]{:S(2)}, u32[]{:S(2)}) collective-permute-start(f32[8,1536]{1,0:T(8,128)S(1)} %constant_dynamic-update-slice_fusion.refs_0_), channel_id=1, source_target_pairs={{5,0},{4,1},{7,2},{6,3},{1,4},{0,5},{3,6},{2,7},{13,8},{12,9},{15,... | collective-permute-start | bytes 147464 | tf_op jit(solution)/shard_map/ppermute | solution.py:299
  8.4 1.6 %collective-permute-start.3 = (f32[8,1536]{1,0:T(8,128)S(1)}, f32[8,1536]{1,0:T(8,128)S(1)}, u32[]{:S(2)}, u32[]{:S(2)}) collective-permute-start(f32[8,1536]{1,0:T(8,128)S(1)} %constant_dynamic-update-slice_fusion.refs_0_), channel_id=1, source_target_pairs={{3,0},{2,1},{1,2},{0,3},{7,4},{6,5},{5,6},{4,7},{11,8},{10,9},{9,1... | collective-permute-start | bytes 147464 | tf_op jit(solution)/shard_map/ppermute | solution.py:299
  10.0 1.1 %pairs_1.3.refs_3_ = f32[48,1024]{1,0:T(8,128)S(1)} custom-call(f32[8,1536]{1,0:T(8,128)S(1)} %constant_dynamic-update-slice_fusion.refs_0_, bf16[32,1024]{1,0:T(8,128)(2,1)S(1)} %get-tuple-element.16.refs_1_.refs_2_, f32[48,1024]{1,0:T(8,128)S(1)} %get-tuple-element.17.refs_2_), custom_call_target="tpu_custom_call" | custom-call | flops 67108864 | bytes 131072 | tf_op jit(solution)/shard_map/pairs_1/pallas_call | solution.py:366
  11.1 0.0 collective-permute-done.1.refs_0_
  11.1 1.0 %collective-permute-start.2 = (f32[8,1536]{1,0:T(8,128)S(1)}, f32[8,1536]{1,0:T(8,128)S(1)}, u32[]{:S(2)}, u32[]{:S(2)}) collective-permute-start(f32[8,1536]{1,0:T(8,128)S(1)} %collective-permute-done.1.refs_0_), channel_id=1, source_target_pairs={{3,0},{2,1},{1,2},{0,3},{7,4},{6,5},{5,6},{4,7},{11,8},{10,9},{9,1... | collective-permute-start | bytes 147464 | tf_op jit(solution)/shard_map/ppermute | solution.py:299
  12.1 0.0 collective-permute-done.3.refs_1_
  12.1 2.9 %pairs_4.1.refs_2_ = f32[48,1024]{1,0:T(8,128)S(1)} custom-call(f32[8,1536]{1,0:T(8,128)S(1)} %collective-permute-done.1.refs_0_, f32[8,1536]{1,0:T(8,128)S(1)} %collective-permute-done.3.refs_1_, bf16[32,1024]{1,0:T(8,128)(2,1)S(1)} %get-tuple-element.16.refs_1_.refs_2_, f32[48,1024]{1,0:T(8,128)S(1)} %pairs_1.3.refs_3_), custom_call_target="tpu_custom_call" | custom-call | flops 268435456 | bytes 131072 | tf_op jit(solution)/shard_map/pairs_4/pallas_call | solution.py:366
  15.0 0.0 collective-permute-done.2.refs_0_
  15.0 1.6 %pairs_2.1.mine = f32[8,1152]{1,0:T(8,128)S(1)} custom-call(f32[8,1536]{1,0:T(8,128)S(1)} %collective-permute-done.2.refs_0_, bf16[32,1024]{1,0:T(8,128)(2,1)S(1)} %get-tuple-element.16.refs_1_.refs_2_, f32[48,1024]{1,0:T(8,128)S(1)} %pairs_4.1.refs_2_, f32[8,128]{1,0:T(8,128)S(1)} %get-tuple-element.20.refs_3_, f32[3,1024]{1,0:T(4,128)S(1)} %get-tuple-element.21.refs_4_, ...), custom_call_target="tpu_custom_call" | custom-call | flops 134217728 | bytes 131072 | tf_op jit(solution)/shard_map/pairs_2/pallas_call | solution.py:366
  16.7 0.6 %collective-permute-start.4 = (f32[8,1152]{1,0:T(8,128)S(1)}, f32[8,1152]{1,0:T(8,128)S(1)}, u32[]{:S(2)}, u32[]{:S(2)}) collective-permute-start(f32[8,1152]{1,0:T(8,128)S(1)} %pairs_2.1.mine), channel_id=1, source_target_pairs={{1,0},{0,1},{3,2},{2,3},{5,4},{4,5},{7,6},{6,7},{9,8},{8,9},{11,10... | collective-permute-start | bytes 110600 | tf_op jit(solution)/shard_map/ppermute | solution.py:299
  17.3 0.9 %collective-permute-done.4.other = f32[8,1152]{1,0:T(8,128)S(1)} collective-permute-done((f32[8,1152]{1,0:T(8,128)S(1)}, f32[8,1152]{1,0:T(8,128)S(1)}, u32[]{:S(2)}, u32[]{:S(2)}) %collective-permute-start.4) | collective-permute-done | bytes 36896 | tf_op jit(solution)/shard_map/ppermute | solution.py:299
  18.2 1.1 %collective-permute-start.5 = (f32[8,128]{1,0:T(8,128)S(1)}, f32[8,128]{1,0:T(8,128)S(1)}, u32[]{:S(2)}, u32[]{:S(2)}) collective-permute-start(f32[8,128]{1,0:T(8,128)S(1)} %slice_add_fusion), channel_id=1, source_target_pairs={{3,0},{2,1},{1,2},{0,3},{7,4},{6,5},{5,6},{4,7},{11,8},{10,9},{9,1... | collective-permute-start | bytes 12296 | tf_op jit(solution)/shard_map/ppermute | solution.py:299
  19.3 1.9 %collective-permute-done.5 = f32[8,128]{1,0:T(8,128)S(1)} collective-permute-done((f32[8,128]{1,0:T(8,128)S(1)}, f32[8,128]{1,0:T(8,128)S(1)}, u32[]{:S(2)}, u32[]{:S(2)}) %collective-permute-start.5) | collective-permute-done | bytes 4128 | tf_op jit(solution)/shard_map/ppermute | solution.py:299
  21.2 1.0 %collective-permute-start.6 = (f32[8,128]{1,0:T(8,128)S(1)}, f32[8,128]{1,0:T(8,128)S(1)}, u32[]{:S(2)}, u32[]{:S(2)}) collective-permute-start(f32[8,128]{1,0:T(8,128)S(1)} %add.13), channel_id=1, source_target_pairs={{5,0},{4,1},{7,2},{6,3},{1,4},{0,5},{3,6},{2,7},{13,8},{12,9},{15,... | collective-permute-start | bytes 12296 | tf_op jit(solution)/shard_map/ppermute | solution.py:299
  22.2 2.1 %collective-permute-done.6 = f32[8,128]{1,0:T(8,128)S(1)} collective-permute-done((f32[8,128]{1,0:T(8,128)S(1)}, f32[8,128]{1,0:T(8,128)S(1)}, u32[]{:S(2)}, u32[]{:S(2)}) %collective-permute-start.6) | collective-permute-done | bytes 4128 | tf_op jit(solution)/shard_map/ppermute | solution.py:299
  24.3 2.8 %collective-permute-start.7 = (f32[8,128]{1,0:T(8,128)S(1)}, f32[8,128]{1,0:T(8,128)S(1)}, u32[]{:S(2)}, u32[]{:S(2)}) collective-permute-start(f32[8,128]{1,0:T(8,128)S(1)} %add.14), channel_id=1, source_target_pairs={{9,0},{8,1},{11,2},{10,3},{13,4},{12,5},{15,6},{14,7},{1,8},{0,9},... | collective-permute-start | bytes 12296 | tf_op jit(solution)/shard_map/ppermute | solution.py:299
  27.1 1.3 %collective-permute-done.7 = f32[8,128]{1,0:T(8,128)S(1)} collective-permute-done((f32[8,128]{1,0:T(8,128)S(1)}, f32[8,128]{1,0:T(8,128)S(1)}, u32[]{:S(2)}, u32[]{:S(2)}) %collective-permute-start.7) | collective-permute-done | bytes 4128 | tf_op jit(solution)/shard_map/ppermute | solution.py:299
  28.5 0.8 %tail.1 = (f32[8,1024]{1,0:T(8,128)}, f32[8,1024]{1,0:T(8,128)}) custom-call(f32[8,128]{1,0:T(8,128)S(1)} %add.15.small, f32[8,1152]{1,0:T(8,128)S(1)} %pairs_2.1.mine, f32[8,1152]{1,0:T(8,128)S(1)} %collective-permute-done.4.other, f32[8,1024]{1,0:T(8,128)S(1)} %get-tuple-element.22.refs_5_.direction_ref), custom_call_target="tpu_custom_call" | custom-call | bytes 131072 | tf_op jit(solution)/shard_map/tail/pallas_call | solution.py:394
  (12 shorter events, 0.1 us)
Async XLA Ops:
  0.6 0.8 %copy-start = (f32[8,1024]{1,0:T(8,128)S(1)}, f32[8,1024]{1,0:T(8,128)}, u32[]{:S(2)}) copy-start(f32[8,1024]{1,0:T(8,128)} %refs_3_.1) | copy-start | bytes 98308
  0.6 0.8 %copy-start.1 = (f32[3,1024]{1,0:T(4,128)S(1)}, f32[3,1024]{1,0:T(4,128)}, u32[]{:S(2)}) copy-start(f32[3,1024]{1,0:T(4,128)} %refs_1_.1) | copy-start | bytes 36868
  1.4 3.6 %copy-start.2 = (f32[1024]{0:T(1024)S(1)}, f32[1024]{0:T(1024)}, u32[]{:S(2)}) copy-start(f32[1024]{0:T(1024)} %refs_2_.1) | copy-start | bytes 12292
  1.4 5.1 %collective-permute-start = (f32[8,768]{1,0:T(8,128)S(1)}, f32[8,768]{1,0:T(8,128)S(1)}, u32[]{:S(2)}, u32[]{:S(2)}) collective-permute-start(f32[8,768]{1,0:T(8,128)S(1)} %pack.1.refs_0_), channel_id=1, source_target_pairs={{9,0},{8,1},{11,2},{10,3},{13,4},{12,5},{15,6},{14,7},{1,8},{0,9},... | collective-permute-start | bytes 73736 | tf_op jit(solution)/shard_map/ppermute | solution.py:299
  6.6 4.5 %collective-permute-start.1 = (f32[8,1536]{1,0:T(8,128)S(1)}, f32[8,1536]{1,0:T(8,128)S(1)}, u32[]{:S(2)}, u32[]{:S(2)}) collective-permute-start(f32[8,1536]{1,0:T(8,128)S(1)} %constant_dynamic-update-slice_fusion.refs_0_), channel_id=1, source_target_pairs={{5,0},{4,1},{7,2},{6,3},{1,4},{0,5},{3,6},{2,7},{13,8},{12,9},{15,... | collective-permute-start | bytes 147464 | tf_op jit(solution)/shard_map/ppermute | solution.py:299
  8.4 3.7 %collective-permute-start.3 = (f32[8,1536]{1,0:T(8,128)S(1)}, f32[8,1536]{1,0:T(8,128)S(1)}, u32[]{:S(2)}, u32[]{:S(2)}) collective-permute-start(f32[8,1536]{1,0:T(8,128)S(1)} %constant_dynamic-update-slice_fusion.refs_0_), channel_id=1, source_target_pairs={{3,0},{2,1},{1,2},{0,3},{7,4},{6,5},{5,6},{4,7},{11,8},{10,9},{9,1... | collective-permute-start | bytes 147464 | tf_op jit(solution)/shard_map/ppermute | solution.py:299
  11.1 3.9 %collective-permute-start.2 = (f32[8,1536]{1,0:T(8,128)S(1)}, f32[8,1536]{1,0:T(8,128)S(1)}, u32[]{:S(2)}, u32[]{:S(2)}) collective-permute-start(f32[8,1536]{1,0:T(8,128)S(1)} %collective-permute-done.1.refs_0_), channel_id=1, source_target_pairs={{3,0},{2,1},{1,2},{0,3},{7,4},{6,5},{5,6},{4,7},{11,8},{10,9},{9,1... | collective-permute-start | bytes 147464 | tf_op jit(solution)/shard_map/ppermute | solution.py:299
  16.7 1.5 %collective-permute-start.4 = (f32[8,1152]{1,0:T(8,128)S(1)}, f32[8,1152]{1,0:T(8,128)S(1)}, u32[]{:S(2)}, u32[]{:S(2)}) collective-permute-start(f32[8,1152]{1,0:T(8,128)S(1)} %pairs_2.1.mine), channel_id=1, source_target_pairs={{1,0},{0,1},{3,2},{2,3},{5,4},{4,5},{7,6},{6,7},{9,8},{8,9},{11,10... | collective-permute-start | bytes 110600 | tf_op jit(solution)/shard_map/ppermute | solution.py:299
  18.2 3.0 %collective-permute-start.5 = (f32[8,128]{1,0:T(8,128)S(1)}, f32[8,128]{1,0:T(8,128)S(1)}, u32[]{:S(2)}, u32[]{:S(2)}) collective-permute-start(f32[8,128]{1,0:T(8,128)S(1)} %slice_add_fusion), channel_id=1, source_target_pairs={{3,0},{2,1},{1,2},{0,3},{7,4},{6,5},{5,6},{4,7},{11,8},{10,9},{9,1... | collective-permute-start | bytes 12296 | tf_op jit(solution)/shard_map/ppermute | solution.py:299
  21.2 3.0 %collective-permute-start.6 = (f32[8,128]{1,0:T(8,128)S(1)}, f32[8,128]{1,0:T(8,128)S(1)}, u32[]{:S(2)}, u32[]{:S(2)}) collective-permute-start(f32[8,128]{1,0:T(8,128)S(1)} %add.13), channel_id=1, source_target_pairs={{5,0},{4,1},{7,2},{6,3},{1,4},{0,5},{3,6},{2,7},{13,8},{12,9},{15,... | collective-permute-start | bytes 12296 | tf_op jit(solution)/shard_map/ppermute | solution.py:299
  24.3 4.2 %collective-permute-start.7 = (f32[8,128]{1,0:T(8,128)S(1)}, f32[8,128]{1,0:T(8,128)S(1)}, u32[]{:S(2)}, u32[]{:S(2)}) collective-permute-start(f32[8,128]{1,0:T(8,128)S(1)} %add.14), channel_id=1, source_target_pairs={{9,0},{8,1},{11,2},{10,3},{13,4},{12,5},{15,6},{14,7},{1,8},{0,9},... | collective-permute-start | bytes 12296 | tf_op jit(solution)/shard_map/ppermute | solution.py:299
